TPU v7x, 32 devices: a whole 2x2x4 slice. The times are simulated.
32 devices in a mesh: seq: 8 (over z, y), head: 4 (over x, core).
Axes of the slice: x: 2, y: 2, z: 4, core: 2. Of those that a mesh axis runs over, the one named last changes fastest.
Arguments:
- query_input: bfloat16 [4096, 2048], P(('seq', 'head')), may hold values from -6 to 6
- key_input: bfloat16 [4096, 2048], P(('seq', 'head')), may hold values from -40 to 40
- value_input: bfloat16 [4096, 4096], P(('seq', 'head')), may hold values from -40 to 40
- gate_input: bfloat16 [4096, 4096], P(('seq', 'head')), may hold values from -6 to 6
- write_strength: bfloat16 [4096, 32], P(('seq', 'head')), may hold values from 0.0009 to 0.91
- log_decay: bfloat16 [4096, 32], P(('seq', 'head')), may hold values from -0.81 to 0
- filter_query: bfloat16 [4, 2048], P(None, 'head'), may hold values from -3 to 3
- filter_key: bfloat16 [4, 2048], P(None, 'head'), may hold values from -3 to 3
- filter_value: bfloat16 [4, 4096], P(None, 'head'), may hold values from -3 to 3
- norm_gain: float32 [128], replicated, may hold values from 0.1 to 1.9
- out_weight: bfloat16 [4096, 2048], P('head'), may hold values from -0.09375 to 0.09375
Outputs:
- stratum_result: bfloat16 [4096, 2048], P(('seq', 'head'))
All inputs are finite; a program needn't handle non-finite values.
Results may differ from a plain program's by a relative error of at most 0.005.
Values may be sent and summed in bfloat16 or wider, within the bound.
No kernel may reach another device: no remote copies, remote signals or barrier semaphores. Data moves between devices by JAX's collectives and lax.ppermute only.
A program may use at most 128 MiB of HBM per device.

v0:
```python
import jax
import jax.numpy as jnp
from jax import lax
from jax.sharding import PartitionSpec as P

HK = 16
HV = 32
DK = 128
DV = 128
CH = 64


exact_mode = lax.Precision.HIGHEST
norm_floor = 1e-06


def passed_along(value, axis, by):
    size = lax.axis_size(axis)
    pairs = [(i, i + by) for i in range(size) if 0 <= i + by < size]
    return lax.ppermute(value, axis, pairs)


def stretch_terms(query_rows, unit_keys, values, strength, forgetting_rates):
    block_width = forgetting_rates.shape[-1]
    value_width = values.shape[-1]
    key_width = unit_keys.shape[-1]
    token_index = lax.broadcasted_iota(jnp.int32, (block_width, block_width), 0)
    column_index = lax.broadcasted_iota(jnp.int32, (block_width, block_width), 1)
    inclusive = (column_index <= token_index).astype(jnp.float32)
    strict = (column_index < token_index).astype(jnp.float32)
    cumulative = jnp.cumsum(forgetting_rates, axis=-1)
    spread = cumulative[..., :, None] - cumulative[..., None, :]
    ratios = jnp.exp(spread * inclusive) * inclusive
    key_key = jnp.einsum("...id,...jd->...ij", unit_keys, unit_keys, precision=exact_mode)
    query_key = jnp.einsum("...id,...jd->...ij", query_rows, unit_keys, precision=exact_mode)
    lower_part = strength[..., :, None] * key_key * ratios * strict
    query_mix = query_key * ratios
    growth = jnp.exp(cumulative)
    right_side = jnp.concatenate(
        [strength[..., None] * values, (strength * growth)[..., None] * unit_keys], axis=-1
    )
    system = lower_part + jnp.eye(block_width, dtype=jnp.float32)
    solved = jax.scipy.linalg.solve_triangular(system, right_side, lower=True, unit_diagonal=True)
    written = solved[..., :value_width]
    erased = solved[..., value_width:]
    tail_decay = jnp.exp(cumulative[..., -1:] - cumulative)
    tailed = unit_keys * tail_decay[..., None]
    carry_map = jnp.exp(cumulative[..., -1])[..., None, None] * jnp.eye(
        key_width, dtype=jnp.float32
    ) - jnp.einsum("...id,...ie->...de", tailed, erased, precision=exact_mode)
    carry_add = jnp.einsum("...id,...ie->...de", tailed, written, precision=exact_mode)
    local_out = jnp.einsum("...ij,...je->...ie", query_mix, written, precision=exact_mode)
    entry_map = growth[..., None] * query_rows - jnp.einsum(
        "...ij,...jd->...id", query_mix, erased, precision=exact_mode
    )
    return (carry_map, carry_add, local_out, entry_map)


def causal_local(signal, before, filter_taps):
    length = signal.shape[0]
    padded = jnp.concatenate([before.astype(jnp.float32), signal.astype(jnp.float32)], axis=0)
    summed = jnp.zeros(signal.shape, jnp.float32)
    for offset in range(filter_taps.shape[0]):
        summed = summed + filter_taps[offset].astype(jnp.float32) * padded[offset : offset + length]
    return jax.nn.silu(summed)


def unit_rows(field):
    return field / jnp.sqrt(jnp.sum(field * field, axis=-1, keepdims=True) + norm_floor)


def to_blocks(per_token, blocks):
    token_count, head_count, inner_width = per_token.shape
    return per_token.reshape(blocks, token_count // blocks, head_count, inner_width).transpose(
        0, 2, 1, 3
    )


def apply_maps(maps, states):
    return jnp.einsum("hde,hef->hdf", maps, states, precision=exact_mode)


def gated_norm(core_out, gate_rows, norm_gain):
    token_count, head_count, head_width = core_out.shape
    inverse_rms = lax.rsqrt(jnp.mean(core_out * core_out, axis=-1, keepdims=True) + norm_floor)
    gating = jax.nn.silu(gate_rows.astype(jnp.float32)).reshape(token_count, head_count, head_width)
    return (
        (core_out * inverse_rms * norm_gain * gating)
        .astype(jnp.bfloat16)
        .reshape(token_count, head_count * head_width)
    )


def on_device(
    query_input,
    key_input,
    value_input,
    gate_input,
    write_strength,
    log_decay,
    filter_query,
    filter_key,
    filter_value,
    norm_gain,
    out_weight,
):
    grouped = (
        lax.all_to_all(query_input, "head", split_axis=1, concat_axis=0, tiled=True),
        lax.all_to_all(key_input, "head", split_axis=1, concat_axis=0, tiled=True),
        lax.all_to_all(value_input, "head", split_axis=1, concat_axis=0, tiled=True),
        lax.all_to_all(gate_input, "head", split_axis=1, concat_axis=0, tiled=True),
        lax.all_to_all(write_strength, "head", split_axis=1, concat_axis=0, tiled=True),
        lax.all_to_all(log_decay, "head", split_axis=1, concat_axis=0, tiled=True),
    )
    query_local, key_local, value_local, gate_local, strength_local, decay_local = grouped
    margin = filter_query.shape[0] - 1
    query_width = query_local.shape[1]
    key_width = key_local.shape[1]
    edge_rows = jnp.concatenate(
        [query_local[-margin:], key_local[-margin:], value_local[-margin:]], axis=1
    )
    before = passed_along(edge_rows, "seq", 1)
    query_rows = causal_local(query_local, before[:, :query_width], filter_query)
    unit_keys = causal_local(
        key_local, before[:, query_width : query_width + key_width], filter_key
    )
    values = causal_local(value_local, before[:, query_width + key_width :], filter_value)
    token_count = query_local.shape[0]
    key_heads = key_width // DK
    value_heads = value_local.shape[1] // DV
    sharing = HV // HK
    unit_keys = unit_rows(unit_keys.reshape(token_count, key_heads, DK))
    unit_keys = jnp.repeat(unit_keys, sharing, axis=1)
    query_rows = unit_rows(query_rows.reshape(token_count, key_heads, DK)) * DK ** (-0.5)
    query_rows = jnp.repeat(query_rows, sharing, axis=1)
    values = values.reshape(token_count, value_heads, DV)
    blocks = token_count // CH
    strength = (
        strength_local.astype(jnp.float32).reshape(blocks, CH, value_heads).transpose(0, 2, 1)
    )
    forgetting_rates = (
        decay_local.astype(jnp.float32).reshape(blocks, CH, value_heads).transpose(0, 2, 1)
    )
    carry_map, carry_add, local_out, entry_map = stretch_terms(
        to_blocks(query_rows, blocks),
        to_blocks(unit_keys, blocks),
        to_blocks(values, blocks),
        strength,
        forgetting_rates,
    )
    identity = jnp.broadcast_to(jnp.eye(DK, dtype=jnp.float32), (value_heads, DK, DK))
    zero_state = jnp.zeros((value_heads, DK, DV), jnp.float32)

    def compose(carried, pieces):
        product, offset = carried
        block_map, block_add = pieces
        return ((apply_maps(block_map, product), apply_maps(block_map, offset) + block_add), None)

    (span_map, span_add), unused = lax.scan(compose, (identity, zero_state), (carry_map, carry_add))

    def handoff_step(step_index, carried):
        arrived = passed_along(carried[1], "seq", 1)
        return (arrived, apply_maps(span_map, arrived) + span_add)

    entry_state, final_state = lax.fori_loop(
        0, lax.axis_size("seq") - 1, handoff_step, (zero_state, span_add)
    )

    def advance(running, pieces):
        block_map, block_add, block_out, block_entry = pieces
        emitted = block_out + jnp.einsum("hcd,hde->hce", block_entry, running, precision=exact_mode)
        return (apply_maps(block_map, running) + block_add, emitted)

    final_entry, core_out = lax.scan(
        advance, entry_state, (carry_map, carry_add, local_out, entry_map)
    )
    core_out = core_out.transpose(0, 2, 1, 3).reshape(token_count, value_heads, DV)
    normed = gated_norm(core_out, gate_local, norm_gain)
    projected = lax.psum_scatter(
        jnp.dot(normed, out_weight, preferred_element_type=jnp.float32),
        "head",
        scatter_dimension=0,
        tiled=True,
    )
    return projected.astype(jnp.bfloat16)


def solution(mesh):
    placed = (
        P(("seq", "head"), None),
        P(("seq", "head"), None),
        P(("seq", "head"), None),
        P(("seq", "head"), None),
        P(("seq", "head"), None),
        P(("seq", "head"), None),
        P(None, "head"),
        P(None, "head"),
        P(None, "head"),
        P(),
        P("head", None),
    )
    return jax.shard_map(
        on_device, mesh=mesh, in_specs=placed, out_specs=P(("seq", "head"), None), check_vma=False
    )
```

profile of v0, /device:TPU:0, one launch (start us, length us, event | category | flops | bytes accessed | tf_op | source)
XLA Modules:
  0.0 707.7 jit_solution(4808241993749980989)
XLA Ops:
  6.5 4.3 all-to-all-start
  14.7 3.2 all-to-all-start.4
  18.0 2.1 copy.64
  21.7 3.5 all-to-all-start.1
  26.9 7.1 %all-to-all-done.1 = bf16[128,4,512]{0,2,1:T(8,128)(2,1)S(1)} async-done(((bf16[128,4,512]{0,2,1:T(8,128)(2,1)}), bf16[128,4,512]{0,2,1:T(8,128)(2,1)S(1)}, u32[]{:S(2)}, u32[]{:S(2)}) %all-to-all-start.1) | async-done | bytes 524320 | tf_op jit(solution)/shard_map/all_to_all | solution.py:108
  34.0 3.5 all-to-all-start.2
  38.9 2.3 copy.81
  41.3 5.0 all-to-all-done.2
  46.3 3.5 all-to-all-start.3
  53.6 10.6 %all-to-all-done.3 = bf16[128,4,1024]{0,2,1:T(8,128)(2,1)S(1)} async-done(((bf16[128,4,1024]{0,2,1:T(8,128)(2,1)}), bf16[128,4,1024]{0,2,1:T(8,128)(2,1)S(1)}, u32[]{:S(2)}, u32[]{:S(2)}) %all-to-all-start.3) | async-done | bytes 1048608 | tf_op jit(solution)/shard_map/all_to_all | solution.py:110
  64.3 4.2 all-to-all-start.5
  70.4 3.9 collective-permute-start.1
  75.9 7.1 %all-to-all-done.5 = bf16[128,4,1024]{0,2,1:T(8,128)(2,1)} async-done(((bf16[128,4,1024]{0,2,1:T(8,128)(2,1)}), bf16[128,4,1024]{0,2,1:T(8,128)(2,1)}, u32[]{:S(2)}, u32[]{:S(2)}) %all-to-all-start.5) | async-done | bytes 1048608 | tf_op jit(solution)/shard_map/all_to_all | solution.py:111
  84.4 1.9 copy.82
  86.4 5.7 divide_multiply_fusion.1
  94.6 5.0 add_bitcast_fusion
  99.6 316.0 %custom-call.4 = f32[8,8,1,64,64]{3,4,2,1,0:T(8,128)} custom-call(f32[8,8,1,64,64]{4,3,2,1,0:T(8,128)} %add_bitcast_fusion), custom_call_target="InvertDiagBlocksLowerTriangular" | custom-call | tf_op jit(solution)/shard_map/jit(_solve_triangular)/vmap(vmap())/triangular_solve | solution.py:43
  421.3 2.6 reshape.129
  423.9 1.9 multiply_reduce_fusion.1
  427.1 3.5 fusion.44
  430.7 4.2 fusion.19
  434.9 3.6 fusion.46
  438.5 4.1 fusion.39
  442.7 8.9 %fusion.45 = f32[8,8,128,128]{3,2,1,0:T(8,128)} fusion(f32[8,8,64,256]{3,2,1,0:T(8,128)S(1)} %fusion.19, f32[8,64,8,128]{3,1,0,2:T(8,128)S(1)} %bitcast.167, f32[8,8,64]{2,1,0:T(8,128)S(1)} %get-tuple-element.154), kind=kOutput, calls=%fused_computation.65 | convolution fusion | flops 805830656 | bytes 8421376 | tf_op jit(solution)/shard_map/...id,...ie->...de/dot_general | solution.py:51
  451.6 9.2 %multiply_subtract_fusion = f32[8,8,128,128]{3,2,1,0:T(8,128)} fusion(f32[128,128]{1,0:T(8,128)S(1)} %fusion.83, f32[8,8]{1,0:T(8,128)S(1)} %exp.40, f32[8,8,64,256]{3,2,1,0:T(8,128)S(1)} %fusion.19, f32[8,64,8,128]{3,1,0,2:T(8,128)S(1)} %bitcast.168, f32[8,8,64]{2,1,0:T(8,128)S(1)} %get-tuple-element.154), kind=kOutput, calls=%fused_computation.27 | convolution fusion | flops 807927808 | bytes 8491008 | tf_op jit(solution)/shard_map/...id,...ie->...de/dot_general | solution.py:50
  460.9 29.6 %while.39 = (s32[]{:T(128)}, f32[8,128,128]{2,1,0:T(8,128)S(1)}, f32[8,128,128]{2,1,0:T(8,128)S(1)}, f32[8,8,128,128]{3,2,1,0:T(8,128)}, f32[8,8,128,128]{3,2,1,0:T(8,128)}, /*index=5*/s32[]{:T(128)}, s32[]{:T(128)}) while((s32[]{:T(128)}, f32[8,128,128]{2,1,0:T(8,128)S(1)}, f32[8,128,128]{2,1,0:T(8,128)S(1)}, ...), condition=%wide.region_3.4_spmd.clone, body=%wide.region_2.3_spmd.clone.sunk | while | flops 402915328 | bytes 5768791 | solution.py:159
  460.9 1.9 convolution_add_fusion.9
  464.6 1.9 convolution_add_fusion.9
  490.6 98.4 %while.37 = (s32[]{:T(128)}, f32[8,128,128]{2,1,0:T(8,128)}, f32[8,128,128]{2,1,0:T(8,128)S(1)}, f32[8,128,128]{2,1,0:T(8,128)S(1)}, f32[8,128,128]{2,1,0:T(8,128)S(1)}, /*index=5*/s32[]{:T(128)}) while((s32[]{:T(128)}, f32[8,128,128]{2,1,0:T(8,128)}, f32[8,128,128]{2,1,0:T(8,128)S(1)}, f32[8,128,128]{2,1,0:T(8,128)S(1)}, ...), condition=%wide.region_5.6_spmd, body=%wide.region_4.5_spmd.sunk | while | flops 201457664 | bytes 6291593 | solution.py:165
  490.6 3.9 collective-permute-start
  494.5 10.9 %collective-permute-done = f32[8,128,128]{2,1,0:T(8,128)S(1)} collective-permute-done((f32[8,128,128]{2,1,0:T(8,128)S(1)}, f32[8,128,128]{2,1,0:T(8,128)S(1)}, u32[]{:S(2)}, u32[]{:S(2)}) %collective-permute-start) | collective-permute-done | bytes 524320 | tf_op jit(solution)/shard_map/while/body/eval_jaxpr/ppermute | solution.py:20
  506.2 4.4 collective-permute-start
  510.6 10.0 %collective-permute-done = f32[8,128,128]{2,1,0:T(8,128)S(1)} collective-permute-done((f32[8,128,128]{2,1,0:T(8,128)S(1)}, f32[8,128,128]{2,1,0:T(8,128)S(1)}, u32[]{:S(2)}, u32[]{:S(2)}) %collective-permute-start) | collective-permute-done | bytes 524320 | tf_op jit(solution)/shard_map/while/body/eval_jaxpr/ppermute | solution.py:20
  521.5 4.4 collective-permute-start
  525.9 9.1 %collective-permute-done = f32[8,128,128]{2,1,0:T(8,128)S(1)} collective-permute-done((f32[8,128,128]{2,1,0:T(8,128)S(1)}, f32[8,128,128]{2,1,0:T(8,128)S(1)}, u32[]{:S(2)}, u32[]{:S(2)}) %collective-permute-start) | collective-permute-done | bytes 524320 | tf_op jit(solution)/shard_map/while/body/eval_jaxpr/ppermute | solution.py:20
  535.8 5.3 collective-permute-start
  541.1 8.2 %collective-permute-done = f32[8,128,128]{2,1,0:T(8,128)S(1)} collective-permute-done((f32[8,128,128]{2,1,0:T(8,128)S(1)}, f32[8,128,128]{2,1,0:T(8,128)S(1)}, u32[]{:S(2)}, u32[]{:S(2)}) %collective-permute-start) | collective-permute-done | bytes 524320 | tf_op jit(solution)/shard_map/while/body/eval_jaxpr/ppermute | solution.py:20
  550.0 5.3 collective-permute-start
  555.4 7.3 %collective-permute-done = f32[8,128,128]{2,1,0:T(8,128)S(1)} collective-permute-done((f32[8,128,128]{2,1,0:T(8,128)S(1)}, f32[8,128,128]{2,1,0:T(8,128)S(1)}, u32[]{:S(2)}, u32[]{:S(2)}) %collective-permute-start) | collective-permute-done | bytes 524320 | tf_op jit(solution)/shard_map/while/body/eval_jaxpr/ppermute | solution.py:20
  563.4 5.3 collective-permute-start
  568.7 6.6 collective-permute-done
  576.2 5.3 collective-permute-start
  581.5 6.6 collective-permute-done
  588.9 48.6 %while.38 = (s32[]{:T(128)}, f32[8,128,128]{2,1,0:T(8,128)}, f32[8,8,64,128]{3,2,1,0:T(8,128)}, f32[8,8,128,128]{3,2,1,0:T(8,128)}, f32[8,8,128,128]{3,2,1,0:T(8...) while((s32[]{:T(128)}, f32[8,128,128]{2,1,0:T(8,128)}, ...), condition=%wide.region_8.9_spmd, body=%wide.region_7.8_spmd.sunk | while | flops 302186496 | bytes 4458581 | solution.py:174
  590.0 2.4 fusion.119
  592.3 2.7 convolution_add_fusion.8
  596.0 2.3 fusion.119
  598.4 2.7 convolution_add_fusion.8
  602.1 2.3 fusion.119
  604.4 2.7 convolution_add_fusion.8
  608.1 2.3 fusion.119
  610.5 2.7 convolution_add_fusion.8
  614.2 2.3 fusion.119
  616.5 2.7 convolution_add_fusion.8
  620.2 2.3 fusion.119
  622.6 2.7 convolution_add_fusion.8
  626.3 2.3 fusion.119
  628.6 2.7 convolution_add_fusion.8
  632.3 2.4 fusion.119
  634.7 2.7 convolution_add_fusion.8
  637.6 2.4 multiply_reduce_fusion
  645.1 4.3 fusion.91
  649.4 49.0 %reduce-scatter.2.cloned.1.call-done = f32[128,2048]{1,0:T(8,128)} async-done(((f32[512,2048]{1,0:T(8,128)}), f32[128,2048]{1,0:T(8,128)}) %reduce-scatter.2.cloned.1.call-update) | async-done | bytes 1048592 | tf_op jit(solution)/shard_map/reduce_scatter | solution.py:179
  698.4 2.1 convert_element_type.127
  (156 shorter events, 71.2 us)
Async XLA Ops:
  6.5 11.4 %copy-start = (f32[128]{0:T(128)S(1)}, f32[128]{0:T(128)}, u32[]{:S(2)}) copy-start(f32[128]{0:T(128)} %param.26) | copy-start | bytes 1540
  6.5 18.7 %copy-start.11 = (bf16[128,2048]{1,0:T(8,128)(2,1)S(1)}, bf16[128,2048]{1,0:T(8,128)(2,1)}, u32[]{:S(2)}) copy-start(bf16[128,2048]{1,0:T(8,128)(2,1)} %param.18) | copy-start | bytes 1572868
  6.5 8.2 %all-to-all-start = ((bf16[128,4,8]{0,2,1:T(8,128)(2,1)}), bf16[128,4,8]{0,2,1:T(8,128)(2,1)S(1)}, u32[]{:S(2)}, u32[]{:S(2)}) async-start(bf16[128,4,8]{0,2,1:T(8,128)(2,1)} %bitcast.197), calls=%async_computation | async-start | bytes 16384 | tf_op jit(solution)/shard_map/all_to_all | solution.py:113
  14.7 7.0 all-to-all-start.4
  18.0 19.6 %copy-start.10 = (bf16[128,4096]{1,0:T(8,128)(2,1)S(1)}, bf16[128,4096]{1,0:T(8,128)(2,1)}, u32[]{:S(2)}) copy-start(bf16[128,4096]{1,0:T(8,128)(2,1)} %param.19) | copy-start | bytes 3145732
  21.7 12.3 %all-to-all-start.1 = ((bf16[128,4,512]{0,2,1:T(8,128)(2,1)}), bf16[128,4,512]{0,2,1:T(8,128)(2,1)S(1)}, u32[]{:S(2)}, u32[]{:S(2)}) async-start(bf16[128,4,512]{0,2,1:T(8,128)(2,1)} %bitcast.9), calls=%async_computation.1 | async-start | bytes 1048576 | tf_op jit(solution)/shard_map/all_to_all | solution.py:108
  34.0 12.3 %all-to-all-start.2 = ((bf16[128,4,512]{0,2,1:T(8,128)(2,1)}), bf16[128,4,512]{0,2,1:T(8,128)(2,1)S(1)}, u32[]{:S(2)}, u32[]{:S(2)}) async-start(bf16[128,4,512]{0,2,1:T(8,128)(2,1)} %bitcast.12), calls=%async_computation.2 | async-start | bytes 1048576 | tf_op jit(solution)/shard_map/all_to_all | solution.py:109
  46.3 18.0 %all-to-all-start.3 = ((bf16[128,4,1024]{0,2,1:T(8,128)(2,1)}), bf16[128,4,1024]{0,2,1:T(8,128)(2,1)S(1)}, u32[]{:S(2)}, u32[]{:S(2)}) async-start(bf16[128,4,1024]{0,2,1:T(8,128)(2,1)} %bitcast.15), calls=%async_computation.3 | async-start | bytes 2097152 | tf_op jit(solution)/shard_map/all_to_all | solution.py:110
  64.3 18.8 %all-to-all-start.5 = ((bf16[128,4,1024]{0,2,1:T(8,128)(2,1)}), bf16[128,4,1024]{0,2,1:T(8,128)(2,1)}, u32[]{:S(2)}, u32[]{:S(2)}) async-start(bf16[128,4,1024]{0,2,1:T(8,128)(2,1)} %bitcast.42), calls=%async_computation.5 | async-start | bytes 2097152 | tf_op jit(solution)/shard_map/all_to_all | solution.py:111
  68.5 629.9 %reduce-scatter.2.cloned.1.call-start = ((), (), s32[]{:S(2)}) async-start(), calls=%async_computation.7 | async-start | bytes 5242880 | tf_op jit(solution)/shard_map/reduce_scatter | solution.py:179
  70.4 16.0 %collective-permute-start.1 = (bf16[3,2048]{1,0:T(4,128)(2,1)S(1)}, bf16[3,2048]{1,0:T(4,128)(2,1)S(1)}, u32[]{:S(2)}, u32[]{:S(2)}) collective-permute-start(bf16[3,2048]{1,0:T(4,128)(2,1)S(1)} %pad_maximum_fusion.3), channel_id=1, source_target_pairs={{0,4},{4,8},{8,12},{12,16},{16,20},{20,24},{24,28},{1,5},{5,9},{9,... | collective-permute-start | bytes 36872 | tf_op jit(solution)/shard_map/ppermute | solution.py:20
  84.4 1.9 copy-start.12
  84.4 1.9 copy-start.13
  84.4 1.9 copy-start.14
  93.9 0.7 copy-start.15
  415.5 2.3 copy-start.8
  423.9 2.0 copy-start.3
  427.1 3.6 copy-start.5
  427.1 3.6 copy-start.6
  427.1 3.6 copy-start.9
  490.6 14.9 %collective-permute-start = (f32[8,128,128]{2,1,0:T(8,128)S(1)}, f32[8,128,128]{2,1,0:T(8,128)S(1)}, u32[]{:S(2)}, u32[]{:S(2)}) collective-permute-start(f32[8,128,128]{2,1,0:T(8,128)S(1)} %get-tuple-element.307), channel_id=1, source_target_pairs={{0,4},{4,8},{8,12},{12,16},{16,20},{20,24},{24,28},{1,5},{5,9},{9,... | collective-permute-start | bytes 1572872 | tf_op jit(solution)/shard_map/while/body/eval_jaxpr/ppermute | solution.py:20
  505.4 0.8 copy-start.2
  506.2 14.4 %collective-permute-start = (f32[8,128,128]{2,1,0:T(8,128)S(1)}, f32[8,128,128]{2,1,0:T(8,128)S(1)}, u32[]{:S(2)}, u32[]{:S(2)}) collective-permute-start(f32[8,128,128]{2,1,0:T(8,128)S(1)} %get-tuple-element.307), channel_id=1, source_target_pairs={{0,4},{4,8},{8,12},{12,16},{16,20},{20,24},{24,28},{1,5},{5,9},{9,... | collective-permute-start | bytes 1572872 | tf_op jit(solution)/shard_map/while/body/eval_jaxpr/ppermute | solution.py:20
  520.7 0.8 copy-start.2
  521.5 13.5 %collective-permute-start = (f32[8,128,128]{2,1,0:T(8,128)S(1)}, f32[8,128,128]{2,1,0:T(8,128)S(1)}, u32[]{:S(2)}, u32[]{:S(2)}) collective-permute-start(f32[8,128,128]{2,1,0:T(8,128)S(1)} %get-tuple-element.307), channel_id=1, source_target_pairs={{0,4},{4,8},{8,12},{12,16},{16,20},{20,24},{24,28},{1,5},{5,9},{9,... | collective-permute-start | bytes 1572872 | tf_op jit(solution)/shard_map/while/body/eval_jaxpr/ppermute | solution.py:20
  535.0 0.8 copy-start.2
  535.8 13.5 %collective-permute-start = (f32[8,128,128]{2,1,0:T(8,128)S(1)}, f32[8,128,128]{2,1,0:T(8,128)S(1)}, u32[]{:S(2)}, u32[]{:S(2)}) collective-permute-start(f32[8,128,128]{2,1,0:T(8,128)S(1)} %get-tuple-element.307), channel_id=1, source_target_pairs={{0,4},{4,8},{8,12},{12,16},{16,20},{20,24},{24,28},{1,5},{5,9},{9,... | collective-permute-start | bytes 1572872 | tf_op jit(solution)/shard_map/while/body/eval_jaxpr/ppermute | solution.py:20
  549.3 0.8 copy-start.2
  550.0 12.6 %collective-permute-start = (f32[8,128,128]{2,1,0:T(8,128)S(1)}, f32[8,128,128]{2,1,0:T(8,128)S(1)}, u32[]{:S(2)}, u32[]{:S(2)}) collective-permute-start(f32[8,128,128]{2,1,0:T(8,128)S(1)} %get-tuple-element.307), channel_id=1, source_target_pairs={{0,4},{4,8},{8,12},{12,16},{16,20},{20,24},{24,28},{1,5},{5,9},{9,... | collective-permute-start | bytes 1572872 | tf_op jit(solution)/shard_map/while/body/eval_jaxpr/ppermute | solution.py:20
  562.6 0.8 copy-start.2
  563.4 12.0 %collective-permute-start = (f32[8,128,128]{2,1,0:T(8,128)S(1)}, f32[8,128,128]{2,1,0:T(8,128)S(1)}, u32[]{:S(2)}, u32[]{:S(2)}) collective-permute-start(f32[8,128,128]{2,1,0:T(8,128)S(1)} %get-tuple-element.307), channel_id=1, source_target_pairs={{0,4},{4,8},{8,12},{12,16},{16,20},{20,24},{24,28},{1,5},{5,9},{9,... | collective-permute-start | bytes 1572872 | tf_op jit(solution)/shard_map/while/body/eval_jaxpr/ppermute | solution.py:20
  575.4 0.8 copy-start.2
  576.2 12.0 %collective-permute-start = (f32[8,128,128]{2,1,0:T(8,128)S(1)}, f32[8,128,128]{2,1,0:T(8,128)S(1)}, u32[]{:S(2)}, u32[]{:S(2)}) collective-permute-start(f32[8,128,128]{2,1,0:T(8,128)S(1)} %get-tuple-element.307), channel_id=1, source_target_pairs={{0,4},{4,8},{8,12},{12,16},{16,20},{20,24},{24,28},{1,5},{5,9},{9,... | collective-permute-start | bytes 1572872 | tf_op jit(solution)/shard_map/while/body/eval_jaxpr/ppermute | solution.py:20
  588.1 0.8 copy-start.2
  637.5 2.5 copy-start.7
  641.3 1.6 copy-start.4
  642.9 2.2 copy-start.16
  649.4 51.1 %copy-start.1 = (f32[128]{0:T(128)S(1)}, f32[128]{0:T(128)}, u32[]{:S(2)}) copy-start(f32[128]{0:T(128)} %param.26) | copy-start | bytes 1540
Sparse Core Ops, SparseCore 0:
  649.5 48.8 reduce-scatter.1
where the time goes:
time: 718 us; the launch traced here: 708 us
  other arithmetic  348 us (48%)
  waiting for transfers between devices  140 us (19%)
  matrix products  116 us (16%)
  starting transfers between devices  60.1 us (8%)
  local copies, waits for them, and re-layouts  28.7 us (4%)
  between operations  14.4 us (2%)
    another operation x4, other arithmetic, stretch_terms(): jax.scipy.linalg.solve_triangular(system, right_side, lower=True, unit_di...  317 us
    ppermute x8, waiting for transfers between devices, passed_along(): return lax.ppermute(value, axis, pairs)  58.8 us
    dot_general x31, matrix products, apply_maps(): return jnp.einsum('hde,hef->hdf', maps, states, precision=exact_mode)  54.6 us
    reduce_scatter x1, waiting for transfers between devices, on_device(): lax.psum_scatter(jnp.dot(normed, out_weight, preferred_element_type=jnp.f...  49 us
    ppermute x8, starting transfers between devices, passed_along(): return lax.ppermute(value, axis, pairs)  37.8 us
    dot_general x8, matrix products, advance(): jnp.einsum('hcd,hde->hce', block_entry, running, precision=exact_mode)  18.8 us
  transfers between devices with their start and end apart: 15, of which 14 were waited for; matrix products, arithmetic and copies ran while one was open for 3% of the time, Pallas kernels for 0%

commit v1 on v0

v1 whole, which is shorter than its diff:
```python
import functools

import jax
import jax.numpy as jnp
from jax import lax
from jax.experimental import pallas as pl
from jax.experimental.pallas import tpu as pltpu
from jax.sharding import PartitionSpec as P

HK = 16
HV = 32
DK = 128
DV = 128
CH = 128
EDGE = 16
SHARE = HV // HK

norm_floor = 1e-06
f32 = jnp.float32
bf16 = jnp.bfloat16


def params(megabytes=48):
    return pltpu.CompilerParams(vmem_limit_bytes=megabytes * 1024 * 1024)


def split(x):
    high = x.astype(bf16)
    return high, (x - high.astype(f32)).astype(bf16)


def as_left(x):
    return jnp.concatenate(split(x), axis=1)


def right_of(high, low):
    row = jnp.concatenate([high, low], axis=1)
    return jnp.concatenate([row, row], axis=0)


def as_right(x):
    return right_of(*split(x))


def product(left, right):
    both = jnp.dot(left, right, preferred_element_type=f32)
    half = both.shape[1] // 2
    return both[:, :half] + both[:, half:]


def grids():
    row = lax.broadcasted_iota(jnp.int32, (CH, CH), 0)
    column = lax.broadcasted_iota(jnp.int32, (CH, CH), 1)
    return row, column


def ones_where(mask):
    return jnp.where(mask, 1.0, 0.0).astype(bf16)


def conv_silu(rows_ref, edge_ref, taps_ref, padded):
    length = rows_ref.shape[0]
    taps = taps_ref[...].astype(f32)
    padded[0:8] = edge_ref[...].astype(f32)[EDGE - 8 : EDGE]
    padded[8 : 8 + length] = rows_ref[...].astype(f32)
    margin = taps.shape[0] - 1
    summed = taps[margin : margin + 1] * padded[8 : 8 + length]
    for offset in range(margin):
        start = 8 - margin + offset
        summed = summed + taps[offset : offset + 1] * padded[start : start + length]
    return summed / (1.0 + jnp.exp(-summed))


def unit_rows(field):
    return field * lax.rsqrt(jnp.sum(field * field, axis=-1, keepdims=True) + norm_floor)


def decay_terms(gates, head, value_heads):
    row, column = grids()
    pick_row = lax.broadcasted_iota(jnp.int32, (gates.shape[1], CH), 0)
    picks = jnp.concatenate(
        [ones_where(pick_row == head), ones_where(pick_row == value_heads + head)], axis=1
    )
    picked = jnp.dot(gates, picks, preferred_element_type=f32)
    strength = picked[:, :CH]
    rate = picked[:, CH:].astype(bf16)
    below = ones_where(column <= row)
    after = jnp.where(row > column, rate, jnp.zeros_like(rate))
    sums = jnp.dot(below, jnp.concatenate([after, rate], axis=1), preferred_element_type=f32)
    ratios = jnp.where(column <= row, jnp.exp(sums[:, :CH]), 0.0)
    growth = jnp.exp(sums[:, CH:])
    return strength, ratios, growth


def key_kernel(value_heads, rows, edge, taps, gates, t_out, kt_out, ktail_out, w_out, d_out, p_out, last_out, map_out, padded):
    kh = pl.program_id(0)
    blocks = rows.shape[0] // CH
    keys = unit_rows(conv_silu(rows, edge, taps, padded))
    row, column = grids()
    eye = jnp.where(row == column, 1.0, 0.0)
    strict = column < row
    problems = [(c, e) for c in range(blocks) for e in range(SHARE)]
    chunk = [keys[c * CH : (c + 1) * CH] for c in range(blocks)]
    turned = [jnp.transpose(x) for x in chunk]
    kk = [product(as_left(x), as_right(y)) for x, y in zip(chunk, turned)]
    for c in range(blocks):
        kt_out[0, c] = turned[c]
    lower, weights = {}, {}
    inverse = {}
    for c, e in problems:
        strength, ratios, growth = decay_terms(
            gates[c * CH : (c + 1) * CH, :], kh * SHARE + e, value_heads
        )
        system = jnp.where(strict, strength * kk[c] * ratios, 0.0)
        lower[c, e] = split(system)
        inverse[c, e] = eye - jnp.where((row // 2 == column // 2) & strict, system, 0.0)
        weights[c, e] = strength * growth * chunk[c]
        tail = as_left(turned[c] * ratios[CH - 1 : CH])
        ktail_out[0, c, e] = tail
        last_out[0, c, e] = growth[CH - 8 : CH]
        strength_row = jnp.dot(
            jnp.ones((8, CH), bf16),
            (strength * eye).astype(bf16),
            preferred_element_type=f32,
        )
        t_out[0, c, e] = jnp.broadcast_to(strength_row[0:1], (CH, CH)).astype(f32)
    size = 2
    while size < CH:
        mask = ones_where(
            (row // (2 * size) == column // (2 * size))
            & ((row // size) % 2 == 1)
            & ((column // size) % 2 == 0)
        )
        parts = {pc: split(inverse[pc]) for pc in problems}
        first = {
            pc: product(
                jnp.concatenate([lower[pc][0] * mask, lower[pc][1] * mask], axis=1),
                right_of(*parts[pc]),
            )
            for pc in problems
        }
        for pc in problems:
            inverse[pc] = inverse[pc] - product(
                jnp.concatenate(parts[pc], axis=1), as_right(first[pc])
            )
        size *= 2
    maps = {}
    for c, e in problems:
        solved = product(as_left(inverse[c, e]), as_right(weights[c, e]))
        w_out[0, c, e] = solved
        t_out[0, c, e] = inverse[c, e] * t_out[0, c, e]
        maps[c, e] = product(ktail_out[0, c, e], as_right(solved))
        d_out[0, c, e] = as_left(maps[c, e])
    for e in range(SHARE):
        running = last_out[0, 0, e][7:8] * eye - maps[0, e]
        for c in range(1, blocks):
            p_out[0, c - 1, e] = running
            running = last_out[0, c, e][7:8] * running - product(
                d_out[0, c, e], as_right(running)
            )
        map_out[e] = (eye - running).astype(bf16)


def value_kernel(rows, edge, taps, t_in, ktail, d_in, last, u_out, z_out, add_out, padded):
    blocks = rows.shape[0] // CH
    values = conv_silu(rows, edge, taps, padded)
    adds = {}
    for c in range(blocks):
        for e in range(SHARE):
            mine = values[c * CH : (c + 1) * CH, e * DV : (e + 1) * DV]
            written = product(as_left(t_in[0, c, e]), as_right(mine))
            u_out[0, c, e] = written
            adds[c, e] = product(ktail[0, c, e], as_right(written))
    running = [adds[0, e] for e in range(SHARE)]
    for c in range(1, blocks):
        for e in range(SHARE):
            z_out[0, c - 1, e] = running[e]
            running[e] = (
                last[0, c, e][7:8] * running[e]
                - product(d_in[0, c, e], as_right(running[e]))
                + adds[c, e]
            )
    for e in range(SHARE):
        add_out[e] = running[e].astype(bf16)


def query_kernel(value_heads, rows, edge, taps, gates, kt_in, w_in, p_in, u_in, z_in, f_out, g_out, padded):
    kh = pl.program_id(0)
    blocks = rows.shape[0] // CH
    queries = unit_rows(conv_silu(rows, edge, taps, padded)) * DK ** (-0.5)
    for c in range(blocks):
        mine = queries[c * CH : (c + 1) * CH]
        qk = product(as_left(mine), as_right(kt_in[0, c]))
        for e in range(SHARE):
            strength, ratios, growth = decay_terms(
                gates[c * CH : (c + 1) * CH, :], kh * SHARE + e, value_heads
            )
            mix = as_left(qk * ratios)
            entry = growth * mine - product(mix, as_right(w_in[0, c, e]))
            local = product(mix, as_right(u_in[0, c, e]))
            here = slice(c * CH, (c + 1) * CH)
            if c == 0:
                f_out[e, here] = as_left(entry)
                g_out[e, here] = local
            else:
                entry = as_left(entry)
                f_out[e, here] = as_left(product(entry, as_right(p_in[0, c - 1, e])))
                g_out[e, here] = local + product(entry, as_right(z_in[0, c - 1, e]))


def handoff_kernel(maps, adds, out):
    spans, heads = maps.shape[0], maps.shape[1]
    for h in range(heads):
        running = jnp.zeros(out.shape[2:], f32)
        for j in range(spans):
            out[j, h] = running.astype(bf16)
            if j + 1 < spans:
                high, low = split(running)
                erased = jnp.dot(maps[j, h], high, preferred_element_type=f32) + jnp.dot(
                    maps[j, h], low, preferred_element_type=f32
                )
                running = running - erased + adds[j, h].astype(f32)


def norm_kernel(order, f_in, g_in, state, gate, gain, out):
    heads = state.shape[0]
    for h in range(heads):
        both = jnp.concatenate([state[h], state[h]], axis=0)
        core = g_in[h] + jnp.dot(f_in[h], both, preferred_element_type=f32)
        scale = lax.rsqrt(jnp.mean(core * core, axis=-1, keepdims=True) + norm_floor)
        columns = slice(h * DV, (h + 1) * DV)
        gates = gate[:, columns].astype(f32)
        gates = gates / (1.0 + jnp.exp(-gates))
        out[0, :, columns] = (core * scale * gain[...] * gates).astype(bf16)


def shape(dims, kind):
    return jax.ShapeDtypeStruct(dims, kind)


def per_head(dims):
    return pl.BlockSpec((1,) + dims, lambda p: (p,) + (0,) * len(dims))


def columns_of(rows, width):
    return pl.BlockSpec((rows, width), lambda p: (0, p))


def key_terms(packed, edge, taps):
    tokens = packed.shape[0]
    key_heads = taps.shape[1] // DK
    blocks = tokens // CH
    sides = (blocks, SHARE, CH)
    return pl.pallas_call(
        functools.partial(key_kernel, key_heads * SHARE),
        grid=(key_heads,),
        in_specs=[
            columns_of(tokens, DK),
            columns_of(EDGE, DK),
            columns_of(taps.shape[0], DK),
            pl.BlockSpec((tokens, 128), lambda p: (0, key_heads)),
        ],
        out_specs=[
            per_head(sides + (CH,)),
            per_head((blocks, DK, CH)),
            per_head((blocks, SHARE, DK, 2 * CH)),
            per_head(sides + (DK,)),
            per_head((blocks, SHARE, DK, 2 * DK)),
            per_head((blocks - 1, SHARE, DK, DK)),
            per_head((blocks, SHARE, 8, CH)),
            pl.BlockSpec((SHARE, DK, DK), lambda p: (p, 0, 0)),
        ],
        out_shape=[
            shape((key_heads,) + sides + (CH,), f32),
            shape((key_heads, blocks, DK, CH), f32),
            shape((key_heads, blocks, SHARE, DK, 2 * CH), bf16),
            shape((key_heads,) + sides + (DK,), f32),
            shape((key_heads, blocks, SHARE, DK, 2 * DK), bf16),
            shape((key_heads, blocks - 1, SHARE, DK, DK), f32),
            shape((key_heads, blocks, SHARE, 8, CH), f32),
            shape((key_heads * SHARE, DK, DK), bf16),
        ],
        scratch_shapes=[pltpu.VMEM((tokens + 8, DK), f32)],
        compiler_params=params(),
        name="key_terms",
    )(packed, edge, taps, packed)


def value_terms(rows, edge, taps, t_in, ktail, d_in, last):
    tokens = rows.shape[0]
    key_heads = t_in.shape[0]
    blocks = tokens // CH
    width = SHARE * DV
    sides = (blocks, SHARE, CH)
    return pl.pallas_call(
        value_kernel,
        grid=(key_heads,),
        in_specs=[
            columns_of(tokens, width),
            columns_of(EDGE, width),
            columns_of(taps.shape[0], width),
            per_head(sides + (CH,)),
            per_head((blocks, SHARE, DK, 2 * CH)),
            per_head((blocks, SHARE, DK, 2 * DK)),
            per_head((blocks, SHARE, 8, CH)),
        ],
        out_specs=[
            per_head(sides + (DV,)),
            per_head((blocks - 1, SHARE, DK, DV)),
            pl.BlockSpec((SHARE, DK, DV), lambda p: (p, 0, 0)),
        ],
        out_shape=[
            shape((key_heads,) + sides + (DV,), f32),
            shape((key_heads, blocks - 1, SHARE, DK, DV), f32),
            shape((key_heads * SHARE, DK, DV), bf16),
        ],
        scratch_shapes=[pltpu.VMEM((tokens + 8, width), f32)],
        compiler_params=params(),
        name="value_terms",
    )(rows, edge, taps, t_in, ktail, d_in, last)


def query_terms(rows, edge, taps, packed, kt, w, p, u, z):
    tokens = rows.shape[0]
    key_heads = kt.shape[0]
    blocks = tokens // CH
    sides = (blocks, SHARE, CH)
    return pl.pallas_call(
        functools.partial(query_kernel, key_heads * SHARE),
        grid=(key_heads,),
        in_specs=[
            columns_of(tokens, DK),
            columns_of(EDGE, DK),
            columns_of(taps.shape[0], DK),
            pl.BlockSpec((tokens, 128), lambda p: (0, key_heads)),
            per_head((blocks, DK, CH)),
            per_head(sides + (DK,)),
            per_head((blocks - 1, SHARE, DK, DK)),
            per_head(sides + (DV,)),
            per_head((blocks - 1, SHARE, DK, DV)),
        ],
        out_specs=[
            pl.BlockSpec((SHARE, tokens, 2 * DK), lambda p: (p, 0, 0)),
            pl.BlockSpec((SHARE, tokens, DV), lambda p: (p, 0, 0)),
        ],
        out_shape=[
            shape((key_heads * SHARE, tokens, 2 * DK), bf16),
            shape((key_heads * SHARE, tokens, DV), f32),
        ],
        scratch_shapes=[pltpu.VMEM((tokens + 8, DK), f32)],
        compiler_params=params(),
        name="query_terms",
    )(rows, edge, taps, packed, kt, w, p, u, z)


def handoff(maps, adds):
    return pl.pallas_call(
        handoff_kernel,
        out_shape=shape(adds.shape, bf16),
        compiler_params=params(),
        name="handoff",
    )(maps, adds)


def normed_rows(order, f, g, state, gate, gain):
    heads, tokens = g.shape[0], g.shape[1]
    own = order.shape[0]
    size = tokens // (2 * own)
    return pl.pallas_call(
        norm_kernel,
        grid_spec=pltpu.PrefetchScalarGridSpec(
            num_scalar_prefetch=1,
            grid=(own,),
            in_specs=[
                pl.BlockSpec((heads, size, 2 * DK), lambda i, order: (0, order[i], 0)),
                pl.BlockSpec((heads, size, DV), lambda i, order: (0, order[i], 0)),
                pl.BlockSpec((heads, DK, DV), lambda i, order: (0, 0, 0)),
                pl.BlockSpec((size, heads * DV), lambda i, order: (order[i], 0)),
                pl.BlockSpec((1, DV), lambda i, order: (0, 0)),
            ],
            out_specs=pl.BlockSpec((1, size, heads * DV), lambda i, order: (i, 0, 0)),
        ),
        out_shape=shape((own, size, heads * DV), bf16),
        compiler_params=params(),
        name="normed_rows",
    )(order, f, g, state, gate, gain)


def by_group(rows, groups):
    return rows.reshape(rows.shape[0], groups, rows.shape[1] // groups).transpose(1, 0, 2)


def spread(pieces):
    got = lax.all_to_all(pieces, "head", 0, 0)
    return got.reshape(got.shape[0] * got.shape[1], got.shape[2])


def entry_states(maps, adds):
    spans = lax.axis_size("seq")
    heads = maps.shape[0]
    each = max(1, heads // spans)
    cuts = max(1, spans // heads)
    width = DV // cuts
    maps = maps.reshape(heads // each, each, DK, DK)
    maps = jnp.repeat(maps, cuts, axis=0) if cuts > 1 else maps
    adds = adds.reshape(heads // each, each, DK, cuts, width)
    adds = adds.transpose(0, 3, 1, 2, 4).reshape(spans, each, DK, width)
    maps = lax.all_to_all(maps, "seq", 0, 0)
    adds = lax.all_to_all(adds, "seq", 0, 0)
    entries = lax.all_to_all(handoff(maps, adds), "seq", 0, 0)
    entries = entries.reshape(heads // each, cuts, each, DK, width)
    return entries.transpose(0, 2, 3, 1, 4).reshape(heads, DK, DV)


def on_device(
    query_input,
    key_input,
    value_input,
    gate_input,
    write_strength,
    log_decay,
    filter_query,
    filter_key,
    filter_value,
    norm_gain,
    out_weight,
):
    groups = lax.axis_size("head")
    spans = lax.axis_size("seq")
    member = lax.axis_index("head")
    own_tokens = query_input.shape[0]

    edges = jnp.concatenate(
        [by_group(x[-EDGE:], groups) for x in (query_input, key_input, value_input)], axis=2
    )
    edge = None
    for h in range(groups):
        pairs = [(s * groups + groups - 1, (s + 1) * groups + h) for s in range(spans - 1)]
        moved = lax.ppermute(edges[h], ("seq", "head"), pairs)
        edge = moved if edge is None else edge + moved
    key_width = filter_key.shape[1]
    query_edge = edge[:, :key_width]
    key_edge = edge[:, key_width : 2 * key_width]
    value_edge = edge[:, 2 * key_width :]

    gates = jnp.concatenate(
        [by_group(write_strength, groups), by_group(log_decay, groups)], axis=2
    )
    gates = jnp.pad(gates, ((0, 0), (0, 0), (0, 128 - gates.shape[2])))
    packed = spread(jnp.concatenate([by_group(key_input, groups), gates], axis=2))
    value_rows = spread(by_group(value_input, groups))
    query_rows = spread(by_group(query_input, groups))
    gate_rows = spread(by_group(gate_input, groups))

    t, kt, ktail, w, d, p, last, maps = key_terms(packed, key_edge, filter_key)
    u, z, adds = value_terms(value_rows, value_edge, filter_value, t, ktail, d, last)
    f, g = query_terms(query_rows, query_edge, filter_query, packed, kt, w, p, u, z)
    state = entry_states(maps, adds)

    side = member % 2
    rank = member // 2
    ranks = groups // 2
    near = jnp.arange(ranks, dtype=jnp.int32) ^ rank
    gain = norm_gain.reshape(1, DV)
    swap = [(i, i ^ 1) for i in range(groups)]
    other_weight = lax.ppermute(out_weight, "head", swap)
    theirs = normed_rows(2 * near + 1 - side, f, g, state, gate_rows, gain)
    theirs = lax.ppermute(theirs, "head", swap)
    mine = normed_rows(2 * near + side, f, g, state, gate_rows, gain)
    total = None
    for step in range(ranks - 1, -1, -1):
        part = jnp.dot(mine[step], out_weight, preferred_element_type=f32) + jnp.dot(
            theirs[step], other_weight, preferred_element_type=f32
        )
        if step > 0:
            part = lax.ppermute(
                part.astype(bf16), "head", [(i, i ^ (2 * step)) for i in range(groups)]
            ).astype(f32)
        total = part if total is None else total + part
    return total.astype(bf16)


def solution(mesh):
    tokens = P(("seq", "head"), None)
    placed = (tokens,) * 6 + (P(None, "head"),) * 3 + (P(), P("head", None))
    return jax.shard_map(
        on_device, mesh=mesh, in_specs=placed, out_specs=tokens, check_vma=False
    )
```

time: 718 us -> 180 us (0.25); the launches traced: 708 us -> 178 us
  other arithmetic: 348 us -> 2.26 us
  matrix products: 116 us -> 8.17 us
  waiting for transfers between devices: 140 us -> 43.2 us
  Pallas kernels: 0 us -> 50.5 us
  between operations: 14.4 us -> 0.34 us
  starting transfers between devices: 60.1 us -> 46.8 us
    another operation x5 -> x0, other arithmetic: 318 us -> none  [the longest x4 317 us: stretch_terms(): jax.scipy.linalg.solve_triangular(system, right_side, lower=True, unit_di...]
    dot_general x46 -> x4, matrix products: 112 us -> 8.17 us  [the longest x2 6.74 us: on_device(): jnp.dot(theirs[step], other_weight, preferred_element_type=f32)]
    pallas_call x0 -> x6, Pallas kernels: none -> 50.5 us  [the longest x1 21 us: key_terms(): pl.pallas_call(functools.partial(key_kernel, key_heads * SHARE), grid=(ke...]
    reduce_scatter x1 -> x0, waiting for transfers between devices: 49 us -> none  [on_device(): lax.psum_scatter(jnp.dot(normed, out_weight, preferred_element_type=jnp.f...]
    ppermute x8 -> x7, waiting for transfers between devices: 58.8 us -> 12.9 us  [the longest x1 12.8 us: on_device(): lax.ppermute(part.astype(bf16), 'head', [(i, i ^ 2 * step) for i in range...]
    ppermute x8 -> x7, starting transfers between devices: 37.8 us -> 3.63 us  [the longest x4 2.66 us: on_device(): moved = lax.ppermute(edges[h], ('seq', 'head'), pairs)]
    all_to_all x6 -> x7, starting transfers between devices: 22.3 us -> 43.2 us  [the longest x1 18.8 us: entry_states(): maps = lax.all_to_all(maps, 'seq', 0, 0)]
    mul x7 -> x0, other arithmetic: 13.1 us -> none  [the longest x1 5.68 us: causal_local(): return jax.nn.silu(summed)]
  transfers between devices with their start and end apart: 15 -> 14, of which waited for: 14 -> 5; matrix products, arithmetic and copies ran while one was open for 3% -> 6% of each run, Pallas kernels for 0% -> 28%
where the time goes in v1:
time: 180 us; the launch traced here: 178 us
  Pallas kernels  50.5 us (28%)
  starting transfers between devices  46.8 us (26%)
  waiting for transfers between devices  43.2 us (24%)
  local copies, waits for them, and re-layouts  27.1 us (15%)
  matrix products  8.17 us (5%)
  other arithmetic  2.26 us (1%)
    all_to_all x4, waiting for transfers between devices, spread(): got = lax.all_to_all(pieces, 'head', 0, 0)  23.6 us
    pallas_call x1, Pallas kernels, key_terms(): pl.pallas_call(functools.partial(key_kernel, key_heads * SHARE), grid=(ke...  21 us
    unnamed x43, local copies, waits for them, and re-layouts  18.9 us
    all_to_all x1, starting transfers between devices, entry_states(): maps = lax.all_to_all(maps, 'seq', 0, 0)  18.8 us
    pallas_call x1, Pallas kernels, query_terms(): pl.pallas_call(functools.partial(query_kernel, key_heads * SHARE), grid=(...  16.8 us
    all_to_all x4, starting transfers between devices, spread(): got = lax.all_to_all(pieces, 'head', 0, 0)  14.7 us
    ppermute x1, waiting for transfers between devices, on_device(): lax.ppermute(part.astype(bf16), 'head', [(i, i ^ 2 * step) for i in range...  12.8 us
    pallas_call x1, Pallas kernels, value_terms(): pl.pallas_call(value_kernel, grid=(key_heads,), in_specs=[columns_of(toke...  7.34 us
  transfers between devices with their start and end apart: 14, of which 5 were waited for; matrix products, arithmetic and copies ran while one was open for 6% of the time, Pallas kernels for 28%

profile of v1, /device:TPU:0, one launch (start us, length us, event | category | flops | bytes accessed | tf_op | source)
XLA Modules:
  0.0 178.3 jit_solution(7360391602071871539)
XLA Ops:
  0.0 2.0 %copy.55 = bf16[16,4,8,512]{3,2,0,1:T(8,128)(2,1)} copy(bf16[16,4,8,512]{3,2,1,0:T(8,128)(2,1)} %bitcast.101) | data formatting | bytes 1048576 | tf_op jit(solution)/shard_map/reshape | solution.py:390
  2.0 4.2 %all-to-all-start = ((bf16[4,128,512]{2,1,0:T(8,128)(2,1)}), bf16[4,128,512]{2,1,0:T(8,128)(2,1)S(1)}, u32[]{:S(2)}, u32[]{:S(2)}) async-start(bf16[4,128,512]{2,1,0:T(8,128)(2,1)} %bitcast.82), calls=%async_computation | async-start | bytes 1048576 | tf_op jit(solution)/shard_map/all_to_all | solution.py:394
  6.2 1.1 copy.54
  7.3 0.7 pad_maximum_fusion.1
  8.0 0.1 copy.37
  8.1 0.9 fusion.2
  9.1 6.0 %all-to-all-done = bf16[4,128,512]{2,1,0:T(8,128)(2,1)S(1)} async-done(((bf16[4,128,512]{2,1,0:T(8,128)(2,1)}), bf16[4,128,512]{2,1,0:T(8,128)(2,1)S(1)}, u32[]{:S(2)}, u32[]{:S(2)}) %all-to-all-start) | async-done | bytes 524320 | tf_op jit(solution)/shard_map/all_to_all | solution.py:394
  15.0 3.5 %all-to-all-start.1 = ((bf16[4,128,640]{2,1,0:T(8,128)(2,1)}), bf16[4,128,640]{2,1,0:T(8,128)(2,1)S(1)}, u32[]{:S(2)}, u32[]{:S(2)}) async-start(bf16[4,128,640]{2,1,0:T(8,128)(2,1)} %fusion.2), calls=%async_computation.1 | async-start | bytes 1310720 | tf_op jit(solution)/shard_map/all_to_all | solution.py:394
  18.5 0.5 collective-permute-start.5
  19.0 0.8 slice.42
  19.8 0.8 slice.43
  20.7 1.1 copy.53
  21.8 6.9 %all-to-all-done.1 = bf16[4,128,640]{2,1,0:T(8,128)(2,1)S(1)} async-done(((bf16[4,128,640]{2,1,0:T(8,128)(2,1)}), bf16[4,128,640]{2,1,0:T(8,128)(2,1)S(1)}, u32[]{:S(2)}, u32[]{:S(2)}) %all-to-all-start.1) | async-done | bytes 655392 | tf_op jit(solution)/shard_map/all_to_all | solution.py:394
  28.7 3.5 %all-to-all-start.2 = ((bf16[4,128,1024]{2,1,0:T(8,128)(2,1)}), bf16[4,128,1024]{2,1,0:T(8,128)(2,1)S(1)}, u32[]{:S(2)}, u32[]{:S(2)}) async-start(bf16[4,128,1024]{2,1,0:T(8,128)(2,1)} %bitcast.78), calls=%async_computation.2 | async-start | bytes 2097152 | tf_op jit(solution)/shard_map/all_to_all | solution.py:394
  32.3 0.7 collective-permute-start
  33.0 0.7 collective-permute-start.1
  33.6 0.7 collective-permute-start.2
  34.3 0.7 collective-permute-start.3
  35.0 0.0 collective-permute-done.2
  35.0 0.0 collective-permute-done.3
  35.1 0.0 copy-start.14
  35.1 0.7 copy-done.14
  35.8 21.0 %key_terms.1 = (f32[4,4,2,128,128]{4,3,2,1,0:T(8,128)S(1)}, f32[4,4,128,128]{3,2,1,0:T(8,128)S(1)}, bf16[4,4,2,128,256]{4,3,2,1,0:T(8,128)(2,1)}, f32[4,4,2,128,...) custom-call(bf16[512,640]{1,0:T(8,128)(2,1)S(1)} %bitcast.85, ...), custom_call_target="tpu_custom_call" | custom-call | tf_op jit(solution)/shard_map/key_terms/pallas_call | solution.py:254
  56.8 1.4 copy-done.2
  58.2 1.1 copy-done.4
  59.3 0.7 copy-done.11
  60.0 18.8 %all-to-all-start.3 = ((bf16[8,1,128,128]{3,2,1,0:T(8,128)(2,1)}), bf16[8,1,128,128]{3,2,1,0:T(8,128)(2,1)}, u32[]{:S(2)}, u32[]{:S(2)}) async-start(bf16[8,1,128,128]{3,2,1,0:T(8,128)(2,1)} %bitcast.17), calls=%async_computation.3 | async-start | bytes 524288 | tf_op jit(solution)/shard_map/all_to_all | solution.py:408
  78.8 0.9 copy-done.12
  79.7 0.7 copy-done.13
  80.4 7.3 %value_terms.1 = (f32[4,4,2,128,128]{4,3,2,1,0:T(8,128)S(1)}, f32[4,3,2,128,128]{4,3,2,1,0:T(8,128)S(1)}, bf16[8,128,128]{2,1,0:T(8,128)(2,1)}) custom-call(bf16[512,1024]{1,0:T(8,128)(2,1)S(1)} %bitcast.90, bf16[16,1024]{1,0:T(8,128)(2,1)S(1)} %slice.62.edge, bf16[4,1024]{1,0:T(4,128)(2,1)S(1)} %copy-done.13, f32[4,4,2,128,128]{4,3,2,1,0:T(8,128)} %copy-done.2, ...), custom_call_target="tpu_custom_call" | custom-call | tf_op jit(solution)/shard_map/value_terms/pallas_call | solution.py:295
  87.8 1.4 copy-done.3
  89.2 1.1 copy-done.6
  90.3 6.0 %all-to-all-start.4 = ((bf16[8,1,128,128]{3,2,1,0:T(8,128)(2,1)}), bf16[8,1,128,128]{3,2,1,0:T(8,128)(2,1)S(1)}, u32[]{:S(2)}, u32[]{:S(2)}) async-start(bf16[8,1,128,128]{3,2,1,0:T(8,128)(2,1)} %bitcast.18), calls=%async_computation.4 | async-start | bytes 524288 | tf_op jit(solution)/shard_map/all_to_all | solution.py:409
  96.3 2.3 %copy.52 = bf16[16,4,8,1024]{3,2,0,1:T(8,128)(2,1)} copy(bf16[16,4,8,1024]{3,2,1,0:T(8,128)(2,1)} %bitcast.100) | data formatting | bytes 2097152 | tf_op jit(solution)/shard_map/reshape | solution.py:390
  98.6 6.7 %all-to-all-done.4.adds = bf16[8,1,128,128]{3,2,1,0:T(8,128)(2,1)S(1)} async-done(((bf16[8,1,128,128]{3,2,1,0:T(8,128)(2,1)}), bf16[8,1,128,128]{3,2,1,0:T(8,128)(2,1)S(1)}, u32[]{:S(2)}, u32[]{:S(2)}) %all-to-all-start.4) | async-done | bytes 262176 | tf_op jit(solution)/shard_map/all_to_all | solution.py:409
  105.4 0.7 copy-done.9
  106.1 3.5 %all-to-all-start.6 = ((bf16[4,128,1024]{2,1,0:T(8,128)(2,1)}), bf16[4,128,1024]{2,1,0:T(8,128)(2,1)S(1)}, u32[]{:S(2)}, u32[]{:S(2)}) async-start(bf16[4,128,1024]{2,1,0:T(8,128)(2,1)} %bitcast.96), calls=%async_computation.6 | async-start | bytes 2097152 | tf_op jit(solution)/shard_map/all_to_all | solution.py:394
  109.6 0.0 copy-start.10
  109.6 0.9 copy-done.10
  110.5 2.0 %handoff.1 = bf16[8,1,128,128]{3,2,1,0:T(8,128)(2,1)S(1)} custom-call(bf16[8,1,128,128]{3,2,1,0:T(8,128)(2,1)} %all-to-all-done.3.maps, bf16[8,1,128,128]{3,2,1,0:T(8,128)(2,1)S(1)} %copy-done.10), custom_call_target="tpu_custom_call" | custom-call | tf_op jit(solution)/shard_map/handoff/pallas_call | solution.py:357
  112.6 0.0 copy-start.8
  112.6 0.7 copy-done.8
  113.3 10.7 %all-to-all-done.6 = bf16[4,128,1024]{2,1,0:T(8,128)(2,1)S(1)} async-done(((bf16[4,128,1024]{2,1,0:T(8,128)(2,1)}), bf16[4,128,1024]{2,1,0:T(8,128)(2,1)S(1)}, u32[]{:S(2)}, u32[]{:S(2)}) %all-to-all-start.6) | async-done | bytes 1048608 | tf_op jit(solution)/shard_map/all_to_all | solution.py:394
  124.0 3.6 %all-to-all-start.5 = ((bf16[8,1,128,128]{3,2,1,0:T(8,128)(2,1)}), bf16[8,1,128,128]{3,2,1,0:T(8,128)(2,1)S(1)}, u32[]{:S(2)}, u32[]{:S(2)}) async-start(bf16[8,1,128,128]{3,2,1,0:T(8,128)(2,1)} %copy-done.8), calls=%async_computation.5 | async-start | bytes 524288 | tf_op jit(solution)/shard_map/all_to_all | solution.py:410
  127.6 0.6 add_subtract_fusion.order
  128.2 1.4 copy-done.5
  129.6 1.4 copy-done.7
  131.0 0.7 copy-done.15
  131.7 16.8 %query_terms.1 = (bf16[8,512,256]{2,1,0:T(8,128)(2,1)}, f32[8,512,128]{2,1,0:T(8,128)}) custom-call(bf16[512,512]{1,0:T(8,128)(2,1)S(1)} %bitcast.93, bf16[16,512]{1,0:T(8,128)(2,1)S(1)} %get-tuple-element.36.edge, bf16[4,512]{1,0:T(4,128)(2,1)S(1)} %copy-done.15, bf16[512,640]{1,0:T(8,128)(2,1)S(1)} %bitcast.87, ...), custom_call_target="tpu_custom_call" | custom-call | tf_op jit(solution)/shard_map/query_terms/pallas_call | solution.py:328
  148.5 1.6 copy-done
  150.1 1.6 copy-done.1
  151.7 0.7 copy-done.16
  152.3 0.7 copy-done.18
  153.0 1.7 normed_rows.3
  154.7 0.0 copy-start.19
  154.7 0.1 collective-permute-start.4
  154.8 1.7 normed_rows.2
  156.5 0.4 copy-done.19
  156.8 0.7 fusion.4
  157.6 2.9 %fusion = bf16[128,2048]{1,0:T(8,128)(2,1)S(1)} fusion(f32[128,2048]{1,0:T(8,128)S(1)} %fusion.4, bf16[1024,2048]{1,0:T(8,128)(2,1)} %collective-permute-done.5, bf16[2,128,1024]{2,1,0:T(8,128)(2,1)S(1)} %collective-permute-done.4), kind=kOutput, calls=%fused_computation.2 | convolution fusion | flops 537395200 | bytes 6029312 | tf_op jit(solution)/shard_map/dot_general | solution.py:472
  160.5 0.4 collective-permute-start.6
  161.0 0.7 fusion.3
  161.7 12.8 %collective-permute-done.6 = bf16[128,2048]{1,0:T(8,128)(2,1)S(1)} collective-permute-done((bf16[128,2048]{1,0:T(8,128)(2,1)S(1)}, bf16[128,2048]{1,0:T(8,128)(2,1)S(1)}, u32[]{:S(2)}, u32[]{:S(2)}) %collective-permute-start.6) | collective-permute-done | bytes 524320 | tf_op jit(solution)/shard_map/ppermute | solution.py:476
  174.5 3.8 %add_convert_fusion = bf16[128,2048]{1,0:T(8,128)(2,1)} fusion(bf16[128,2048]{1,0:T(8,128)(2,1)S(1)} %collective-permute-done.6, f32[128,2048]{1,0:T(8,128)S(1)} %fusion.3, bf16[1024,2048]{1,0:T(8,128)(2,1)} %collective-permute-done.5, bf16[2,128,1024]{2,1,0:T(8,128)(2,1)S(1)} %collective-permute-done.4), kind=kOutput, calls=%fused_computation.7 | convolution fusion | flops 537919488 | bytes 6553600 | tf_op jit(solution)/shard_map/dot_general | solution.py:472
  (36 shorter events, 0.1 us)
Async XLA Ops:
  0.0 20.7 %slice-start = ((bf16[128,4096]{1,0:T(8,128)(2,1)}), bf16[16,4096]{1,0:T(8,128)(2,1)S(1)}, s32[]{:S(2)}) async-start(bf16[128,4096]{1,0:T(8,128)(2,1)} %param.13), calls=%async_computation.7 | async-start | bytes 262144 | tf_op jit(solution)/shard_map/slice | solution.py:434
  0.0 20.7 %copy-start.20 = (bf16[128,4096]{1,0:T(8,128)(2,1)S(1)}, bf16[128,4096]{1,0:T(8,128)(2,1)}, u32[]{:S(2)}) copy-start(bf16[128,4096]{1,0:T(8,128)(2,1)} %param.13) | copy-start | bytes 3145732
  2.0 13.1 %all-to-all-start = ((bf16[4,128,512]{2,1,0:T(8,128)(2,1)}), bf16[4,128,512]{2,1,0:T(8,128)(2,1)S(1)}, u32[]{:S(2)}, u32[]{:S(2)}) async-start(bf16[4,128,512]{2,1,0:T(8,128)(2,1)} %bitcast.82), calls=%async_computation | async-start | bytes 1048576 | tf_op jit(solution)/shard_map/all_to_all | solution.py:394
  15.0 13.7 %all-to-all-start.1 = ((bf16[4,128,640]{2,1,0:T(8,128)(2,1)}), bf16[4,128,640]{2,1,0:T(8,128)(2,1)S(1)}, u32[]{:S(2)}, u32[]{:S(2)}) async-start(bf16[4,128,640]{2,1,0:T(8,128)(2,1)} %fusion.2), calls=%async_computation.1 | async-start | bytes 1310720 | tf_op jit(solution)/shard_map/all_to_all | solution.py:394
  18.5 139.1 %collective-permute-start.5 = (bf16[1024,2048]{1,0:T(8,128)(2,1)}, bf16[1024,2048]{1,0:T(8,128)(2,1)}, u32[]{:S(2)}, u32[]{:S(2)}) collective-permute-start(bf16[1024,2048]{1,0:T(8,128)(2,1)} %param.21), channel_id=1, source_target_pairs={{0,1},{1,0},{2,3},{3,2},{4,5},{5,4},{6,7},{7,6},{8,9},{9,8},{10,11... | collective-permute-start | bytes 12582920 | tf_op jit(solution)/shard_map/ppermute | solution.py:466
  28.7 31.2 %all-to-all-start.2 = ((bf16[4,128,1024]{2,1,0:T(8,128)(2,1)}), bf16[4,128,1024]{2,1,0:T(8,128)(2,1)S(1)}, u32[]{:S(2)}, u32[]{:S(2)}) async-start(bf16[4,128,1024]{2,1,0:T(8,128)(2,1)} %bitcast.78), calls=%async_computation.2 | async-start | bytes 2097152 | tf_op jit(solution)/shard_map/all_to_all | solution.py:394
  32.3 2.7 %collective-permute-start = (bf16[16,2048]{1,0:T(8,128)(2,1)S(1)}, bf16[16,2048]{1,0:T(8,128)(2,1)S(1)}, u32[]{:S(2)}, u32[]{:S(2)}) collective-permute-start(bf16[16,2048]{1,0:T(8,128)(2,1)S(1)} %get-tuple-element.34), channel_id=1, source_target_pairs={{3,4},{7,8},{11,12},{15,16},{19,20},{23,24},{27,28}} | collective-permute-start | bytes 196616 | tf_op jit(solution)/shard_map/ppermute | solution.py:439
  33.0 2.0 %collective-permute-start.1 = (bf16[16,2048]{1,0:T(8,128)(2,1)S(1)}, bf16[16,2048]{1,0:T(8,128)(2,1)S(1)}, u32[]{:S(2)}, u32[]{:S(2)}) collective-permute-start(bf16[16,2048]{1,0:T(8,128)(2,1)S(1)} %get-tuple-element.31), channel_id=1, source_target_pairs={{3,5},{7,9},{11,13},{15,17},{19,21},{23,25},{27,29}} | collective-permute-start | bytes 196616 | tf_op jit(solution)/shard_map/ppermute | solution.py:439
  33.6 1.4 collective-permute-start.2
  34.3 0.7 collective-permute-start.3
  35.1 0.7 copy-start.14
  56.8 1.4 copy-start.2
  58.2 1.1 copy-start.4
  59.3 0.7 copy-start.11
  60.0 30.3 %all-to-all-start.3 = ((bf16[8,1,128,128]{3,2,1,0:T(8,128)(2,1)}), bf16[8,1,128,128]{3,2,1,0:T(8,128)(2,1)}, u32[]{:S(2)}, u32[]{:S(2)}) async-start(bf16[8,1,128,128]{3,2,1,0:T(8,128)(2,1)} %bitcast.17), calls=%async_computation.3 | async-start | bytes 524288 | tf_op jit(solution)/shard_map/all_to_all | solution.py:408
  78.8 0.9 copy-start.12
  79.7 0.7 copy-start.13
  87.8 1.4 copy-start.3
  89.2 1.1 copy-start.6
  90.3 15.0 %all-to-all-start.4 = ((bf16[8,1,128,128]{3,2,1,0:T(8,128)(2,1)}), bf16[8,1,128,128]{3,2,1,0:T(8,128)(2,1)S(1)}, u32[]{:S(2)}, u32[]{:S(2)}) async-start(bf16[8,1,128,128]{3,2,1,0:T(8,128)(2,1)} %bitcast.18), calls=%async_computation.4 | async-start | bytes 524288 | tf_op jit(solution)/shard_map/all_to_all | solution.py:409
  105.4 0.7 copy-start.9
  106.1 18.0 %all-to-all-start.6 = ((bf16[4,128,1024]{2,1,0:T(8,128)(2,1)}), bf16[4,128,1024]{2,1,0:T(8,128)(2,1)S(1)}, u32[]{:S(2)}, u32[]{:S(2)}) async-start(bf16[4,128,1024]{2,1,0:T(8,128)(2,1)} %bitcast.96), calls=%async_computation.6 | async-start | bytes 2097152 | tf_op jit(solution)/shard_map/all_to_all | solution.py:394
  109.6 1.0 copy-start.10
  112.6 0.7 copy-start.8
  124.0 24.5 %all-to-all-start.5 = ((bf16[8,1,128,128]{3,2,1,0:T(8,128)(2,1)}), bf16[8,1,128,128]{3,2,1,0:T(8,128)(2,1)S(1)}, u32[]{:S(2)}, u32[]{:S(2)}) async-start(bf16[8,1,128,128]{3,2,1,0:T(8,128)(2,1)} %copy-done.8), calls=%async_computation.5 | async-start | bytes 524288 | tf_op jit(solution)/shard_map/all_to_all | solution.py:410
  128.2 1.4 copy-start.5
  129.6 1.4 copy-start.7
  131.0 0.7 copy-start.15
  148.5 6.3 %copy-start.17 = (f32[128]{0:T(128)S(1)}, f32[128]{0:T(128)}, u32[]{:S(2)}) copy-start(f32[128]{0:T(128)} %param.20) | copy-start | bytes 1540
  148.5 1.6 copy-start
  150.1 1.6 copy-start.1
  151.7 0.7 copy-start.16
  152.3 0.7 copy-start.18
  154.7 2.2 %copy-start.19 = (bf16[1024,2048]{1,0:T(8,128)(2,1)S(1)}, bf16[1024,2048]{1,0:T(8,128)(2,1)}, u32[]{:S(2)}) copy-start(bf16[1024,2048]{1,0:T(8,128)(2,1)} %param.21) | copy-start | bytes 12582916
  154.7 2.9 %collective-permute-start.4 = (bf16[2,128,1024]{2,1,0:T(8,128)(2,1)S(1)}, bf16[2,128,1024]{2,1,0:T(8,128)(2,1)S(1)}, u32[]{:S(2)}, u32[]{:S(2)}) collective-permute-start(bf16[2,128,1024]{2,1,0:T(8,128)(2,1)S(1)} %normed_rows.3), channel_id=1, source_target_pairs={{0,1},{1,0},{2,3},{3,2},{4,5},{5,4},{6,7},{7,6},{8,9},{9,8},{10,11... | collective-permute-start | bytes 1572872 | tf_op jit(solution)/shard_map/ppermute | solution.py:468
  160.5 14.0 %collective-permute-start.6 = (bf16[128,2048]{1,0:T(8,128)(2,1)S(1)}, bf16[128,2048]{1,0:T(8,128)(2,1)S(1)}, u32[]{:S(2)}, u32[]{:S(2)}) collective-permute-start(bf16[128,2048]{1,0:T(8,128)(2,1)S(1)} %fusion), channel_id=1, source_target_pairs={{0,2},{1,3},{2,0},{3,1},{4,6},{5,7},{6,4},{7,5},{8,10},{9,11},{10,... | collective-permute-start | bytes 1572872 | tf_op jit(solution)/shard_map/ppermute | solution.py:476

commit v2 on v0

v2 whole, which is shorter than its diff:
```python
import functools

import jax
import jax.numpy as jnp
from jax import lax
from jax.experimental import pallas as pl
from jax.experimental.pallas import tpu as pltpu
from jax.sharding import PartitionSpec as P

HK = 16
HV = 32
DK = 128
DV = 128
CH = 128
EDGE = 16
SHARE = HV // HK

norm_floor = 1e-06
f32 = jnp.float32
bf16 = jnp.bfloat16


def params(megabytes=60):
    return pltpu.CompilerParams(vmem_limit_bytes=megabytes * 1024 * 1024)


def split(x):
    high = x.astype(bf16)
    return high, (x - high.astype(f32)).astype(bf16)


def as_left(x):
    return jnp.concatenate(split(x), axis=1)


def right_of(high, low):
    row = jnp.concatenate([high, low], axis=1)
    return jnp.concatenate([row, row], axis=0)


def as_right(x):
    return right_of(*split(x))


def product(left, right):
    both = jnp.dot(left, right, preferred_element_type=f32)
    half = both.shape[1] // 2
    return both[:, :half] + both[:, half:]


def grids():
    row = lax.broadcasted_iota(jnp.int32, (CH, CH), 0)
    column = lax.broadcasted_iota(jnp.int32, (CH, CH), 1)
    return row, column


def ones_where(mask):
    return jnp.where(mask, 1.0, 0.0).astype(bf16)


def place(me, pieces, out, margin):
    size = pieces[0].shape[0]
    for d, piece in enumerate(pieces):
        at = pl.multiple_of((me ^ d) * size + margin, 8)
        out[pl.ds(at, size), :] = piece[...].astype(out.dtype)


def conv_silu(me, pieces, edges, taps_ref, padded):
    length = padded.shape[0] - 8
    taps = taps_ref[...].astype(f32)
    edge = edges[0][...].astype(f32)
    for other in edges[1:]:
        edge = edge + other[...].astype(f32)
    padded[0:8] = edge[EDGE - 8 : EDGE]
    place(me, pieces, padded, 8)
    margin = taps.shape[0] - 1
    summed = taps[margin : margin + 1] * padded[8 : 8 + length]
    for offset in range(margin):
        start = 8 - margin + offset
        summed = summed + taps[offset : offset + 1] * padded[start : start + length]
    return summed / (1.0 + jnp.exp(-summed))


def unit_rows(field):
    return field * lax.rsqrt(jnp.sum(field * field, axis=-1, keepdims=True) + norm_floor)


def strengths_and_rates(gates, first, count):
    lane = lax.broadcasted_iota(jnp.int32, (gates.shape[1], CH), 0)
    picks = [ones_where(lane == first + e) for e in range(count)]
    picks += [ones_where(lane == HV + first + e) for e in range(count)]
    picked = jnp.dot(gates, jnp.concatenate(picks, axis=1), preferred_element_type=f32)
    return picked[:, : count * CH], picked[:, count * CH :].astype(bf16)


def decay_terms(rates, count):
    row, column = grids()
    below = ones_where(column <= row)
    pieces = []
    for e in range(count):
        rate = rates[:, e * CH : (e + 1) * CH]
        pieces += [jnp.where(row > column, rate, jnp.zeros_like(rate)), rate]
    sums = jnp.dot(below, jnp.concatenate(pieces, axis=1), preferred_element_type=f32)
    ratios, growth = [], []
    for e in range(count):
        at = 2 * e * CH
        ratios.append(jnp.where(column <= row, jnp.exp(sums[:, at : at + CH]), 0.0))
        growth.append(jnp.exp(sums[:, at + CH : at + 2 * CH]))
    return ratios, growth


def unit_lower_inverses(lower):
    row, column = grids()
    names = list(lower)
    eye = jnp.where(row == column, 1.0, 0.0)
    pair = (row // 2 == column // 2) & (column < row)
    halves = {n: split(lower[n]) for n in names}
    inverse = {n: eye - jnp.where(pair, lower[n], 0.0) for n in names}
    size = 2
    while size < CH:
        mask = ones_where(
            (row // (2 * size) == column // (2 * size))
            & ((row // size) % 2 == 1)
            & ((column // size) % 2 == 0)
        )
        rounded = {n: inverse[n].astype(bf16) for n in names}
        first = {
            n: jnp.dot(halves[n][0] * mask, rounded[n], preferred_element_type=f32).astype(bf16)
            for n in names
        }
        for n in names:
            inverse[n] = inverse[n] - jnp.dot(rounded[n], first[n], preferred_element_type=f32)
        size *= 2
    parts = {n: split(inverse[n]) for n in names}
    left = {
        n: (
            eye
            - inverse[n]
            - product(jnp.concatenate(halves[n], axis=1), right_of(*parts[n]))
        ).astype(bf16)
        for n in names
    }
    return {
        n: inverse[n] + jnp.dot(parts[n][0], left[n], preferred_element_type=f32) for n in names
    }


def key_kernel(groups_count, heads, member, *refs):
    pieces, refs = refs[:groups_count], refs[groups_count:]
    edges, refs = refs[:groups_count], refs[groups_count:]
    gate_pieces, refs = refs[:groups_count], refs[groups_count:]
    taps, t_out, kt_out, ktail_out, w_out, d_out, p_out, last_out, map_out, padded, gates = refs
    here = pieces[0].shape[1] // DK
    count = here * SHARE
    blocks = gates.shape[0] // CH
    me = member[0]
    first = me * heads + pl.program_id(0) * count
    filtered = conv_silu(me, pieces, edges, taps, padded)
    place(me, gate_pieces, gates, 0)
    row, column = grids()
    eye = jnp.where(row == column, 1.0, 0.0)
    groups = [(c, k) for c in range(blocks) for k in range(here)]
    problems = [(c, e) for c in range(blocks) for e in range(count)]

    def chunk_of(x, c):
        return x[c * CH : (c + 1) * CH]

    strengths, rates = strengths_and_rates(gates[...], first, count)
    unit = [unit_rows(filtered[:, k * DK : (k + 1) * DK]) for k in range(here)]
    decays = [decay_terms(chunk_of(rates, c), count) for c in range(blocks)]
    keys = {(c, k): chunk_of(unit[k], c) for c, k in groups}
    turned = {g: jnp.transpose(keys[g]) for g in groups}
    sides = {g: split(turned[g]) for g in groups}
    kk = {g: product(as_left(keys[g]), right_of(*sides[g])) for g in groups}
    lane = lax.broadcasted_iota(jnp.int32, (8, gates.shape[1]), 1)
    order = lax.broadcasted_iota(jnp.int32, (8, gates.shape[1]), 0)
    pick = ones_where(lane == first + order)
    across = [
        lax.dot_general(
            pick,
            gates[c * CH : (c + 1) * CH, :],
            (((1,), (1,)), ((), ())),
            preferred_element_type=f32,
        )
        for c in range(blocks)
    ]
    lower, ktail = {}, {}
    for c, k in groups:
        kt_out[k, c] = jnp.concatenate(sides[c, k], axis=1)
    for c, e in problems:
        ratios, growth = decays[c][0][e], decays[c][1][e]
        strength = chunk_of(strengths, c)[:, e * CH : (e + 1) * CH]
        k = e // SHARE
        lower[c, e] = jnp.where(column < row, strength * kk[c, k] * ratios, 0.0)
        ktail[c, e] = as_left(turned[c, k] * ratios[CH - 1 : CH])
        ktail_out[k, c, e % SHARE] = ktail[c, e]
        last_out[k, c, e % SHARE] = growth[CH - 8 : CH]
    inverse = unit_lower_inverses(lower)
    solving = {(c, e): as_left(inverse[c, e] * across[c][e : e + 1]) for c, e in problems}
    solved = {
        (c, e): product(solving[c, e], as_right(decays[c][1][e] * keys[c, e // SHARE]))
        for c, e in problems
    }
    erasing = {pc: split(solved[pc]) for pc in problems}
    maps = {pc: as_left(product(ktail[pc], right_of(*erasing[pc]))) for pc in problems}
    for c, e in problems:
        k = e // SHARE
        t_out[k, c, e % SHARE] = solving[c, e]
        w_out[k, c, e % SHARE] = jnp.concatenate(erasing[c, e], axis=1)
        d_out[k, c, e % SHARE] = maps[c, e]
    running = []
    for e in range(count):
        high, low = maps[0, e][:, :DK], maps[0, e][:, DK:]
        running.append(
            decays[0][1][e][CH - 1 : CH] * eye - (high.astype(f32) + low.astype(f32))
        )
    for c in range(1, blocks):
        parts = [split(x) for x in running]
        for e in range(count):
            p_out[e // SHARE, c - 1, e % SHARE] = jnp.concatenate(parts[e], axis=1)
        running = [
            decays[c][1][e][CH - 1 : CH] * running[e] - product(maps[c, e], right_of(*parts[e]))
            for e in range(count)
        ]
    for e in range(count):
        map_out[e] = (eye - running[e]).astype(bf16)


def right_from(both):
    return jnp.concatenate([both, both], axis=0)


def value_kernel(groups_count, member, *refs):
    pieces, refs = refs[:groups_count], refs[groups_count:]
    edges, refs = refs[:groups_count], refs[groups_count:]
    taps, t_in, ktail, d_in, last, u_out, z_out, add_out, padded = refs
    blocks = t_in.shape[1]
    count = pieces[0].shape[1] // DV
    values = conv_silu(member[0], pieces, edges, taps, padded)
    problems = [(c, e) for c in range(blocks) for e in range(count)]

    def at(ref, c, e):
        return ref[e // SHARE, c, e % SHARE]

    written = {
        (c, e): split(
            product(
                at(t_in, c, e),
                as_right(values[c * CH : (c + 1) * CH, e * DV : (e + 1) * DV]),
            )
        )
        for c, e in problems
    }
    adds = {pc: product(at(ktail, *pc), right_of(*written[pc])) for pc in problems}
    for c, e in problems:
        u_out[e // SHARE, c, e % SHARE] = jnp.concatenate(written[c, e], axis=1)
    running = [adds[0, e] for e in range(count)]
    for c in range(1, blocks):
        parts = [split(x) for x in running]
        for e in range(count):
            z_out[e // SHARE, c - 1, e % SHARE] = jnp.concatenate(parts[e], axis=1)
        running = [
            at(last, c, e)[7:8] * running[e]
            - product(at(d_in, c, e), right_of(*parts[e]))
            + adds[c, e]
            for e in range(count)
        ]
    for e in range(count):
        add_out[e] = running[e].astype(bf16)


def query_kernel(groups_count, heads, member, *refs):
    pieces, refs = refs[:groups_count], refs[groups_count:]
    edges, refs = refs[:groups_count], refs[groups_count:]
    gate_pieces, refs = refs[:groups_count], refs[groups_count:]
    taps, kt_in, w_in, p_in, u_in, z_in, f_out, g_out, padded, gates = refs
    here = pieces[0].shape[1] // DK
    count = here * SHARE
    blocks = gates.shape[0] // CH
    me = member[0]
    first = me * heads + pl.program_id(0) * count
    filtered = conv_silu(me, pieces, edges, taps, padded)
    place(me, gate_pieces, gates, 0)
    unit = [unit_rows(filtered[:, k * DK : (k + 1) * DK]) * DK ** (-0.5) for k in range(here)]
    problems = [(c, e) for c in range(blocks) for e in range(count)]
    strengths, rates = strengths_and_rates(gates[...], first, count)
    decays = [decay_terms(rates[c * CH : (c + 1) * CH], count) for c in range(blocks)]

    def at(ref, c, e):
        return right_from(ref[e // SHARE, c, e % SHARE])

    queries = {
        (c, k): unit[k][c * CH : (c + 1) * CH] for c in range(blocks) for k in range(here)
    }
    qk = {
        (c, k): product(as_left(queries[c, k]), right_from(kt_in[k, c])) for c, k in queries
    }
    mix = {(c, e): as_left(qk[c, e // SHARE] * decays[c][0][e]) for c, e in problems}
    entry = {
        (c, e): as_left(
            decays[c][1][e] * queries[c, e // SHARE] - product(mix[c, e], at(w_in, c, e))
        )
        for c, e in problems
    }
    local = {pc: product(mix[pc], at(u_in, *pc)) for pc in problems}
    for c, e in problems:
        here = slice(c * CH, (c + 1) * CH)
        if c == 0:
            f_out[e, here] = entry[c, e]
            g_out[e, here] = local[c, e]
        else:
            f_out[e, here] = as_left(product(entry[c, e], at(p_in, c - 1, e)))
            g_out[e, here] = local[c, e] + product(entry[c, e], at(z_in, c - 1, e))


def handoff_kernel(maps, adds, out):
    spans, heads = maps.shape[0], maps.shape[1]
    width = out.shape[3]
    running = [jnp.zeros(out.shape[2:], f32) for h in range(heads)]
    for j in range(spans):
        for h in range(heads):
            out[j, h] = running[h].astype(bf16)
        if j + 1 < spans:
            for h in range(heads):
                high, low = split(running[h])
                both = jnp.concatenate([high, low], axis=1) if width % 128 == 0 else None
                if both is None:
                    erased = jnp.dot(maps[j, h], high, preferred_element_type=f32)
                    erased = erased + jnp.dot(maps[j, h], low, preferred_element_type=f32)
                else:
                    erased = jnp.dot(maps[j, h], both, preferred_element_type=f32)
                    erased = erased[:, :width] + erased[:, width:]
                running[h] = running[h] - erased + adds[j, h].astype(f32)


def norm_kernel(count, member, *refs):
    f_in, refs = refs[:count], refs[count:]
    g_in, refs = refs[:count], refs[count:]
    gate, refs = refs[:count], refs[count:]
    state, gain, out = refs
    heads = state.shape[0]
    cells = [(i, h) for i in range(count) for h in range(heads)]
    states = [jnp.concatenate([state[h], state[h]], axis=0) for h in range(heads)]
    core = {
        (i, h): g_in[i][h] + jnp.dot(f_in[i][h], states[h], preferred_element_type=f32)
        for i, h in cells
    }
    scale = {
        n: lax.rsqrt(jnp.mean(core[n] * core[n], axis=-1, keepdims=True) + norm_floor)
        for n in cells
    }
    for i, h in cells:
        columns = slice(h * DV, (h + 1) * DV)
        gates = gate[i][:, columns].astype(f32)
        gates = gates / (1.0 + jnp.exp(-gates))
        out[i, :, columns] = (core[i, h] * scale[i, h] * gain[...] * gates).astype(bf16)


def project_kernel(mine, theirs, own_weight, other_weight, kept, *sent):
    rows, depth = mine.shape[0] * mine.shape[1], mine.shape[2]
    product_ = jnp.dot(
        mine[...].reshape(rows, depth), own_weight[...], preferred_element_type=f32
    ) + jnp.dot(theirs[...].reshape(rows, depth), other_weight[...], preferred_element_type=f32)
    size = mine.shape[1]
    kept[...] = product_[:size]
    for i, out in enumerate(sent):
        out[...] = product_[(i + 1) * size : (i + 2) * size].astype(bf16)


def pack_kernel(groups_count, member, *refs):
    array, outs = refs[0], refs[1:]
    me = member[0]
    width = array.shape[1] // groups_count
    for d in range(groups_count):
        at = pl.multiple_of((me ^ d) * width, 128)
        outs[d][...] = array[:, pl.ds(at, width)]


def pack_keys_kernel(groups_count, member, *refs):
    key, value_end, key_end, query_end, strength, decay = refs[:6]
    outs, edges = refs[6 : 6 + groups_count], refs[6 + groups_count :]
    me = member[0]
    width = key.shape[1] // groups_count
    for d in range(groups_count):
        at = pl.multiple_of((me ^ d) * width, 128)
        outs[d][:, :width] = key[:, pl.ds(at, width)]
        outs[d][:, width:] = jnp.zeros((key.shape[0], 128), bf16)
        outs[d][:, width : width + HV] = strength[...]
        outs[d][:, width + HV : width + 2 * HV] = decay[...]
    for h in range(groups_count):
        start = 0
        for array in (value_end, key_end, query_end):
            width = array.shape[1] // groups_count
            edges[h][:, start : start + width] = array[:, h * width : (h + 1) * width]
            start += width


def shape(dims, kind):
    return jax.ShapeDtypeStruct(dims, kind)


def pack(member, array, groups):
    tokens, width = array.shape[0], array.shape[1] // groups
    return pl.pallas_call(
        functools.partial(pack_kernel, groups),
        grid_spec=grid_of(
            1,
            [pl.BlockSpec(array.shape, lambda p, me: (0, 0))],
            [pl.BlockSpec((tokens, width), lambda p, me: (0, 0))] * groups,
            [],
        ),
        out_shape=[shape((tokens, width), bf16)] * groups,
        compiler_params=params(),
        name="pack",
    )(member, array)


def pack_keys(member, key, value, query, strength, decay, groups):
    tokens, width = key.shape[0], key.shape[1] // groups
    edge = (EDGE, sum(x.shape[1] for x in (value, key, query)) // groups)

    def whole(dims):
        return pl.BlockSpec(dims, lambda p, me: (0, 0))

    def end(x):
        return pl.BlockSpec((EDGE, x.shape[1]), lambda p, me: (tokens // EDGE - 1, 0))

    outs = pl.pallas_call(
        functools.partial(pack_keys_kernel, groups),
        grid_spec=grid_of(
            1,
            [whole(key.shape), end(value), end(key), end(query)]
            + [whole(strength.shape), whole(decay.shape)],
            [whole((tokens, width + 128))] * groups + [whole(edge)] * groups,
            [],
        ),
        out_shape=[shape((tokens, width + 128), bf16)] * groups + [shape(edge, bf16)] * groups,
        compiler_params=params(),
        name="pack_keys",
    )(member, key, value, key, query, strength, decay)
    return outs[:groups], outs[groups:]


def per_head(each, dims):
    return pl.BlockSpec((each,) + dims, lambda p, me: (p,) + (0,) * len(dims))


def columns_of(rows, width, skip=0):
    return pl.BlockSpec((rows, width), lambda p, me: (0, p + skip))


def heads_at_once(key_heads):
    return 2 if key_heads % 2 == 0 else 1


def cost(microseconds):
    return pl.CostEstimate(
        flops=int(microseconds * 1e9), bytes_accessed=int(microseconds * 3e6), transcendentals=0
    )


def grid_of(steps, in_specs, out_specs, scratch):
    return pltpu.PrefetchScalarGridSpec(
        num_scalar_prefetch=1,
        grid=(steps,),
        in_specs=in_specs,
        out_specs=out_specs,
        scratch_shapes=scratch,
    )


def key_terms(member, packed, edges, taps):
    groups = len(packed)
    own = packed[0].shape[0]
    tokens = groups * own
    key_heads = taps.shape[1] // DK
    each = heads_at_once(key_heads)
    blocks = tokens // CH
    wide = (blocks, SHARE, CH, 2 * CH)
    kinds = [
        wide,
        (blocks, DK, 2 * CH),
        wide,
        wide,
        wide,
        (blocks - 1, SHARE, DK, 2 * DK),
        (blocks, SHARE, 8, CH),
    ]
    types = [bf16] * 6 + [f32]
    return pl.pallas_call(
        functools.partial(key_kernel, groups, key_heads * SHARE),
        grid_spec=grid_of(
            key_heads // each,
            [columns_of(own, each * DK)] * groups
            + [columns_of(EDGE, each * DK, key_heads * SHARE // each)] * groups
            + [pl.BlockSpec((own, 128), lambda p, me: (0, key_heads))] * groups
            + [columns_of(taps.shape[0], each * DK)],
            [per_head(each, kind) for kind in kinds]
            + [pl.BlockSpec((each * SHARE, DK, DK), lambda p, me: (p, 0, 0))],
            [pltpu.VMEM((tokens + 8, each * DK), f32), pltpu.VMEM((tokens, 128), bf16)],
        ),
        out_shape=[shape((key_heads,) + kind, t) for kind, t in zip(kinds, types)]
        + [shape((key_heads * SHARE, DK, DK), bf16)],
        compiler_params=params(),
        cost_estimate=cost(12),
        name="key_terms",
    )(member, *packed, *edges, *packed, taps)


def value_terms(member, pieces, edges, taps, t_in, ktail, d_in, last):
    groups = len(pieces)
    own = pieces[0].shape[0]
    tokens = groups * own
    key_heads = t_in.shape[0]
    each = heads_at_once(key_heads)
    blocks = tokens // CH
    width = each * SHARE * DV
    return pl.pallas_call(
        functools.partial(value_kernel, groups),
        grid_spec=grid_of(
            key_heads // each,
            [columns_of(own, width)] * groups
            + [columns_of(EDGE, width)] * groups
            + [columns_of(taps.shape[0], width)]
            + [per_head(each, x.shape[1:]) for x in (t_in, ktail, d_in, last)],
            [
                per_head(each, (blocks, SHARE, CH, 2 * DV)),
                per_head(each, (blocks - 1, SHARE, DK, 2 * DV)),
                pl.BlockSpec((each * SHARE, DK, DV), lambda p, me: (p, 0, 0)),
            ],
            [pltpu.VMEM((tokens + 8, width), f32)],
        ),
        out_shape=[
            shape((key_heads, blocks, SHARE, CH, 2 * DV), bf16),
            shape((key_heads, blocks - 1, SHARE, DK, 2 * DV), bf16),
            shape((key_heads * SHARE, DK, DV), bf16),
        ],
        compiler_params=params(),
        cost_estimate=cost(7),
        name="value_terms",
    )(member, *pieces, *edges, taps, t_in, ktail, d_in, last)


def query_terms(member, pieces, edges, packed, taps, kt, w, p, u, z):
    groups = len(pieces)
    own = pieces[0].shape[0]
    tokens = groups * own
    key_heads = kt.shape[0]
    each = heads_at_once(key_heads)
    skip = (key_heads + key_heads * SHARE) // each
    return pl.pallas_call(
        functools.partial(query_kernel, groups, key_heads * SHARE),
        grid_spec=grid_of(
            key_heads // each,
            [columns_of(own, each * DK)] * groups
            + [columns_of(EDGE, each * DK, skip)] * groups
            + [pl.BlockSpec((own, 128), lambda p, me: (0, key_heads))] * groups
            + [columns_of(taps.shape[0], each * DK)]
            + [per_head(each, x.shape[1:]) for x in (kt, w, p, u, z)],
            [
                pl.BlockSpec((each * SHARE, tokens, 2 * DK), lambda p, me: (p, 0, 0)),
                pl.BlockSpec((each * SHARE, tokens, DV), lambda p, me: (p, 0, 0)),
            ],
            [pltpu.VMEM((tokens + 8, each * DK), f32), pltpu.VMEM((tokens, 128), bf16)],
        ),
        out_shape=[
            shape((key_heads * SHARE, tokens, 2 * DK), bf16),
            shape((key_heads * SHARE, tokens, DV), f32),
        ],
        compiler_params=params(),
        cost_estimate=cost(8),
        name="query_terms",
    )(member, *pieces, *edges, *packed, taps, kt, w, p, u, z)


def handoff(maps, adds):
    return pl.pallas_call(
        handoff_kernel,
        out_shape=shape(adds.shape, bf16),
        compiler_params=params(),
        cost_estimate=cost(3),
        name="handoff",
    )(maps, adds)


def normed_rows(member, f, g, state, gate, gain, parity):
    heads = g.shape[0]
    count = len(gate)
    size, width = gate[0].shape

    def token_block(i, depth):
        return pl.BlockSpec(
            (heads, size, depth), lambda p, me: (0, me[0] ^ (2 * i + parity), 0)
        )

    whole = pl.BlockSpec((size, width), lambda p, me: (0, 0))
    return pl.pallas_call(
        functools.partial(norm_kernel, count),
        grid_spec=grid_of(
            1,
            [token_block(i, 2 * DK) for i in range(count)]
            + [token_block(i, DV) for i in range(count)]
            + [whole] * count
            + [
                pl.BlockSpec((heads, DK, DV), lambda p, me: (0, 0, 0)),
                pl.BlockSpec((1, DV), lambda p, me: (0, 0)),
            ],
            pl.BlockSpec((count, size, width), lambda p, me: (0, 0, 0)),
            [],
        ),
        out_shape=shape((count, size, width), bf16),
        compiler_params=params(),
        cost_estimate=cost(3),
        name="normed_rows",
    )(member, *([f] * count), *([g] * count), *gate, state, gain)


def projected(mine, theirs, own_weight, other_weight, start, width):
    ranks, size, depth = mine.shape
    tile = min(width, 512)
    whole = pl.BlockSpec((ranks, size, depth), lambda j: (0, 0, 0))
    weight = pl.BlockSpec((depth, tile), lambda j: (0, j + start // tile))
    out = pl.BlockSpec((size, tile), lambda j: (0, j))
    return pl.pallas_call(
        project_kernel,
        grid=(width // tile,),
        in_specs=[whole, whole, weight, weight],
        out_specs=[out] * ranks,
        out_shape=[shape((size, width), f32)] + [shape((size, width), bf16)] * (ranks - 1),
        compiler_params=params(),
        cost_estimate=cost(3),
        name="projected",
    )(mine, theirs, own_weight, other_weight)


def to_members(pieces):
    groups = len(pieces)
    return [pieces[0]] + [
        lax.ppermute(pieces[d], "head", [(i, i ^ d) for i in range(groups)])
        for d in range(1, groups)
    ]


def after_all(values, others):
    return lax.optimization_barrier((*values, *others))[: len(values)]


def to_runners(maps):
    spans = lax.axis_size("seq")
    heads = maps.shape[0]
    each = max(1, heads // spans)
    maps = maps.reshape(heads // each, each, DK, DK)
    if spans > heads:
        maps = jnp.repeat(maps, spans // heads, axis=0)
    return lax.all_to_all(maps, "seq", 0, 0)


def columns_to_runners(adds):
    spans = lax.axis_size("seq")
    heads = adds.shape[0]
    each = max(1, heads // spans)
    cuts = max(1, spans // heads)
    adds = adds.reshape(heads // each, each, DK, cuts, DV // cuts)
    adds = adds.transpose(0, 3, 1, 2, 4).reshape(spans, each, DK, DV // cuts)
    return lax.all_to_all(adds, "seq", 0, 0)


def from_runners(entries, heads):
    spans, each, depth, width = entries.shape
    entries = lax.all_to_all(entries, "seq", 0, 0)
    entries = entries.reshape(heads // each, DV // width, each, depth, width)
    return entries.transpose(0, 2, 3, 1, 4).reshape(heads, depth, DV)


def on_device(
    query_input,
    key_input,
    value_input,
    gate_input,
    write_strength,
    log_decay,
    filter_query,
    filter_key,
    filter_value,
    norm_gain,
    out_weight,
):
    groups = lax.axis_size("head")
    spans = lax.axis_size("seq")
    member = lax.axis_index("head").astype(jnp.int32).reshape(1)
    heads = filter_value.shape[1] // DV

    key_out, edges = pack_keys(
        member, key_input, value_input, query_input, write_strength, log_decay, groups
    )
    edges = [
        lax.ppermute(
            edges[h],
            ("seq", "head"),
            [(s * groups + groups - 1, (s + 1) * groups + h) for s in range(spans - 1)],
        )
        for h in range(groups)
    ]
    packed = to_members(key_out)
    value_rows = to_members(after_all(pack(member, value_input, groups), packed))
    query_rows = to_members(after_all(pack(member, query_input, groups), value_rows))
    gate_rows = to_members(after_all(pack(member, gate_input, groups), query_rows))

    t, kt, ktail, w, d, p, last, maps = key_terms(member, packed, edges, filter_key)
    maps = to_runners(maps)
    u, z, adds = value_terms(member, value_rows, edges, filter_value, t, ktail, d, last)
    adds, maps = after_all([adds, maps], [])
    adds = columns_to_runners(adds)
    f, g = query_terms(member, query_rows, edges, packed, filter_query, kt, w, p, u, z)
    adds, f, g = after_all([adds, f, g], [])
    state = from_runners(handoff(maps, adds), heads)

    gain = norm_gain.reshape(1, DV)
    swap = [(i, i ^ 1) for i in range(groups)]
    other_weight = lax.ppermute(out_weight, "head", swap)
    theirs = normed_rows(member, f, g, state, gate_rows[1::2], gain, 1)
    theirs = lax.ppermute(theirs, "head", swap)
    mine = normed_rows(member, f, g, state, gate_rows[0::2], gain, 0)
    width = out_weight.shape[1]
    cuts = 2
    totals = []
    for cut in range(cuts):
        kept, *sent = projected(
            mine, theirs, out_weight, other_weight, cut * width // cuts, width // cuts
        )
        totals.append(
            [kept]
            + [
                lax.ppermute(part, "head", [(i, i ^ (2 * step + 2)) for i in range(groups)])
                for step, part in enumerate(sent)
            ]
        )
    return jnp.concatenate(
        [sum(x.astype(f32) for x in parts).astype(bf16) for parts in totals], axis=1
    )


def solution(mesh):
    tokens = P(("seq", "head"), None)
    placed = (tokens,) * 6 + (P(None, "head"),) * 3 + (P(), P("head", None))
    return jax.shard_map(
        on_device, mesh=mesh, in_specs=placed, out_specs=tokens, check_vma=False
    )
```

time: 718 us -> 120 us (0.17); the launches traced: 708 us -> 120 us
  other arithmetic: 348 us -> 1.99 us
  waiting for transfers between devices: 140 us -> 21.1 us
  matrix products: 116 us -> 0 us
  Pallas kernels: 0 us -> 54 us
  starting transfers between devices: 60.1 us -> 34.4 us
  local copies, waits for them, and re-layouts: 28.7 us -> 7.75 us
  between operations: 14.4 us -> 0.31 us
    another operation x5 -> x0, other arithmetic: 318 us -> none  [the longest x4 317 us: stretch_terms(): jax.scipy.linalg.solve_triangular(system, right_side, lower=True, unit_di...]
    dot_general x46 -> x0, matrix products: 112 us -> none  [the longest x31 54.6 us: apply_maps(): return jnp.einsum('hde,hef->hdf', maps, states, precision=exact_mode)]
    pallas_call x0 -> x12, Pallas kernels: none -> 54 us  [the longest x1 12.9 us: key_terms(): pl.pallas_call(functools.partial(key_kernel, groups, key_heads * SHARE),...]
    reduce_scatter x1 -> x0, waiting for transfers between devices: 49 us -> none  [on_device(): lax.psum_scatter(jnp.dot(normed, out_weight, preferred_element_type=jnp.f...]
    ppermute x8 -> x20, waiting for transfers between devices: 58.8 us -> 20.5 us  [the longest x12 13.1 us: to_members(): lax.ppermute(pieces[d], 'head', [(i, i ^ d) for i in range(groups)])]
    all_to_all x6 -> x3, waiting for transfers between devices: 32.1 us -> 0.61 us  [the longest x1 0.61 us: columns_to_runners(): return lax.all_to_all(adds, 'seq', 0, 0)]
    ppermute x8 -> x20, starting transfers between devices: 37.8 us -> 18.2 us  [the longest x12 12.2 us: to_members(): lax.ppermute(pieces[d], 'head', [(i, i ^ d) for i in range(groups)])]
    mul x7 -> x0, other arithmetic: 13.1 us -> none  [the longest x1 5.68 us: causal_local(): return jax.nn.silu(summed)]
  transfers between devices with their start and end apart: 15 -> 23, of which waited for: 14 -> 7; matrix products, arithmetic and copies ran while one was open for 3% -> 0% of each run, Pallas kernels for 0% -> 40%
where the time goes in v2:
time: 120 us
  Pallas kernels  54 us (45%)
  starting transfers between devices  34.4 us (29%)
  waiting for transfers between devices  21.1 us (18%)
  local copies, waits for them, and re-layouts  7.75 us (6%)
  other arithmetic  1.99 us (2%)
    ppermute x12, waiting for transfers between devices, to_members(): lax.ppermute(pieces[d], 'head', [(i, i ^ d) for i in range(groups)])  13.1 us
    pallas_call x1, Pallas kernels, key_terms(): pl.pallas_call(functools.partial(key_kernel, groups, key_heads * SHARE),...  12.9 us
    ppermute x12, starting transfers between devices, to_members(): lax.ppermute(pieces[d], 'head', [(i, i ^ d) for i in range(groups)])  12.2 us
    pallas_call x2, Pallas kernels, projected(): pl.pallas_call(project_kernel, grid=(width // tile,), in_specs=[whole, wh...  8.09 us
    pallas_call x1, Pallas kernels, query_terms(): pl.pallas_call(functools.partial(query_kernel, groups, key_heads * SHARE)...  8.05 us
    unnamed x50, local copies, waits for them, and re-layouts  7.75 us
    ppermute x2, waiting for transfers between devices, on_device(): lax.ppermute(part, 'head', [(i, i ^ 2 * step + 2) for i in range(groups)])  7.37 us
    pallas_call x1, Pallas kernels, value_terms(): pl.pallas_call(functools.partial(value_kernel, groups), grid_spec=grid_of...  6.95 us
  transfers between devices with their start and end apart: 23, of which 7 were waited for; matrix products, arithmetic and copies ran while one was open for 0% of the time, Pallas kernels for 40%

profile of v2, /device:TPU:0, one launch (start us, length us, event | category | flops | bytes accessed | tf_op | source)
XLA Modules:
  0.0 119.5 jit_solution(11067641369638977140)
XLA Ops:
  0.0 1.4 %copy.15.refs_4_ = bf16[128,32]{1,0:T(8,128)(2,1)} copy(bf16[128,32]{0,1:T(8,128)(2,1)} %param.15) | data formatting | bytes 16384 | tf_op args[4]
  1.4 1.4 %copy.16.refs_5_ = bf16[128,32]{1,0:T(8,128)(2,1)} copy(bf16[128,32]{0,1:T(8,128)(2,1)} %param.16) | data formatting | bytes 16384 | tf_op args[5]
  2.8 2.1 %pack_keys.1 = (bf16[128,640]{1,0:T(8,128)(2,1)}, bf16[128,640]{1,0:T(8,128)(2,1)}, bf16[128,640]{1,0:T(8,128)(2,1)}, bf16[128,640]{1,0:T(8,128)(2,1)}, bf16[16,...) custom-call(s32[1]{0:T(128)} %bitcast.member, ...), custom_call_target="tpu_custom_call" | custom-call | tf_op jit(solution)/shard_map/pack_keys/pallas_call | solution.py:428
  5.0 0.5 collective-permute-start
  5.4 2.6 %collective-permute-start.1 = (bf16[128,640]{1,0:T(8,128)(2,1)}, bf16[128,640]{1,0:T(8,128)(2,1)S(1)}, u32[]{:S(2)}, u32[]{:S(2)}) collective-permute-start(bf16[128,640]{1,0:T(8,128)(2,1)} %get-tuple-element.65), channel_id=1, source_target_pairs={{0,2},{1,3},{2,0},{3,1},{4,6},{5,7},{6,4},{7,5},{8,10},{9,11},{10,... | collective-permute-start | bytes 491528 | tf_op jit(solution)/shard_map/ppermute | solution.py:639
  8.0 0.1 collective-permute-start.2
  8.1 0.1 collective-permute-start.17
  8.2 0.7 collective-permute-start.6
  8.9 0.7 collective-permute-start.7
  9.5 3.7 %collective-permute-done.1.refs_2_.refs_10_ = bf16[128,640]{1,0:T(8,128)(2,1)S(1)} collective-permute-done((bf16[128,640]{1,0:T(8,128)(2,1)}, bf16[128,640]{1,0:T(8,128)(2,1)S(1)}, u32[]{:S(2)}, u32[]{:S(2)}) %collective-permute-start.1) | collective-permute-done | bytes 163872 | tf_op jit(solution)/shard_map/ppermute | solution.py:639
  13.3 0.7 collective-permute-start.8
  13.9 2.3 %collective-permute-done.2.refs_3_.refs_11_ = bf16[128,640]{1,0:T(8,128)(2,1)S(1)} collective-permute-done((bf16[128,640]{1,0:T(8,128)(2,1)}, bf16[128,640]{1,0:T(8,128)(2,1)S(1)}, u32[]{:S(2)}, u32[]{:S(2)}) %collective-permute-start.2) | collective-permute-done | bytes 163872 | tf_op jit(solution)/shard_map/ppermute | solution.py:639
  16.2 0.7 collective-permute-start.9
  16.9 2.3 %pack.3 = (bf16[128,1024]{1,0:T(8,128)(2,1)}, bf16[128,1024]{1,0:T(8,128)(2,1)}, bf16[128,1024]{1,0:T(8,128)(2,1)}, bf16[128,1024]{1,0:T(8,128)(2,1)}) custom-call(s32[1]{0:T(128)} %bitcast.member, bf16[128,4096]{1,0:T(8,128)(2,1)} %refs_1_.1), custom_call_target="tpu_custom_call" | custom-call | tf_op jit(solution)/shard_map/pack/pallas_call | solution.py:404
  19.2 1.9 %pack.4 = (bf16[128,512]{1,0:T(8,128)(2,1)}, bf16[128,512]{1,0:T(8,128)(2,1)}, bf16[128,512]{1,0:T(8,128)(2,1)}, bf16[128,512]{1,0:T(8,128)(2,1)}) custom-call(s32[1]{0:T(128)} %bitcast.member, bf16[128,2048]{1,0:T(8,128)(2,1)} %refs_0_.6), custom_call_target="tpu_custom_call" | custom-call | tf_op jit(solution)/shard_map/pack/pallas_call | solution.py:404
  21.1 0.0 collective-permute-done.6.refs_4_
  21.1 0.4 collective-permute-start.3
  21.5 0.0 collective-permute-done.7.refs_5_
  21.5 4.7 %collective-permute-start.4 = (bf16[128,1024]{1,0:T(8,128)(2,1)}, bf16[128,1024]{1,0:T(8,128)(2,1)S(1)}, u32[]{:S(2)}, u32[]{:S(2)}) collective-permute-start(bf16[128,1024]{1,0:T(8,128)(2,1)} %get-tuple-element.69), channel_id=1, source_target_pairs={{0,2},{1,3},{2,0},{3,1},{4,6},{5,7},{6,4},{7,5},{8,10},{9,11},{10,... | collective-permute-start | bytes 786440 | tf_op jit(solution)/shard_map/ppermute | solution.py:639
  26.2 0.0 collective-permute-done.8.refs_6_
  26.2 0.0 collective-permute-start.5
  26.2 0.6 copy-done.22
  26.8 0.6 copy-done.23
  27.4 12.9 %key_terms.1 = (bf16[4,4,2,128,256]{4,3,2,1,0:T(8,128)(2,1)}, bf16[4,4,128,256]{3,2,1,0:T(8,128)(2,1)}, bf16[4,4,2,128,256]{4,3,2,1,0:T(8,128)(2,1)}, bf16[4,4,2...) custom-call(s32[1]{0:T(128)} %bitcast.member, ...), custom_call_target="tpu_custom_call" | custom-call | flops 12000000000 | bytes 36000000 | tf_op jit(solution)/shard_map/key_terms/pallas_call | solution.py:490
  40.3 4.8 %all-to-all-start = ((bf16[8,1,128,128]{3,2,1,0:T(8,128)(2,1)}), bf16[8,1,128,128]{3,2,1,0:T(8,128)(2,1)S(1)}, u32[]{:S(2)}, u32[]{:S(2)}) async-start(bf16[8,1,128,128]{3,2,1,0:T(8,128)(2,1)} %bitcast.8), calls=%async_computation | async-start | bytes 524288 | tf_op jit(solution)/shard_map/all_to_all | solution.py:655
  45.2 0.0 collective-permute-done.4.refs_2_
  45.2 0.0 collective-permute-done.5.refs_3_
  45.2 0.1 collective-permute-start.10
  45.3 1.3 %collective-permute-start.11 = (bf16[128,512]{1,0:T(8,128)(2,1)S(1)}, bf16[128,512]{1,0:T(8,128)(2,1)S(1)}, u32[]{:S(2)}, u32[]{:S(2)}) collective-permute-start(bf16[128,512]{1,0:T(8,128)(2,1)S(1)} %copy-done.15), channel_id=1, source_target_pairs={{0,2},{1,3},{2,0},{3,1},{4,6},{5,7},{6,4},{7,5},{8,10},{9,11},{10,... | collective-permute-start | bytes 393224 | tf_op jit(solution)/shard_map/ppermute | solution.py:639
  46.6 0.6 collective-permute-start.12
  47.2 7.0 %value_terms.1 = (bf16[4,4,2,128,256]{4,3,2,1,0:T(8,128)(2,1)}, bf16[4,3,2,128,256]{4,3,2,1,0:T(8,128)(2,1)}, bf16[8,128,128]{2,1,0:T(8,128)(2,1)}) custom-call(s32[1]{0:T(128)} %bitcast.member, bf16[128,1024]{1,0:T(8,128)(2,1)} %get-tuple-element.67.refs_0_, bf16[128,1024]{1,0:T(8,128)(2,1)} %copy-done.5, bf16[128,1024]{1,0:T(8,128)(2,1)} %copy-done.6, ...), custom_call_target="tpu_custom_call" | custom-call | flops 7000000000 | bytes 21000000 | tf_op jit(solution)/shard_map/value_terms/pallas_call | solution.py:518
  54.1 0.0 all-to-all-done.maps
  54.1 0.0 copy-start.1
  54.1 6.0 %all-to-all-start.1 = ((bf16[8,1,128,128]{3,2,1,0:T(8,128)(2,1)}), bf16[8,1,128,128]{3,2,1,0:T(8,128)(2,1)S(1)}, u32[]{:S(2)}, u32[]{:S(2)}) async-start(bf16[8,1,128,128]{3,2,1,0:T(8,128)(2,1)} %bitcast.5), calls=%async_computation.1 | async-start | bytes 524288 | tf_op jit(solution)/shard_map/all_to_all | solution.py:665
  60.2 0.0 collective-permute-done.11.refs_2_
  60.2 0.6 copy-done.17
  60.8 0.1 copy-done.18
  60.9 0.0 copy-done.19
  60.9 8.1 %query_terms.1 = (bf16[8,512,256]{2,1,0:T(8,128)(2,1)}, f32[8,512,128]{2,1,0:T(8,128)}) custom-call(s32[1]{0:T(128)} %bitcast.member, bf16[128,512]{1,0:T(8,128)(2,1)} %get-tuple-element.86.refs_0_, bf16[128,512]{1,0:T(8,128)(2,1)} %copy-done.17, bf16[128,512]{1,0:T(8,128)(2,1)} %copy-done.18, bf16[128,512]{1,0:T(8,128)(2,1)} %copy-done.19, ...), custom_call_target="tpu_custom_call" | custom-call | flops 8000000000 | bytes 24000000 | tf_op jit(solution)/shard_map/query_terms/pallas_call | solution.py:551
  69.0 0.6 all-to-all-done.1.adds
  69.6 0.7 copy-done.3
  70.3 2.8 %handoff.1 = bf16[8,1,128,128]{3,2,1,0:T(8,128)(2,1)} custom-call(bf16[8,1,128,128]{3,2,1,0:T(8,128)(2,1)} %copy-done.1, bf16[8,1,128,128]{3,2,1,0:T(8,128)(2,1)} %copy-done.3), custom_call_target="tpu_custom_call" | custom-call | flops 3000000000 | bytes 9000000 | tf_op jit(solution)/shard_map/handoff/pallas_call | solution.py:577
  73.1 5.4 %all-to-all-start.2 = ((bf16[8,1,128,128]{3,2,1,0:T(8,128)(2,1)}), bf16[8,1,128,128]{3,2,1,0:T(8,128)(2,1)S(1)}, u32[]{:S(2)}, u32[]{:S(2)}) async-start(bf16[8,1,128,128]{3,2,1,0:T(8,128)(2,1)} %handoff.1), calls=%async_computation.2 | async-start | bytes 524288 | tf_op jit(solution)/shard_map/all_to_all | solution.py:670
  78.5 2.3 %pack.5 = (bf16[128,1024]{1,0:T(8,128)(2,1)}, bf16[128,1024]{1,0:T(8,128)(2,1)}, bf16[128,1024]{1,0:T(8,128)(2,1)}, bf16[128,1024]{1,0:T(8,128)(2,1)}) custom-call(s32[1]{0:T(128)} %bitcast.member, bf16[128,4096]{1,0:T(8,128)(2,1)} %refs_0_.7), custom_call_target="tpu_custom_call" | custom-call | tf_op jit(solution)/shard_map/pack/pallas_call | solution.py:404
  80.8 1.0 collective-permute-start.15
  81.7 1.2 collective-permute-start.13
  82.9 6.0 %collective-permute-done.15.refs_5_ = bf16[128,1024]{1,0:T(8,128)(2,1)S(1)} collective-permute-done((bf16[128,1024]{1,0:T(8,128)(2,1)}, bf16[128,1024]{1,0:T(8,128)(2,1)S(1)}, u32[]{:S(2)}, u32[]{:S(2)}) %collective-permute-start.15) | collective-permute-done | bytes 262176 | tf_op jit(solution)/shard_map/ppermute | solution.py:639
  88.9 0.7 copy-done.10
  89.6 0.1 copy-done.2
  89.7 3.3 %normed_rows.3 = bf16[2,128,1024]{2,1,0:T(8,128)(2,1)} custom-call(s32[1]{0:T(128)} %bitcast.member, bf16[8,512,256]{2,1,0:T(8,128)(2,1)} %get-tuple-element.97.refs_0_.refs_1_, bf16[8,512,256]{2,1,0:T(8,128)(2,1)} %get-tuple-element.97.refs_0_.refs_1_, f32[8,512,128]{2,1,0:T(8,128)} %get-tuple-element.98.refs_2_.refs_3_, ...), custom_call_target="tpu_custom_call" | custom-call | flops 3000000000 | bytes 9000000 | tf_op jit(solution)/shard_map/normed_rows/pallas_call | solution.py:597
  93.1 1.1 collective-permute-start.16
  94.2 1.0 collective-permute-done.13.refs_5_
  95.2 0.7 copy-done.8
  95.9 3.3 %normed_rows.2.mine = bf16[2,128,1024]{2,1,0:T(8,128)(2,1)} custom-call(s32[1]{0:T(128)} %bitcast.member, bf16[8,512,256]{2,1,0:T(8,128)(2,1)} %get-tuple-element.97.refs_0_.refs_1_, bf16[8,512,256]{2,1,0:T(8,128)(2,1)} %get-tuple-element.97.refs_0_.refs_1_, f32[8,512,128]{2,1,0:T(8,128)} %get-tuple-element.98.refs_2_.refs_3_, ...), custom_call_target="tpu_custom_call" | custom-call | flops 3000000000 | bytes 9000000 | tf_op jit(solution)/shard_map/normed_rows/pallas_call | solution.py:597
  99.2 0.8 copy-done.4
  100.0 4.0 %projected.2 = (f32[128,1024]{1,0:T(8,128)}, bf16[128,1024]{1,0:T(8,128)(2,1)}) custom-call(bf16[2,128,1024]{2,1,0:T(8,128)(2,1)} %normed_rows.2.mine, bf16[2,128,1024]{2,1,0:T(8,128)(2,1)} %copy-done.4, bf16[1024,2048]{1,0:T(8,128)(2,1)} %own_weight.3, bf16[1024,2048]{1,0:T(8,128)(2,1)} %collective-permute-done.17.other_weight), custom_call_target="tpu_custom_call" | custom-call | flops 3000000000 | bytes 9000000 | tf_op jit(solution)/shard_map/projected/pallas_call | solution.py:624
  104.1 0.9 collective-permute-start.18
  104.9 4.0 %projected.3 = (f32[128,1024]{1,0:T(8,128)}, bf16[128,1024]{1,0:T(8,128)(2,1)}) custom-call(bf16[2,128,1024]{2,1,0:T(8,128)(2,1)} %normed_rows.2.mine, bf16[2,128,1024]{2,1,0:T(8,128)(2,1)} %copy-done.4, bf16[1024,2048]{1,0:T(8,128)(2,1)} %own_weight.3, bf16[1024,2048]{1,0:T(8,128)(2,1)} %collective-permute-done.17.other_weight), custom_call_target="tpu_custom_call" | custom-call | flops 3000000000 | bytes 9000000 | tf_op jit(solution)/shard_map/projected/pallas_call | solution.py:624
  109.0 1.2 collective-permute-start.19
  110.2 2.8 %collective-permute-done.18 = bf16[128,1024]{1,0:T(8,128)(2,1)S(1)} collective-permute-done((bf16[128,1024]{1,0:T(8,128)(2,1)}, bf16[128,1024]{1,0:T(8,128)(2,1)S(1)}, u32[]{:S(2)}, u32[]{:S(2)}) %collective-permute-start.18) | collective-permute-done | bytes 262176 | tf_op jit(solution)/shard_map/ppermute | solution.py:734
  112.9 0.1 add_convert_fusion.1
  113.0 4.6 %collective-permute-done.19 = bf16[128,1024]{1,0:T(8,128)(2,1)S(1)} collective-permute-done((bf16[128,1024]{1,0:T(8,128)(2,1)}, bf16[128,1024]{1,0:T(8,128)(2,1)S(1)}, u32[]{:S(2)}, u32[]{:S(2)}) %collective-permute-start.19) | collective-permute-done | bytes 262176 | tf_op jit(solution)/shard_map/ppermute | solution.py:734
  117.6 1.1 add_convert_fusion
  118.7 0.8 pad_maximum_fusion
  (47 shorter events, 0.1 us)
Async XLA Ops:
  5.0 3.9 %collective-permute-start = (bf16[128,640]{1,0:T(8,128)(2,1)}, bf16[128,640]{1,0:T(8,128)(2,1)S(1)}, u32[]{:S(2)}, u32[]{:S(2)}) collective-permute-start(bf16[128,640]{1,0:T(8,128)(2,1)} %get-tuple-element.64), channel_id=1, source_target_pairs={{0,1},{1,0},{2,3},{3,2},{4,5},{5,4},{6,7},{7,6},{8,9},{9,8},{10,11... | collective-permute-start | bytes 491528 | tf_op jit(solution)/shard_map/ppermute | solution.py:639
  5.4 7.8 %collective-permute-start.1 = (bf16[128,640]{1,0:T(8,128)(2,1)}, bf16[128,640]{1,0:T(8,128)(2,1)S(1)}, u32[]{:S(2)}, u32[]{:S(2)}) collective-permute-start(bf16[128,640]{1,0:T(8,128)(2,1)} %get-tuple-element.65), channel_id=1, source_target_pairs={{0,2},{1,3},{2,0},{3,1},{4,6},{5,7},{6,4},{7,5},{8,10},{9,11},{10,... | collective-permute-start | bytes 491528 | tf_op jit(solution)/shard_map/ppermute | solution.py:639
  8.0 8.3 %collective-permute-start.2 = (bf16[128,640]{1,0:T(8,128)(2,1)}, bf16[128,640]{1,0:T(8,128)(2,1)S(1)}, u32[]{:S(2)}, u32[]{:S(2)}) collective-permute-start(bf16[128,640]{1,0:T(8,128)(2,1)} %get-tuple-element.66), channel_id=1, source_target_pairs={{0,3},{1,2},{2,1},{3,0},{4,7},{5,6},{6,5},{7,4},{8,11},{9,10},{10,... | collective-permute-start | bytes 491528 | tf_op jit(solution)/shard_map/ppermute | solution.py:639
  8.1 91.1 %collective-permute-start.17 = (bf16[1024,2048]{1,0:T(8,128)(2,1)}, bf16[1024,2048]{1,0:T(8,128)(2,1)}, u32[]{:S(2)}, u32[]{:S(2)}) collective-permute-start(bf16[1024,2048]{1,0:T(8,128)(2,1)} %own_weight.3), channel_id=1, source_target_pairs={{0,1},{1,0},{2,3},{3,2},{4,5},{5,4},{6,7},{7,6},{8,9},{9,8},{10,11... | collective-permute-start | bytes 12582920 | tf_op jit(solution)/shard_map/ppermute | solution.py:720
  8.2 12.9 %collective-permute-start.6 = (bf16[16,2048]{1,0:T(8,128)(2,1)}, bf16[16,2048]{1,0:T(8,128)(2,1)S(1)}, u32[]{:S(2)}, u32[]{:S(2)}) collective-permute-start(bf16[16,2048]{1,0:T(8,128)(2,1)} %get-tuple-element.71), channel_id=1, source_target_pairs={{3,4},{7,8},{11,12},{15,16},{19,20},{23,24},{27,28}} | collective-permute-start | bytes 196616 | tf_op jit(solution)/shard_map/ppermute | solution.py:697
  8.9 17.3 %copy-start.11 = (bf16[128,640]{1,0:T(8,128)(2,1)}, bf16[128,640]{1,0:T(8,128)(2,1)S(1)}, u32[]{:S(2)}) copy-start(bf16[128,640]{1,0:T(8,128)(2,1)S(1)} %collective-permute-done.refs_1_.refs_9_) | copy-start | bytes 491524
  8.9 12.6 %collective-permute-start.7 = (bf16[16,2048]{1,0:T(8,128)(2,1)}, bf16[16,2048]{1,0:T(8,128)(2,1)S(1)}, u32[]{:S(2)}, u32[]{:S(2)}) collective-permute-start(bf16[16,2048]{1,0:T(8,128)(2,1)} %get-tuple-element.72), channel_id=1, source_target_pairs={{3,5},{7,9},{11,13},{15,17},{19,21},{23,25},{27,29}} | collective-permute-start | bytes 196616 | tf_op jit(solution)/shard_map/ppermute | solution.py:697
  13.2 13.0 %copy-start.12 = (bf16[128,640]{1,0:T(8,128)(2,1)}, bf16[128,640]{1,0:T(8,128)(2,1)S(1)}, u32[]{:S(2)}) copy-start(bf16[128,640]{1,0:T(8,128)(2,1)S(1)} %collective-permute-done.1.refs_2_.refs_10_) | copy-start | bytes 491524
  13.3 12.9 %collective-permute-start.8 = (bf16[16,2048]{1,0:T(8,128)(2,1)}, bf16[16,2048]{1,0:T(8,128)(2,1)S(1)}, u32[]{:S(2)}, u32[]{:S(2)}) collective-permute-start(bf16[16,2048]{1,0:T(8,128)(2,1)} %get-tuple-element.73), channel_id=1, source_target_pairs={{3,6},{7,10},{11,14},{15,18},{19,22},{23,26},{27,30}} | collective-permute-start | bytes 196616 | tf_op jit(solution)/shard_map/ppermute | solution.py:697
  16.2 10.0 %copy-start.13 = (bf16[128,640]{1,0:T(8,128)(2,1)}, bf16[128,640]{1,0:T(8,128)(2,1)S(1)}, u32[]{:S(2)}) copy-start(bf16[128,640]{1,0:T(8,128)(2,1)S(1)} %collective-permute-done.2.refs_3_.refs_11_) | copy-start | bytes 491524
  16.2 9.9 %collective-permute-start.9 = (bf16[16,2048]{1,0:T(8,128)(2,1)}, bf16[16,2048]{1,0:T(8,128)(2,1)S(1)}, u32[]{:S(2)}, u32[]{:S(2)}) collective-permute-start(bf16[16,2048]{1,0:T(8,128)(2,1)} %get-tuple-element.74), channel_id=1, source_target_pairs={{3,7},{7,11},{11,15},{15,19},{19,23},{23,27},{27,31}} | collective-permute-start | bytes 196616 | tf_op jit(solution)/shard_map/ppermute | solution.py:697
  21.1 24.1 %copy-start.16 = (bf16[128,512]{1,0:T(8,128)(2,1)S(1)}, bf16[128,512]{1,0:T(8,128)(2,1)}, u32[]{:S(2)}) copy-start(bf16[128,512]{1,0:T(8,128)(2,1)} %get-tuple-element.87) | copy-start | bytes 393220
  21.1 24.2 %copy-start.15 = (bf16[128,512]{1,0:T(8,128)(2,1)S(1)}, bf16[128,512]{1,0:T(8,128)(2,1)}, u32[]{:S(2)}) copy-start(bf16[128,512]{1,0:T(8,128)(2,1)} %get-tuple-element.88) | copy-start | bytes 393220
  21.1 25.5 %copy-start.14 = (bf16[128,512]{1,0:T(8,128)(2,1)S(1)}, bf16[128,512]{1,0:T(8,128)(2,1)}, u32[]{:S(2)}) copy-start(bf16[128,512]{1,0:T(8,128)(2,1)} %get-tuple-element.89) | copy-start | bytes 393220
  21.1 5.1 %copy-start.20 = (bf16[16,2048]{1,0:T(8,128)(2,1)}, bf16[16,2048]{1,0:T(8,128)(2,1)S(1)}, u32[]{:S(2)}) copy-start(bf16[16,2048]{1,0:T(8,128)(2,1)S(1)} %collective-permute-done.6.refs_4_) | copy-start | bytes 196612
  21.1 24.1 %collective-permute-start.3 = (bf16[128,1024]{1,0:T(8,128)(2,1)}, bf16[128,1024]{1,0:T(8,128)(2,1)S(1)}, u32[]{:S(2)}, u32[]{:S(2)}) collective-permute-start(bf16[128,1024]{1,0:T(8,128)(2,1)} %get-tuple-element.68), channel_id=1, source_target_pairs={{0,1},{1,0},{2,3},{3,2},{4,5},{5,4},{6,7},{7,6},{8,9},{9,8},{10,11... | collective-permute-start | bytes 786440 | tf_op jit(solution)/shard_map/ppermute | solution.py:639
  21.5 4.7 %copy-start.21 = (bf16[16,2048]{1,0:T(8,128)(2,1)}, bf16[16,2048]{1,0:T(8,128)(2,1)S(1)}, u32[]{:S(2)}) copy-start(bf16[16,2048]{1,0:T(8,128)(2,1)S(1)} %collective-permute-done.7.refs_5_) | copy-start | bytes 196612
  21.5 23.7 %collective-permute-start.4 = (bf16[128,1024]{1,0:T(8,128)(2,1)}, bf16[128,1024]{1,0:T(8,128)(2,1)S(1)}, u32[]{:S(2)}, u32[]{:S(2)}) collective-permute-start(bf16[128,1024]{1,0:T(8,128)(2,1)} %get-tuple-element.69), channel_id=1, source_target_pairs={{0,2},{1,3},{2,0},{3,1},{4,6},{5,7},{6,4},{7,5},{8,10},{9,11},{10,... | collective-permute-start | bytes 786440 | tf_op jit(solution)/shard_map/ppermute | solution.py:639
  26.2 0.6 copy-start.22
  26.2 19.0 %collective-permute-start.5 = (bf16[128,1024]{1,0:T(8,128)(2,1)}, bf16[128,1024]{1,0:T(8,128)(2,1)S(1)}, u32[]{:S(2)}, u32[]{:S(2)}) collective-permute-start(bf16[128,1024]{1,0:T(8,128)(2,1)} %get-tuple-element.70), channel_id=1, source_target_pairs={{0,3},{1,2},{2,1},{3,0},{4,7},{5,6},{6,5},{7,4},{8,11},{9,10},{10,... | collective-permute-start | bytes 786440 | tf_op jit(solution)/shard_map/ppermute | solution.py:639
  26.8 0.6 copy-start.23
  40.3 13.8 %all-to-all-start = ((bf16[8,1,128,128]{3,2,1,0:T(8,128)(2,1)}), bf16[8,1,128,128]{3,2,1,0:T(8,128)(2,1)S(1)}, u32[]{:S(2)}, u32[]{:S(2)}) async-start(bf16[8,1,128,128]{3,2,1,0:T(8,128)(2,1)} %bitcast.8), calls=%async_computation | async-start | bytes 524288 | tf_op jit(solution)/shard_map/all_to_all | solution.py:655
  45.1 2.0 %copy-start.5 = (bf16[128,1024]{1,0:T(8,128)(2,1)}, bf16[128,1024]{1,0:T(8,128)(2,1)S(1)}, u32[]{:S(2)}) copy-start(bf16[128,1024]{1,0:T(8,128)(2,1)S(1)} %collective-permute-done.3.refs_1_) | copy-start | bytes 786436
  45.2 2.0 %copy-start.6 = (bf16[128,1024]{1,0:T(8,128)(2,1)}, bf16[128,1024]{1,0:T(8,128)(2,1)S(1)}, u32[]{:S(2)}) copy-start(bf16[128,1024]{1,0:T(8,128)(2,1)S(1)} %collective-permute-done.4.refs_2_) | copy-start | bytes 786436
  45.2 2.0 %copy-start.7 = (bf16[128,1024]{1,0:T(8,128)(2,1)}, bf16[128,1024]{1,0:T(8,128)(2,1)S(1)}, u32[]{:S(2)}) copy-start(bf16[128,1024]{1,0:T(8,128)(2,1)S(1)} %collective-permute-done.5.refs_3_) | copy-start | bytes 786436
  45.2 14.9 %collective-permute-start.10 = (bf16[128,512]{1,0:T(8,128)(2,1)S(1)}, bf16[128,512]{1,0:T(8,128)(2,1)S(1)}, u32[]{:S(2)}, u32[]{:S(2)}) collective-permute-start(bf16[128,512]{1,0:T(8,128)(2,1)S(1)} %copy-done.16), channel_id=1, source_target_pairs={{0,1},{1,0},{2,3},{3,2},{4,5},{5,4},{6,7},{7,6},{8,9},{9,8},{10,11... | collective-permute-start | bytes 393224 | tf_op jit(solution)/shard_map/ppermute | solution.py:639
  45.3 14.9 %collective-permute-start.11 = (bf16[128,512]{1,0:T(8,128)(2,1)S(1)}, bf16[128,512]{1,0:T(8,128)(2,1)S(1)}, u32[]{:S(2)}, u32[]{:S(2)}) collective-permute-start(bf16[128,512]{1,0:T(8,128)(2,1)S(1)} %copy-done.15), channel_id=1, source_target_pairs={{0,2},{1,3},{2,0},{3,1},{4,6},{5,7},{6,4},{7,5},{8,10},{9,11},{10,... | collective-permute-start | bytes 393224 | tf_op jit(solution)/shard_map/ppermute | solution.py:639
  46.6 13.6 %collective-permute-start.12 = (bf16[128,512]{1,0:T(8,128)(2,1)S(1)}, bf16[128,512]{1,0:T(8,128)(2,1)S(1)}, u32[]{:S(2)}, u32[]{:S(2)}) collective-permute-start(bf16[128,512]{1,0:T(8,128)(2,1)S(1)} %copy-done.14), channel_id=1, source_target_pairs={{0,3},{1,2},{2,1},{3,0},{4,7},{5,6},{6,5},{7,4},{8,11},{9,10},{10,... | collective-permute-start | bytes 393224 | tf_op jit(solution)/shard_map/ppermute | solution.py:639
  54.1 14.8 %copy-start.1 = (bf16[8,1,128,128]{3,2,1,0:T(8,128)(2,1)}, bf16[8,1,128,128]{3,2,1,0:T(8,128)(2,1)S(1)}, u32[]{:S(2)}) copy-start(bf16[8,1,128,128]{3,2,1,0:T(8,128)(2,1)S(1)} %all-to-all-done.maps) | copy-start | bytes 786436
  54.1 15.4 %all-to-all-start.1 = ((bf16[8,1,128,128]{3,2,1,0:T(8,128)(2,1)}), bf16[8,1,128,128]{3,2,1,0:T(8,128)(2,1)S(1)}, u32[]{:S(2)}, u32[]{:S(2)}) async-start(bf16[8,1,128,128]{3,2,1,0:T(8,128)(2,1)} %bitcast.5), calls=%async_computation.1 | async-start | bytes 524288 | tf_op jit(solution)/shard_map/all_to_all | solution.py:665
  60.2 0.7 copy-start.17
  60.2 0.7 copy-start.18
  60.2 0.7 copy-start.19
  69.6 0.7 copy-start.3
  73.1 15.8 %all-to-all-start.2 = ((bf16[8,1,128,128]{3,2,1,0:T(8,128)(2,1)}), bf16[8,1,128,128]{3,2,1,0:T(8,128)(2,1)S(1)}, u32[]{:S(2)}, u32[]{:S(2)}) async-start(bf16[8,1,128,128]{3,2,1,0:T(8,128)(2,1)} %handoff.1), calls=%async_computation.2 | async-start | bytes 524288 | tf_op jit(solution)/shard_map/all_to_all | solution.py:670
  80.8 2.1 %collective-permute-start.14 = (bf16[128,1024]{1,0:T(8,128)(2,1)}, bf16[128,1024]{1,0:T(8,128)(2,1)S(1)}, u32[]{:S(2)}, u32[]{:S(2)}) collective-permute-start(bf16[128,1024]{1,0:T(8,128)(2,1)} %get-tuple-element.107), channel_id=1, source_target_pairs={{0,1},{1,0},{2,3},{3,2},{4,5},{5,4},{6,7},{7,6},{8,9},{9,8},{10,11... | collective-permute-start | bytes 786440 | tf_op jit(solution)/shard_map/ppermute | solution.py:639
  80.8 8.2 %collective-permute-start.15 = (bf16[128,1024]{1,0:T(8,128)(2,1)}, bf16[128,1024]{1,0:T(8,128)(2,1)S(1)}, u32[]{:S(2)}, u32[]{:S(2)}) collective-permute-start(bf16[128,1024]{1,0:T(8,128)(2,1)} %get-tuple-element.108), channel_id=1, source_target_pairs={{0,3},{1,2},{2,1},{3,0},{4,7},{5,6},{6,5},{7,4},{8,11},{9,10},{10,... | collective-permute-start | bytes 786440 | tf_op jit(solution)/shard_map/ppermute | solution.py:639
  81.7 13.5 %collective-permute-start.13 = (bf16[128,1024]{1,0:T(8,128)(2,1)}, bf16[128,1024]{1,0:T(8,128)(2,1)S(1)}, u32[]{:S(2)}, u32[]{:S(2)}) collective-permute-start(bf16[128,1024]{1,0:T(8,128)(2,1)} %get-tuple-element.104), channel_id=1, source_target_pairs={{0,2},{1,3},{2,0},{3,1},{4,6},{5,7},{6,4},{7,5},{8,10},{9,11},{10,... | collective-permute-start | bytes 786440 | tf_op jit(solution)/shard_map/ppermute | solution.py:639
  82.9 6.0 %copy-start.9 = (bf16[128,1024]{1,0:T(8,128)(2,1)}, bf16[128,1024]{1,0:T(8,128)(2,1)S(1)}, u32[]{:S(2)}) copy-start(bf16[128,1024]{1,0:T(8,128)(2,1)S(1)} %collective-permute-done.14.refs_4_) | copy-start | bytes 786436
  88.9 0.7 copy-start.10
  88.9 0.8 copy-start.2
  93.1 6.1 %collective-permute-start.16 = (bf16[2,128,1024]{2,1,0:T(8,128)(2,1)}, bf16[2,128,1024]{2,1,0:T(8,128)(2,1)S(1)}, u32[]{:S(2)}, u32[]{:S(2)}) collective-permute-start(bf16[2,128,1024]{2,1,0:T(8,128)(2,1)} %normed_rows.3), channel_id=1, source_target_pairs={{0,1},{1,0},{2,3},{3,2},{4,5},{5,4},{6,7},{7,6},{8,9},{9,8},{10,11... | collective-permute-start | bytes 1572872 | tf_op jit(solution)/shard_map/ppermute | solution.py:722
  95.2 0.7 copy-start.8
  99.2 0.8 copy-start.4
  104.1 8.9 %copy-start = (f32[128,1024]{1,0:T(8,128)S(1)}, f32[128,1024]{1,0:T(8,128)}, u32[]{:S(2)}) copy-start(f32[128,1024]{1,0:T(8,128)} %get-tuple-element.109) | copy-start | bytes 1572868
  104.1 8.9 %collective-permute-start.18 = (bf16[128,1024]{1,0:T(8,128)(2,1)}, bf16[128,1024]{1,0:T(8,128)(2,1)S(1)}, u32[]{:S(2)}, u32[]{:S(2)}) collective-permute-start(bf16[128,1024]{1,0:T(8,128)(2,1)} %get-tuple-element.110), channel_id=1, source_target_pairs={{0,2},{1,3},{2,0},{3,1},{4,6},{5,7},{6,4},{7,5},{8,10},{9,11},{10,... | collective-permute-start | bytes 786440 | tf_op jit(solution)/shard_map/ppermute | solution.py:734
  109.0 8.6 %collective-permute-start.19 = (bf16[128,1024]{1,0:T(8,128)(2,1)}, bf16[128,1024]{1,0:T(8,128)(2,1)S(1)}, u32[]{:S(2)}, u32[]{:S(2)}) collective-permute-start(bf16[128,1024]{1,0:T(8,128)(2,1)} %get-tuple-element.112), channel_id=1, source_target_pairs={{0,2},{1,3},{2,0},{3,1},{4,6},{5,7},{6,4},{7,5},{8,10},{9,11},{10,... | collective-permute-start | bytes 786440 | tf_op jit(solution)/shard_map/ppermute | solution.py:734

commit v3 on v2

--- a/solution.py
+++ b/solution.py
@@ -14,6 +14,7 @@
 CH = 128
 EDGE = 16
 SHARE = HV // HK
+ODD_ROWS = 16
 
 norm_floor = 1e-06
 f32 = jnp.float32
@@ -65,13 +66,19 @@
         out[pl.ds(at, size), :] = piece[...].astype(out.dtype)
 
 
-def conv_silu(me, pieces, edges, taps_ref, padded):
+def place_gates(me, pieces, out, heads, size):
+    for d, piece in enumerate(pieces):
+        ends = piece[...].astype(f32)[12:16]
+        sets = [ends[:, i * size : (i + 1) * size] for i in range(heads // 2)]
+        rows = jnp.concatenate(sets + [jnp.zeros((128 - 2 * heads, size), f32)], axis=0)
+        at = pl.multiple_of((me ^ d) * size, 16)
+        out[pl.ds(at, size), :] = jnp.transpose(rows).astype(bf16)
+
+
+def conv_silu(me, pieces, edge, taps_ref, padded):
     length = padded.shape[0] - 8
     taps = taps_ref[...].astype(f32)
-    edge = edges[0][...].astype(f32)
-    for other in edges[1:]:
-        edge = edge + other[...].astype(f32)
-    padded[0:8] = edge[EDGE - 8 : EDGE]
+    padded[8 - edge.shape[0] : 8] = edge
     place(me, pieces, padded, 8)
     margin = taps.shape[0] - 1
     summed = taps[margin : margin + 1] * padded[8 : 8 + length]
@@ -85,10 +92,10 @@
     return field * lax.rsqrt(jnp.sum(field * field, axis=-1, keepdims=True) + norm_floor)
 
 
-def strengths_and_rates(gates, first, count):
+def strengths_and_rates(gates, first, count, heads):
     lane = lax.broadcasted_iota(jnp.int32, (gates.shape[1], CH), 0)
     picks = [ones_where(lane == first + e) for e in range(count)]
-    picks += [ones_where(lane == HV + first + e) for e in range(count)]
+    picks += [ones_where(lane == heads + first + e) for e in range(count)]
     picked = jnp.dot(gates, jnp.concatenate(picks, axis=1), preferred_element_type=f32)
     return picked[:, : count * CH], picked[:, count * CH :].astype(bf16)
 
@@ -124,12 +131,38 @@
             & ((column // size) % 2 == 0)
         )
         rounded = {n: inverse[n].astype(bf16) for n in names}
-        first = {
-            n: jnp.dot(halves[n][0] * mask, rounded[n], preferred_element_type=f32).astype(bf16)
-            for n in names
-        }
-        for n in names:
-            inverse[n] = inverse[n] - jnp.dot(rounded[n], first[n], preferred_element_type=f32)
+        if size < ODD_ROWS:
+            first = {
+                n: jnp.dot(halves[n][0] * mask, rounded[n], preferred_element_type=f32).astype(bf16)
+                for n in names
+            }
+            for n in names:
+                inverse[n] = inverse[n] - jnp.dot(rounded[n], first[n], preferred_element_type=f32)
+        else:
+            starts = range(size, CH, 2 * size)
+
+            def odd(x):
+                return jnp.concatenate([x[s : s + size] for s in starts], axis=0)
+
+            def back(x, even):
+                rows = []
+                for i, s in enumerate(starts):
+                    rows += [even[s - size : s], x[i * size : (i + 1) * size]]
+                return jnp.concatenate(rows, axis=0)
+
+            some = odd(mask)
+            nothing = jnp.zeros((CH, CH), bf16)
+            first = {
+                n: jnp.dot(
+                    odd(halves[n][0]) * some, rounded[n], preferred_element_type=f32
+                ).astype(bf16)
+                for n in names
+            }
+            for n in names:
+                change = jnp.dot(
+                    odd(rounded[n]), back(first[n], nothing), preferred_element_type=f32
+                )
+                inverse[n] = back(odd(inverse[n]) - change, inverse[n])
         size *= 2
     parts = {n: split(inverse[n]) for n in names}
     left = {
@@ -147,16 +180,15 @@
 
 def key_kernel(groups_count, heads, member, *refs):
     pieces, refs = refs[:groups_count], refs[groups_count:]
-    edges, refs = refs[:groups_count], refs[groups_count:]
     gate_pieces, refs = refs[:groups_count], refs[groups_count:]
-    taps, t_out, kt_out, ktail_out, w_out, d_out, p_out, last_out, map_out, padded, gates = refs
+    edge, taps, t_out, kt_out, ktail_out, w_out, d_out, p_out, last_out, map_out, padded, gates = refs
     here = pieces[0].shape[1] // DK
     count = here * SHARE
     blocks = gates.shape[0] // CH
     me = member[0]
-    first = me * heads + pl.program_id(0) * count
-    filtered = conv_silu(me, pieces, edges, taps, padded)
-    place(me, gate_pieces, gates, 0)
+    first = pl.program_id(0) * count
+    filtered = conv_silu(me, pieces, edge[...].astype(f32)[EDGE - 8 :], taps, padded)
+    place_gates(me, gate_pieces, gates, heads, pieces[0].shape[0])
     row, column = grids()
     eye = jnp.where(row == column, 1.0, 0.0)
     groups = [(c, k) for c in range(blocks) for k in range(here)]
@@ -165,7 +197,7 @@
     def chunk_of(x, c):
         return x[c * CH : (c + 1) * CH]
 
-    strengths, rates = strengths_and_rates(gates[...], first, count)
+    strengths, rates = strengths_and_rates(gates[...], first, count, heads)
     unit = [unit_rows(filtered[:, k * DK : (k + 1) * DK]) for k in range(here)]
     decays = [decay_terms(chunk_of(rates, c), count) for c in range(blocks)]
     keys = {(c, k): chunk_of(unit[k], c) for c, k in groups}
@@ -232,11 +264,15 @@
 
 def value_kernel(groups_count, member, *refs):
     pieces, refs = refs[:groups_count], refs[groups_count:]
-    edges, refs = refs[:groups_count], refs[groups_count:]
-    taps, t_in, ktail, d_in, last, u_out, z_out, add_out, padded = refs
+    edge, taps, t_in, ktail, d_in, last, maps, u_out, z_out, span_out, padded, before = refs
     blocks = t_in.shape[1]
-    count = pieces[0].shape[1] // DV
-    values = conv_silu(member[0], pieces, edges, taps, padded)
+    width = pieces[0].shape[1]
+    count = width // DV
+    ends = edge[...].astype(f32)
+    for r in range(SHARE):
+        before[:, r * edge.shape[1] : (r + 1) * edge.shape[1]] = ends[4 * r : 4 * r + 4]
+    at = pl.multiple_of(pl.program_id(0) * width, 128)
+    values = conv_silu(member[0], pieces, before[:, pl.ds(at, width)], taps, padded)
     problems = [(c, e) for c in range(blocks) for e in range(count)]
 
     def at(ref, c, e):
@@ -266,24 +302,24 @@
             for e in range(count)
         ]
     for e in range(count):
-        add_out[e] = running[e].astype(bf16)
+        span_out[e, :, :DK] = maps[e]
+        span_out[e, :, DK:] = running[e].astype(bf16)
 
 
 def query_kernel(groups_count, heads, member, *refs):
     pieces, refs = refs[:groups_count], refs[groups_count:]
-    edges, refs = refs[:groups_count], refs[groups_count:]
     gate_pieces, refs = refs[:groups_count], refs[groups_count:]
-    taps, kt_in, w_in, p_in, u_in, z_in, f_out, g_out, padded, gates = refs
+    edge, taps, kt_in, w_in, p_in, u_in, z_in, f_out, g_out, padded, gates = refs
     here = pieces[0].shape[1] // DK
     count = here * SHARE
     blocks = gates.shape[0] // CH
     me = member[0]
-    first = me * heads + pl.program_id(0) * count
-    filtered = conv_silu(me, pieces, edges, taps, padded)
-    place(me, gate_pieces, gates, 0)
+    first = pl.program_id(0) * count
+    filtered = conv_silu(me, pieces, edge[...].astype(f32)[8:12], taps, padded)
+    place_gates(me, gate_pieces, gates, heads, pieces[0].shape[0])
     unit = [unit_rows(filtered[:, k * DK : (k + 1) * DK]) * DK ** (-0.5) for k in range(here)]
     problems = [(c, e) for c in range(blocks) for e in range(count)]
-    strengths, rates = strengths_and_rates(gates[...], first, count)
+    strengths, rates = strengths_and_rates(gates[...], first, count, heads)
     decays = [decay_terms(rates[c * CH : (c + 1) * CH], count) for c in range(blocks)]
 
     def at(ref, c, e):
@@ -306,31 +342,29 @@
     for c, e in problems:
         here = slice(c * CH, (c + 1) * CH)
         if c == 0:
-            f_out[e, here] = entry[c, e]
-            g_out[e, here] = local[c, e]
+            f_out[e, here] = entry[c, e][:, :DK]
+            g_out[e, here] = local[c, e].astype(bf16)
         else:
-            f_out[e, here] = as_left(product(entry[c, e], at(p_in, c - 1, e)))
-            g_out[e, here] = local[c, e] + product(entry[c, e], at(z_in, c - 1, e))
-
-
-def handoff_kernel(maps, adds, out):
-    spans, heads = maps.shape[0], maps.shape[1]
-    width = out.shape[3]
+            f_out[e, here] = product(entry[c, e], at(p_in, c - 1, e)).astype(bf16)
+            total = local[c, e] + product(entry[c, e], at(z_in, c - 1, e))
+            g_out[e, here] = total.astype(bf16)
+
+
+def handoff_kernel(spans_in, out):
+    spans, heads, width = out.shape[0], out.shape[1], out.shape[3]
     running = [jnp.zeros(out.shape[2:], f32) for h in range(heads)]
     for j in range(spans):
         for h in range(heads):
             out[j, h] = running[h].astype(bf16)
         if j + 1 < spans:
             for h in range(heads):
-                high, low = split(running[h])
-                both = jnp.concatenate([high, low], axis=1) if width % 128 == 0 else None
-                if both is None:
-                    erased = jnp.dot(maps[j, h], high, preferred_element_type=f32)
-                    erased = erased + jnp.dot(maps[j, h], low, preferred_element_type=f32)
-                else:
-                    erased = jnp.dot(maps[j, h], both, preferred_element_type=f32)
-                    erased = erased[:, :width] + erased[:, width:]
-                running[h] = running[h] - erased + adds[j, h].astype(f32)
+                erased = jnp.dot(
+                    spans_in[j, h, :, :DK],
+                    jnp.concatenate(split(running[h]), axis=1),
+                    preferred_element_type=f32,
+                )
+                erased = erased[:, :width] + erased[:, width:]
+                running[h] = running[h] - erased + spans_in[j, h, :, DK:].astype(f32)
 
 
 def norm_kernel(count, member, *refs):
@@ -338,11 +372,10 @@
     g_in, refs = refs[:count], refs[count:]
     gate, refs = refs[:count], refs[count:]
     state, gain, out = refs
-    heads = state.shape[0]
-    cells = [(i, h) for i in range(count) for h in range(heads)]
-    states = [jnp.concatenate([state[h], state[h]], axis=0) for h in range(heads)]
+    cells = [(i, h) for i in range(count) for h in range(state.shape[0])]
     core = {
-        (i, h): g_in[i][h] + jnp.dot(f_in[i][h], states[h], preferred_element_type=f32)
+        (i, h): g_in[i][h].astype(f32)
+        + jnp.dot(f_in[i][h], state[h], preferred_element_type=f32)
         for i, h in cells
     }
     scale = {
@@ -377,22 +410,30 @@
 
 
 def pack_keys_kernel(groups_count, member, *refs):
-    key, value_end, key_end, query_end, strength, decay = refs[:6]
-    outs, edges = refs[6 : 6 + groups_count], refs[6 + groups_count :]
+    key, value_end, query_end, strength, decay = refs[:5]
+    outs = refs[5:]
     me = member[0]
-    width = key.shape[1] // groups_count
+    tokens, width = key.shape[0], key.shape[1] // groups_count
+    heads = HV // groups_count
+    gates = jnp.concatenate([strength[...], decay[...]], axis=0)
+    row = lax.broadcasted_iota(jnp.int32, (2 * heads, 2 * HV), 0)
+    column = lax.broadcasted_iota(jnp.int32, (2 * heads, 2 * HV), 1)
     for d in range(groups_count):
-        at = pl.multiple_of((me ^ d) * width, 128)
-        outs[d][:, :width] = key[:, pl.ds(at, width)]
-        outs[d][:, width:] = jnp.zeros((key.shape[0], 128), bf16)
-        outs[d][:, width : width + HV] = strength[...]
-        outs[d][:, width + HV : width + 2 * HV] = decay[...]
-    for h in range(groups_count):
-        start = 0
-        for array in (value_end, key_end, query_end):
-            width = array.shape[1] // groups_count
-            edges[h][:, start : start + width] = array[:, h * width : (h + 1) * width]
-            start += width
+        at = me ^ d
+        outs[d][:tokens] = key[:, pl.ds(pl.multiple_of(at * width, 128), width)]
+        ends = []
+        for r in range(SHARE):
+            start = pl.multiple_of((at * SHARE + r) * width, 128)
+            ends.append(value_end[:, pl.ds(start, width)].astype(f32)[EDGE - 4 :])
+        start = pl.multiple_of(at * width, 128)
+        ends.append(query_end[:, pl.ds(start, width)].astype(f32)[EDGE - 4 :])
+        wanted = jnp.where(row < heads, row, row - heads + HV) + at * heads
+        picked = jnp.dot(ones_where(column == wanted), gates, preferred_element_type=f32)
+        sets = [picked[4 * i : 4 * i + 4] for i in range(heads // 2)]
+        if width > tokens * len(sets):
+            sets.append(jnp.zeros((4, width - tokens * len(sets)), f32))
+        ends.append(jnp.concatenate(sets, axis=1))
+        outs[d][tokens:] = jnp.concatenate(ends, axis=0).astype(bf16)
 
 
 def shape(dims, kind):
@@ -411,13 +452,13 @@
         ),
         out_shape=[shape((tokens, width), bf16)] * groups,
         compiler_params=params(),
+        cost_estimate=cost(3),
         name="pack",
     )(member, array)
 
 
 def pack_keys(member, key, value, query, strength, decay, groups):
     tokens, width = key.shape[0], key.shape[1] // groups
-    edge = (EDGE, sum(x.shape[1] for x in (value, key, query)) // groups)
 
     def whole(dims):
         return pl.BlockSpec(dims, lambda p, me: (0, 0))
@@ -425,28 +466,28 @@
     def end(x):
         return pl.BlockSpec((EDGE, x.shape[1]), lambda p, me: (tokens // EDGE - 1, 0))
 
-    outs = pl.pallas_call(
+    packed = (tokens + EDGE, width)
+    return pl.pallas_call(
         functools.partial(pack_keys_kernel, groups),
         grid_spec=grid_of(
             1,
-            [whole(key.shape), end(value), end(key), end(query)]
-            + [whole(strength.shape), whole(decay.shape)],
-            [whole((tokens, width + 128))] * groups + [whole(edge)] * groups,
+            [whole(key.shape), end(value), end(query), whole(strength.shape), whole(decay.shape)],
+            [whole(packed)] * groups,
             [],
         ),
-        out_shape=[shape((tokens, width + 128), bf16)] * groups + [shape(edge, bf16)] * groups,
+        out_shape=[shape(packed, bf16)] * groups,
         compiler_params=params(),
+        cost_estimate=cost(3),
         name="pack_keys",
-    )(member, key, value, key, query, strength, decay)
-    return outs[:groups], outs[groups:]
+    )(member, key, value, query, strength, decay)
 
 
 def per_head(each, dims):
     return pl.BlockSpec((each,) + dims, lambda p, me: (p,) + (0,) * len(dims))
 
 
-def columns_of(rows, width, skip=0):
-    return pl.BlockSpec((rows, width), lambda p, me: (0, p + skip))
+def columns_of(rows, width):
+    return pl.BlockSpec((rows, width), lambda p, me: (0, p))
 
 
 def heads_at_once(key_heads):
@@ -469,9 +510,9 @@
     )
 
 
-def key_terms(member, packed, edges, taps):
+def key_terms(member, packed, edge, taps):
     groups = len(packed)
-    own = packed[0].shape[0]
+    own = packed[0].shape[0] - EDGE
     tokens = groups * own
     key_heads = taps.shape[1] // DK
     each = heads_at_once(key_heads)
@@ -492,8 +533,8 @@
         grid_spec=grid_of(
             key_heads // each,
             [columns_of(own, each * DK)] * groups
-            + [columns_of(EDGE, each * DK, key_heads * SHARE // each)] * groups
-            + [pl.BlockSpec((own, 128), lambda p, me: (0, key_heads))] * groups
+            + [pl.BlockSpec((EDGE, key_heads * DK), lambda p, me: (own // EDGE, 0))] * groups
+            + [columns_of(EDGE, each * DK)]
             + [columns_of(taps.shape[0], each * DK)],
             [per_head(each, kind) for kind in kinds]
             + [pl.BlockSpec((each * SHARE, DK, DK), lambda p, me: (p, 0, 0))],
@@ -504,10 +545,10 @@
         compiler_params=params(),
         cost_estimate=cost(12),
         name="key_terms",
-    )(member, *packed, *edges, *packed, taps)
-
-
-def value_terms(member, pieces, edges, taps, t_in, ktail, d_in, last):
+    )(member, *packed, *packed, edge, taps)
+
+
+def value_terms(member, pieces, edge, taps, t_in, ktail, d_in, last, maps):
     groups = len(pieces)
     own = pieces[0].shape[0]
     tokens = groups * own
@@ -520,77 +561,76 @@
         grid_spec=grid_of(
             key_heads // each,
             [columns_of(own, width)] * groups
-            + [columns_of(EDGE, width)] * groups
+            + [pl.BlockSpec((EDGE, key_heads * DK), lambda p, me: (1, 0))]
             + [columns_of(taps.shape[0], width)]
-            + [per_head(each, x.shape[1:]) for x in (t_in, ktail, d_in, last)],
+            + [per_head(each, x.shape[1:]) for x in (t_in, ktail, d_in, last)]
+            + [pl.BlockSpec((each * SHARE, DK, DK), lambda p, me: (p, 0, 0))],
             [
                 per_head(each, (blocks, SHARE, CH, 2 * DV)),
                 per_head(each, (blocks - 1, SHARE, DK, 2 * DV)),
-                pl.BlockSpec((each * SHARE, DK, DV), lambda p, me: (p, 0, 0)),
+                pl.BlockSpec((each * SHARE, DK, DK + DV), lambda p, me: (p, 0, 0)),
             ],
-            [pltpu.VMEM((tokens + 8, width), f32)],
+            [
+                pltpu.VMEM((tokens + 8, width), f32),
+                pltpu.VMEM((4, key_heads * SHARE * DV), f32),
+            ],
         ),
         out_shape=[
             shape((key_heads, blocks, SHARE, CH, 2 * DV), bf16),
             shape((key_heads, blocks - 1, SHARE, DK, 2 * DV), bf16),
-            shape((key_heads * SHARE, DK, DV), bf16),
+            shape((key_heads * SHARE, DK, DK + DV), bf16),
         ],
         compiler_params=params(),
         cost_estimate=cost(7),
         name="value_terms",
-    )(member, *pieces, *edges, taps, t_in, ktail, d_in, last)
-
-
-def query_terms(member, pieces, edges, packed, taps, kt, w, p, u, z):
+    )(member, *pieces, edge, taps, t_in, ktail, d_in, last, maps)
+
+
+def query_terms(member, pieces, edge, packed, taps, kt, w, p, u, z):
     groups = len(pieces)
     own = pieces[0].shape[0]
     tokens = groups * own
     key_heads = kt.shape[0]
     each = heads_at_once(key_heads)
-    skip = (key_heads + key_heads * SHARE) // each
+    out = pl.BlockSpec((each * SHARE, tokens, DK), lambda p, me: (p, 0, 0))
     return pl.pallas_call(
         functools.partial(query_kernel, groups, key_heads * SHARE),
         grid_spec=grid_of(
             key_heads // each,
             [columns_of(own, each * DK)] * groups
-            + [columns_of(EDGE, each * DK, skip)] * groups
-            + [pl.BlockSpec((own, 128), lambda p, me: (0, key_heads))] * groups
+            + [pl.BlockSpec((EDGE, key_heads * DK), lambda p, me: (own // EDGE, 0))] * groups
+            + [pl.BlockSpec((EDGE, each * DK), lambda p, me: (1, p))]
             + [columns_of(taps.shape[0], each * DK)]
             + [per_head(each, x.shape[1:]) for x in (kt, w, p, u, z)],
-            [
-                pl.BlockSpec((each * SHARE, tokens, 2 * DK), lambda p, me: (p, 0, 0)),
-                pl.BlockSpec((each * SHARE, tokens, DV), lambda p, me: (p, 0, 0)),
-            ],
+            [out, out],
             [pltpu.VMEM((tokens + 8, each * DK), f32), pltpu.VMEM((tokens, 128), bf16)],
         ),
-        out_shape=[
-            shape((key_heads * SHARE, tokens, 2 * DK), bf16),
-            shape((key_heads * SHARE, tokens, DV), f32),
-        ],
+        out_shape=[shape((key_heads * SHARE, tokens, DK), bf16)] * 2,
         compiler_params=params(),
-        cost_estimate=cost(8),
+        cost_estimate=cost(9),
         name="query_terms",
-    )(member, *pieces, *edges, *packed, taps, kt, w, p, u, z)
-
-
-def handoff(maps, adds):
+    )(member, *pieces, *packed, edge, taps, kt, w, p, u, z)
+
+
+def handoff(spans):
+    dims = spans.shape[:3] + (spans.shape[3] - DK,)
     return pl.pallas_call(
         handoff_kernel,
-        out_shape=shape(adds.shape, bf16),
-        compiler_params=params(),
-        cost_estimate=cost(3),
+        out_shape=shape(dims, bf16),
+        compiler_params=params(16),
+        cost_estimate=cost(1),
         name="handoff",
-    )(maps, adds)
+    )(spans)
 
 
 def normed_rows(member, f, g, state, gate, gain, parity):
-    heads = g.shape[0]
+    heads = state.shape[0]
     count = len(gate)
     size, width = gate[0].shape
 
-    def token_block(i, depth):
+    def token_block(i):
         return pl.BlockSpec(
-            (heads, size, depth), lambda p, me: (0, me[0] ^ (2 * i + parity), 0)
+            (heads, size, DK), lambda p, me: (0, me[0] ^ (2 * i + parity), 0)
         )
 
     whole = pl.BlockSpec((size, width), lambda p, me: (0, 0))
@@ -598,8 +638,7 @@
         functools.partial(norm_kernel, count),
         grid_spec=grid_of(
             1,
-            [token_block(i, 2 * DK) for i in range(count)]
-            + [token_block(i, DV) for i in range(count)]
+            [token_block(i) for i in range(count)] * 2
             + [whole] * count
             + [
                 pl.BlockSpec((heads, DK, DV), lambda p, me: (0, 0, 0)),
@@ -609,8 +648,8 @@
             [],
         ),
         out_shape=shape((count, size, width), bf16),
-        compiler_params=params(),
-        cost_estimate=cost(3),
+        compiler_params=params(16),
+        cost_estimate=cost(1),
         name="normed_rows",
     )(member, *([f] * count), *([g] * count), *gate, state, gain)
 
@@ -627,10 +666,32 @@
         in_specs=[whole, whole, weight, weight],
         out_specs=[out] * ranks,
         out_shape=[shape((size, width), f32)] + [shape((size, width), bf16)] * (ranks - 1),
-        compiler_params=params(),
+        compiler_params=params(16),
         cost_estimate=cost(3),
         name="projected",
     )(mine, theirs, own_weight, other_weight)
+
+
+def sum_kernel(cuts, *refs):
+    parts, out = refs[:-1], refs[-1]
+    each = len(parts) // cuts
+    for cut in range(cuts):
+        total = parts[cut * each][...]
+        for part in parts[cut * each + 1 : (cut + 1) * each]:
+            total = total + part[...].astype(f32)
+        width = total.shape[1]
+        out[:, cut * width : (cut + 1) * width] = total.astype(bf16)
+
+
+def summed_parts(parts, cuts):
+    rows, width = parts[0].shape
+    return pl.pallas_call(
+        functools.partial(sum_kernel, cuts),
+        out_shape=shape((rows, width * cuts), bf16),
+        compiler_params=params(16),
+        cost_estimate=cost(1),
+        name="summed_parts",
+    )(*parts)
 
 
 def to_members(pieces):
@@ -645,24 +706,18 @@
     return lax.optimization_barrier((*values, *others))[: len(values)]
 
 
-def to_runners(maps):
+def to_runners(terms):
     spans = lax.axis_size("seq")
-    heads = maps.shape[0]
-    each = max(1, heads // spans)
-    maps = maps.reshape(heads // each, each, DK, DK)
-    if spans > heads:
-        maps = jnp.repeat(maps, spans // heads, axis=0)
-    return lax.all_to_all(maps, "seq", 0, 0)
-
-
-def columns_to_runners(adds):
-    spans = lax.axis_size("seq")
-    heads = adds.shape[0]
-    each = max(1, heads // spans)
-    cuts = max(1, spans // heads)
-    adds = adds.reshape(heads // each, each, DK, cuts, DV // cuts)
-    adds = adds.transpose(0, 3, 1, 2, 4).reshape(spans, each, DK, DV // cuts)
-    return lax.all_to_all(adds, "seq", 0, 0)
+    heads = terms.shape[0]
+    if spans <= heads:
+        pieces = terms.reshape(spans, heads // spans, DK, DK + DV)
+    else:
+        cuts = spans // heads
+        maps = jnp.repeat(terms[:, :, :DK], cuts, axis=0)
+        adds = terms[:, :, DK:].reshape(heads, DK, cuts, DV // cuts)
+        adds = adds.transpose(0, 2, 1, 3).reshape(spans, DK, DV // cuts)
+        pieces = jnp.concatenate([maps, adds], axis=2)[:, None]
+    return lax.all_to_all(pieces, "seq", 0, 0)
 
 
 def from_runners(entries, heads):
@@ -690,54 +745,51 @@
     member = lax.axis_index("head").astype(jnp.int32).reshape(1)
     heads = filter_value.shape[1] // DV
 
-    key_out, edges = pack_keys(
-        member, key_input, value_input, query_input, write_strength, log_decay, groups
+    key_out = pack_keys(
+        member, key_input, value_input, query_input, write_strength.T, log_decay.T, groups
     )
-    edges = [
-        lax.ppermute(
-            edges[h],
-            ("seq", "head"),
-            [(s * groups + groups - 1, (s + 1) * groups + h) for s in range(spans - 1)],
-        )
-        for h in range(groups)
-    ]
     packed = to_members(key_out)
-    value_rows = to_members(after_all(pack(member, value_input, groups), packed))
-    query_rows = to_members(after_all(pack(member, query_input, groups), value_rows))
-    gate_rows = to_members(after_all(pack(member, gate_input, groups), query_rows))
-
-    t, kt, ktail, w, d, p, last, maps = key_terms(member, packed, edges, filter_key)
-    maps = to_runners(maps)
-    u, z, adds = value_terms(member, value_rows, edges, filter_value, t, ktail, d, last)
-    adds, maps = after_all([adds, maps], [])
-    adds = columns_to_runners(adds)
-    f, g = query_terms(member, query_rows, edges, packed, filter_query, kt, w, p, u, z)
-    adds, f, g = after_all([adds, f, g], [])
-    state = from_runners(handoff(maps, adds), heads)
+    edge = packed[0][-2 * EDGE :]
+    for d in range(1, groups):
+        edge = jnp.where((member[0] ^ d) == groups - 1, packed[d][-2 * EDGE :], edge)
+    value_out = pack(member, value_input, groups)
+    query_out = pack(member, query_input, groups)
+    gate_out = pack(member, gate_input, groups)
+    edge, *value_out = after_all([edge, *value_out], [*query_out, *gate_out])
+    edge = lax.ppermute(edge, "seq", [(s, s + 1) for s in range(spans - 1)])
+    value_rows = to_members(value_out)
+    t, kt, ktail, w, d, p, last, maps = key_terms(member, packed, edge, filter_key)
+    u, z, terms = value_terms(
+        member, value_rows, edge, filter_value, t, ktail, d, last, maps
+    )
+    query_rows = to_members(after_all(query_out, [terms]))
+    gate_rows = to_members(after_all(gate_out, [terms]))
+    (own_weight,) = after_all([out_weight], [terms])
+    swap = [(i, i ^ 1) for i in range(groups)]
+    other_weight = lax.ppermute(own_weight, "head", swap)
+    terms = to_runners(terms)
+    entries = handoff(terms)
+    query_rows = after_all(query_rows, [entries, *gate_rows])
+    f, g = query_terms(member, query_rows, edge, packed, filter_query, kt, w, p, u, z)
+    state = from_runners(entries, heads)
 
     gain = norm_gain.reshape(1, DV)
-    swap = [(i, i ^ 1) for i in range(groups)]
-    other_weight = lax.ppermute(out_weight, "head", swap)
     theirs = normed_rows(member, f, g, state, gate_rows[1::2], gain, 1)
     theirs = lax.ppermute(theirs, "head", swap)
     mine = normed_rows(member, f, g, state, gate_rows[0::2], gain, 0)
     width = out_weight.shape[1]
     cuts = 2
-    totals = []
+    parts = []
     for cut in range(cuts):
         kept, *sent = projected(
             mine, theirs, out_weight, other_weight, cut * width // cuts, width // cuts
         )
-        totals.append(
-            [kept]
-            + [
-                lax.ppermute(part, "head", [(i, i ^ (2 * step + 2)) for i in range(groups)])
-                for step, part in enumerate(sent)
-            ]
-        )
-    return jnp.concatenate(
-        [sum(x.astype(f32) for x in parts).astype(bf16) for parts in totals], axis=1
-    )
+        parts.append(kept)
+        parts += [
+            lax.ppermute(part, "head", [(i, i ^ (2 * step + 2)) for i in range(groups)])
+            for step, part in enumerate(sent)
+        ]
+    return summed_parts(parts, cuts)
 
 
 def solution(mesh):

time: 120 us -> 101 us (0.84)
  starting transfers between devices: 34.4 us -> 25.1 us
  Pallas kernels: 54 us -> 47.3 us
  local copies, waits for them, and re-layouts: 7.75 us -> 4.8 us
    ppermute x12, waiting for transfers between devices: 13.1 us -> 3.54 us  [to_members(): lax.ppermute(pieces[d], 'head', [(i, i ^ d) for i in range(groups)])]
    all_to_all x2 -> x1, waiting for transfers between devices: 0.61 us -> 8.53 us  [to_runners(): return lax.all_to_all(pieces, 'seq', 0, 0)]
    pallas_call x2, Pallas kernels: 6.63 us -> 1.61 us  [normed_rows(): pl.pallas_call(functools.partial(norm_kernel, count), grid_spec=grid_of(1...]
    all_to_all x2 -> x1, starting transfers between devices: 10.8 us -> 5.92 us  [to_runners(): return lax.all_to_all(pieces, 'seq', 0, 0)]
    ppermute x12, starting transfers between devices: 12.2 us -> 8.66 us  [to_members(): lax.ppermute(pieces[d], 'head', [(i, i ^ d) for i in range(groups)])]
    unnamed x50 -> x48, local copies, waits for them, and re-layouts: 7.75 us -> 4.8 us
    pallas_call x2, Pallas kernels: 8.09 us -> 5.56 us  [projected(): pl.pallas_call(project_kernel, grid=(width // tile,), in_specs=[whole, wh...]
    ppermute x5 -> x2, starting transfers between devices: 2.76 us -> 4.65 us  [the longest x1 4.24 us: on_device(): edge = lax.ppermute(edge, 'seq', [(s, s + 1) for s in range(spans - 1)])]
  transfers between devices with their start and end apart: 23 -> 19, of which waited for: 7 -> 7; matrix products, arithmetic and copies ran while one was open for 0% -> 0% of each run, Pallas kernels for 40% -> 34%
where the time goes in v3:
time: 101 us; the launch traced here: 100 us
  Pallas kernels  47.3 us (47%)
  starting transfers between devices  25.1 us (25%)
  waiting for transfers between devices  22.2 us (22%)
  local copies, waits for them, and re-layouts  4.8 us (5%)
    pallas_call x1, Pallas kernels, key_terms(): pl.pallas_call(functools.partial(key_kernel, groups, key_heads * SHARE),...  13.1 us
    ppermute x2, waiting for transfers between devices, on_device(): lax.ppermute(part, 'head', [(i, i ^ 2 * step + 2) for i in range(groups)])  8.87 us
    ppermute x12, starting transfers between devices, to_members(): lax.ppermute(pieces[d], 'head', [(i, i ^ d) for i in range(groups)])  8.66 us
    all_to_all x1, waiting for transfers between devices, to_runners(): return lax.all_to_all(pieces, 'seq', 0, 0)  8.53 us
    pallas_call x1, Pallas kernels, query_terms(): pl.pallas_call(functools.partial(query_kernel, groups, key_heads * SHARE)...  8.25 us
    pallas_call x1, Pallas kernels, value_terms(): pl.pallas_call(functools.partial(value_kernel, groups), grid_spec=grid_of...  7.59 us
    pallas_call x3, Pallas kernels, pack(): pl.pallas_call(functools.partial(pack_kernel, groups), grid_spec=grid_of(...  6.47 us
    all_to_all x1, starting transfers between devices, to_runners(): return lax.all_to_all(pieces, 'seq', 0, 0)  5.92 us
  transfers between devices with their start and end apart: 19, of which 7 were waited for; matrix products, arithmetic and copies ran while one was open for 0% of the time, Pallas kernels for 34%

profile of v3, /device:TPU:0, one launch (start us, length us, event | category | flops | bytes accessed | tf_op | source)
XLA Modules:
  0.0 100.5 jit_solution(7238713977133869534)
XLA Ops:
  0.0 2.1 %pack_keys.1 = (bf16[144,512]{1,0:T(8,128)(2,1)}, bf16[144,512]{1,0:T(8,128)(2,1)}, bf16[144,512]{1,0:T(8,128)(2,1)}, bf16[144,512]{1,0:T(8,128)(2,1)}) custom-call(s32[1]{0:T(128)} %bitcast.member, bf16[128,2048]{1,0:T(8,128)(2,1)} %refs_0_.5, bf16[128,4096]{1,0:T(8,128)(2,1)} %refs_0_.6, bf16[128,2048]{1,0:T(8,128)(2,1)} %refs_2_.1, ...), custom_call_target="tpu_custom_call" | custom-call | flops 3000000000 | bytes 9000000 | tf_op jit(solution)/shard_map/pack_keys/pallas_call | solution.py:470
  2.1 2.4 %collective-permute-start = (bf16[144,512]{1,0:T(8,128)(2,1)}, bf16[144,512]{1,0:T(8,128)(2,1)S(1)}, u32[]{:S(2)}, u32[]{:S(2)}) collective-permute-start(bf16[144,512]{1,0:T(8,128)(2,1)} %get-tuple-element.60), channel_id=1, source_target_pairs={{0,3},{1,2},{2,1},{3,0},{4,7},{5,6},{6,5},{7,4},{8,11},{9,10},{10,... | collective-permute-start | bytes 442376 | tf_op jit(solution)/shard_map/ppermute | solution.py:700
  4.5 0.6 collective-permute-start.1
  5.0 0.1 collective-permute-start.2
  5.1 1.9 %pack.3 = (bf16[128,512]{1,0:T(8,128)(2,1)}, bf16[128,512]{1,0:T(8,128)(2,1)}, bf16[128,512]{1,0:T(8,128)(2,1)}, bf16[128,512]{1,0:T(8,128)(2,1)}) custom-call(s32[1]{0:T(128)} %bitcast.member, bf16[128,2048]{1,0:T(8,128)(2,1)} %refs_2_.1), custom_call_target="tpu_custom_call" | custom-call | flops 3000000000 | bytes 9000000 | tf_op jit(solution)/shard_map/pack/pallas_call | solution.py:445
  7.0 2.2 %pack.4 = (bf16[128,1024]{1,0:T(8,128)(2,1)}, bf16[128,1024]{1,0:T(8,128)(2,1)}, bf16[128,1024]{1,0:T(8,128)(2,1)}, bf16[128,1024]{1,0:T(8,128)(2,1)}) custom-call(s32[1]{0:T(128)} %bitcast.member, bf16[128,4096]{1,0:T(8,128)(2,1)} %refs_0_.6), custom_call_target="tpu_custom_call" | custom-call | flops 3000000000 | bytes 9000000 | tf_op jit(solution)/shard_map/pack/pallas_call | solution.py:445
  9.2 2.4 %pack.5 = (bf16[128,1024]{1,0:T(8,128)(2,1)}, bf16[128,1024]{1,0:T(8,128)(2,1)}, bf16[128,1024]{1,0:T(8,128)(2,1)}, bf16[128,1024]{1,0:T(8,128)(2,1)}) custom-call(s32[1]{0:T(128)} %bitcast.member, bf16[128,4096]{1,0:T(8,128)(2,1)} %refs_0_.7), custom_call_target="tpu_custom_call" | custom-call | flops 3000000000 | bytes 9000000 | tf_op jit(solution)/shard_map/pack/pallas_call | solution.py:445
  11.6 0.0 collective-permute-done.refs_3_.refs_7_
  11.6 0.6 collective-permute-done.1.refs_2_.refs_6_
  12.2 0.0 collective-permute-done.2.refs_1_.refs_5_
  12.2 0.8 fusion.1
  13.0 4.2 %collective-permute-start.6 = (bf16[32,512]{1,0:T(8,128)(2,1)S(1)}, bf16[32,512]{1,0:T(8,128)(2,1)S(1)}, u32[]{:S(2)}, u32[]{:S(2)}) collective-permute-start(bf16[32,512]{1,0:T(8,128)(2,1)S(1)} %fusion.1), channel_id=1, source_target_pairs={{0,4},{4,8},{8,12},{12,16},{16,20},{20,24},{24,28},{1,5},{5,9},{9,... | collective-permute-start | bytes 98312 | tf_op jit(solution)/shard_map/ppermute | solution.py:759
  17.3 0.1 collective-permute-start.3
  17.4 1.6 %collective-permute-start.4 = (bf16[128,1024]{1,0:T(8,128)(2,1)S(1)}, bf16[128,1024]{1,0:T(8,128)(2,1)S(1)}, u32[]{:S(2)}, u32[]{:S(2)}) collective-permute-start(bf16[128,1024]{1,0:T(8,128)(2,1)S(1)} %copy-done.12), channel_id=1, source_target_pairs={{0,2},{1,3},{2,0},{3,1},{4,6},{5,7},{6,4},{7,5},{8,10},{9,11},{10,... | collective-permute-start | bytes 786440 | tf_op jit(solution)/shard_map/ppermute | solution.py:700
  18.9 0.3 collective-permute-start.5
  19.2 0.0 collective-permute-done.6.refs_8_.refs_4_
  19.2 0.0 copy-done.7
  19.3 0.0 copy-start.23
  19.3 0.6 copy-done.23
  19.9 13.1 %key_terms.1 = (bf16[4,4,2,128,256]{4,3,2,1,0:T(8,128)(2,1)}, bf16[4,4,128,256]{3,2,1,0:T(8,128)(2,1)}, bf16[4,4,2,128,256]{4,3,2,1,0:T(8,128)(2,1)}, bf16[4,4,2...) custom-call(s32[1]{0:T(128)} %bitcast.member, ...), custom_call_target="tpu_custom_call" | custom-call | flops 12000000000 | bytes 36000000 | tf_op jit(solution)/shard_map/key_terms/pallas_call | solution.py:531
  33.0 0.0 collective-permute-done.3.refs_1_
  33.0 0.0 collective-permute-done.4.refs_2_
  33.0 0.0 collective-permute-done.5.refs_3_
  33.0 0.7 copy-done.14
  33.7 0.1 copy-done.15
  33.8 0.1 copy-done.16
  33.9 7.6 %value_terms.1 = (bf16[4,4,2,128,256]{4,3,2,1,0:T(8,128)(2,1)}, bf16[4,3,2,128,256]{4,3,2,1,0:T(8,128)(2,1)}, bf16[8,128,256]{2,1,0:T(8,128)(2,1)}) custom-call(s32[1]{0:T(128)} %bitcast.member, bf16[128,1024]{1,0:T(8,128)(2,1)} %get-tuple-element.72.refs_0_, bf16[128,1024]{1,0:T(8,128)(2,1)} %copy-done.14, bf16[128,1024]{1,0:T(8,128)(2,1)} %copy-done.15, ...), custom_call_target="tpu_custom_call" | custom-call | flops 7000000000 | bytes 21000000 | tf_op jit(solution)/shard_map/value_terms/pallas_call | solution.py:559
  41.5 0.4 collective-permute-start.14
  41.9 5.9 %all-to-all-start = ((bf16[8,1,128,256]{3,2,1,0:T(8,128)(2,1)}), bf16[8,1,128,256]{3,2,1,0:T(8,128)(2,1)S(1)}, u32[]{:S(2)}, u32[]{:S(2)}) async-start(bf16[8,1,128,256]{3,2,1,0:T(8,128)(2,1)} %bitcast.10), calls=%async_computation | async-start | bytes 1048576 | tf_op jit(solution)/shard_map/all_to_all | solution.py:720
  47.8 0.3 collective-permute-start.7
  48.1 1.5 %collective-permute-start.8 = (bf16[128,512]{1,0:T(8,128)(2,1)S(1)}, bf16[128,512]{1,0:T(8,128)(2,1)S(1)}, u32[]{:S(2)}, u32[]{:S(2)}) collective-permute-start(bf16[128,512]{1,0:T(8,128)(2,1)S(1)} %copy-done.18), channel_id=1, source_target_pairs={{0,2},{1,3},{2,0},{3,1},{4,6},{5,7},{6,4},{7,5},{8,10},{9,11},{10,... | collective-permute-start | bytes 393224 | tf_op jit(solution)/shard_map/ppermute | solution.py:700
  49.6 0.0 collective-permute-start.10
  49.6 0.6 collective-permute-start.11
  50.2 0.0 collective-permute-done.7.refs_1_
  50.2 1.3 %collective-permute-start.12 = (bf16[128,1024]{1,0:T(8,128)(2,1)S(1)}, bf16[128,1024]{1,0:T(8,128)(2,1)S(1)}, u32[]{:S(2)}, u32[]{:S(2)}) collective-permute-start(bf16[128,1024]{1,0:T(8,128)(2,1)S(1)} %copy-done.8), channel_id=1, source_target_pairs={{0,3},{1,2},{2,1},{3,0},{4,7},{5,6},{6,5},{7,4},{8,11},{9,10},{10,... | collective-permute-start | bytes 786440 | tf_op jit(solution)/shard_map/ppermute | solution.py:700
  51.5 2.9 %collective-permute-done.8.refs_2_ = bf16[128,512]{1,0:T(8,128)(2,1)S(1)} collective-permute-done((bf16[128,512]{1,0:T(8,128)(2,1)S(1)}, bf16[128,512]{1,0:T(8,128)(2,1)S(1)}, u32[]{:S(2)}, u32[]{:S(2)}) %collective-permute-start.8) | collective-permute-done | bytes 131104 | tf_op jit(solution)/shard_map/ppermute | solution.py:700
  54.4 0.0 collective-permute-start.9
  54.4 8.5 %all-to-all-done.spans_in = bf16[8,1,128,256]{3,2,1,0:T(8,128)(2,1)S(1)} async-done(((bf16[8,1,128,256]{3,2,1,0:T(8,128)(2,1)}), bf16[8,1,128,256]{3,2,1,0:T(8,128)(2,1)S(1)}, u32[]{:S(2)}, u32[]{:S(2)}) %all-to-all-start) | async-done | bytes 524320 | tf_op jit(solution)/shard_map/all_to_all | solution.py:720
  62.9 1.8 %handoff.1 = bf16[8,1,128,128]{3,2,1,0:T(8,128)(2,1)} custom-call(bf16[8,1,128,256]{3,2,1,0:T(8,128)(2,1)S(1)} %all-to-all-done.spans_in), custom_call_target="tpu_custom_call" | custom-call | flops 1000000000 | bytes 3000000 | tf_op jit(solution)/shard_map/handoff/pallas_call | solution.py:617
  64.7 3.6 %all-to-all-start.1 = ((bf16[8,1,128,128]{3,2,1,0:T(8,128)(2,1)}), bf16[8,1,128,128]{3,2,1,0:T(8,128)(2,1)S(1)}, u32[]{:S(2)}, u32[]{:S(2)}) async-start(bf16[8,1,128,128]{3,2,1,0:T(8,128)(2,1)} %handoff.1), calls=%async_computation.1 | async-start | bytes 524288 | tf_op jit(solution)/shard_map/all_to_all | solution.py:725
  68.4 0.0 collective-permute-done.9.refs_3_
  68.4 0.0 collective-permute-done.10.refs_4_
  68.4 0.0 collective-permute-done.11.refs_5_
  68.4 0.0 collective-permute-done.12.refs_5_
  68.4 0.6 copy-done.22
  69.0 8.3 %query_terms.1 = (bf16[8,512,128]{2,1,0:T(8,128)(2,1)}, bf16[8,512,128]{2,1,0:T(8,128)(2,1)}) custom-call(s32[1]{0:T(128)} %bitcast.member, bf16[128,512]{1,0:T(8,128)(2,1)} %get-tuple-element.91.refs_0_, bf16[128,512]{1,0:T(8,128)(2,1)} %copy-done.20, bf16[128,512]{1,0:T(8,128)(2,1)} %copy-done.21, bf16[128,512]{1,0:T(8,128)(2,1)} %copy-done.22, ...), custom_call_target="tpu_custom_call" | custom-call | flops 8999999488 | bytes 27000000 | tf_op jit(solution)/shard_map/query_terms/pallas_call | solution.py:596
  77.3 0.2 all-to-all-done.1
  77.5 1.2 %copy-done = bf16[8,512,128]{2,1,0:T(8,128)(2,1)S(1)} copy-done((bf16[8,512,128]{2,1,0:T(8,128)(2,1)S(1)}, bf16[8,512,128]{2,1,0:T(8,128)(2,1)}, u32[]{:S(2)}) %copy-start) | copy-done | bytes 1048600
  78.7 1.2 %copy-done.1 = bf16[8,512,128]{2,1,0:T(8,128)(2,1)S(1)} copy-done((bf16[8,512,128]{2,1,0:T(8,128)(2,1)S(1)}, bf16[8,512,128]{2,1,0:T(8,128)(2,1)}, u32[]{:S(2)}) %copy-start.1) | copy-done | bytes 1048600
  79.9 0.8 normed_rows.3
  80.8 0.0 copy-start.4
  80.8 0.1 collective-permute-start.13
  80.9 0.0 copy-done.2
  80.9 0.8 normed_rows.2.mine
  81.7 1.0 %collective-permute-done.13.theirs = bf16[2,128,1024]{2,1,0:T(8,128)(2,1)S(1)} collective-permute-done((bf16[2,128,1024]{2,1,0:T(8,128)(2,1)S(1)}, bf16[2,128,1024]{2,1,0:T(8,128)(2,1)S(1)}, u32[]{:S(2)}, u32[]{:S(2)}) %collective-permute-start.13) | collective-permute-done | bytes 524320 | tf_op jit(solution)/shard_map/ppermute | solution.py:778
  82.8 0.0 collective-permute-done.14.other_weight
  82.8 0.2 copy-done.4
  83.0 2.8 %projected.3 = (f32[128,1024]{1,0:T(8,128)S(1)}, bf16[128,1024]{1,0:T(8,128)(2,1)S(1)}) custom-call(bf16[2,128,1024]{2,1,0:T(8,128)(2,1)S(1)} %normed_rows.2.mine, bf16[2,128,1024]{2,1,0:T(8,128)(2,1)S(1)} %collective-permute-done.13.theirs, bf16[1024,2048]{1,0:T(8,128)(2,1)S(1)} %copy-done.4, bf16[1024,2048]{1,0:T(8,128)(2,1)} %collective-permute-done.14.other_weight), custom_call_target="tpu_custom_call" | custom-call | flops 3000000000 | bytes 9000000 | tf_op jit(solution)/shard_map/projected/pallas_call | solution.py:663
  85.8 1.6 %collective-permute-start.16 = (bf16[128,1024]{1,0:T(8,128)(2,1)S(1)}, bf16[128,1024]{1,0:T(8,128)(2,1)S(1)}, u32[]{:S(2)}, u32[]{:S(2)}) collective-permute-start(bf16[128,1024]{1,0:T(8,128)(2,1)S(1)} %get-tuple-element.106), channel_id=1, source_target_pairs={{0,2},{1,3},{2,0},{3,1},{4,6},{5,7},{6,4},{7,5},{8,10},{9,11},{10,... | collective-permute-start | bytes 786440 | tf_op jit(solution)/shard_map/ppermute | solution.py:789
  87.3 2.8 %projected.2 = (f32[128,1024]{1,0:T(8,128)S(1)}, bf16[128,1024]{1,0:T(8,128)(2,1)S(1)}) custom-call(bf16[2,128,1024]{2,1,0:T(8,128)(2,1)S(1)} %normed_rows.2.mine, bf16[2,128,1024]{2,1,0:T(8,128)(2,1)S(1)} %collective-permute-done.13.theirs, bf16[1024,2048]{1,0:T(8,128)(2,1)S(1)} %copy-done.4, bf16[1024,2048]{1,0:T(8,128)(2,1)} %collective-permute-done.14.other_weight), custom_call_target="tpu_custom_call" | custom-call | flops 3000000000 | bytes 9000000 | tf_op jit(solution)/shard_map/projected/pallas_call | solution.py:663
  90.1 0.6 collective-permute-start.15
  90.7 4.3 %collective-permute-done.16.refs_3_ = bf16[128,1024]{1,0:T(8,128)(2,1)S(1)} collective-permute-done((bf16[128,1024]{1,0:T(8,128)(2,1)S(1)}, bf16[128,1024]{1,0:T(8,128)(2,1)S(1)}, u32[]{:S(2)}, u32[]{:S(2)}) %collective-permute-start.16) | collective-permute-done | bytes 262176 | tf_op jit(solution)/shard_map/ppermute | solution.py:789
  95.0 4.6 %collective-permute-done.15.refs_1_ = bf16[128,1024]{1,0:T(8,128)(2,1)S(1)} collective-permute-done((bf16[128,1024]{1,0:T(8,128)(2,1)S(1)}, bf16[128,1024]{1,0:T(8,128)(2,1)S(1)}, u32[]{:S(2)}, u32[]{:S(2)}) %collective-permute-start.15) | collective-permute-done | bytes 262176 | tf_op jit(solution)/shard_map/ppermute | solution.py:789
  99.6 0.9 summed_parts.1
  (36 shorter events, 0.1 us)
Async XLA Ops:
  2.1 9.5 %collective-permute-start = (bf16[144,512]{1,0:T(8,128)(2,1)}, bf16[144,512]{1,0:T(8,128)(2,1)S(1)}, u32[]{:S(2)}, u32[]{:S(2)}) collective-permute-start(bf16[144,512]{1,0:T(8,128)(2,1)} %get-tuple-element.60), channel_id=1, source_target_pairs={{0,3},{1,2},{2,1},{3,0},{4,7},{5,6},{6,5},{7,4},{8,11},{9,10},{10,... | collective-permute-start | bytes 442376 | tf_op jit(solution)/shard_map/ppermute | solution.py:700
  4.5 7.8 %collective-permute-start.1 = (bf16[144,512]{1,0:T(8,128)(2,1)}, bf16[144,512]{1,0:T(8,128)(2,1)S(1)}, u32[]{:S(2)}, u32[]{:S(2)}) collective-permute-start(bf16[144,512]{1,0:T(8,128)(2,1)} %get-tuple-element.61), channel_id=1, source_target_pairs={{0,2},{1,3},{2,0},{3,1},{4,6},{5,7},{6,4},{7,5},{8,10},{9,11},{10,... | collective-permute-start | bytes 442376 | tf_op jit(solution)/shard_map/ppermute | solution.py:700
  5.0 7.2 %collective-permute-start.2 = (bf16[144,512]{1,0:T(8,128)(2,1)}, bf16[144,512]{1,0:T(8,128)(2,1)S(1)}, u32[]{:S(2)}, u32[]{:S(2)}) collective-permute-start(bf16[144,512]{1,0:T(8,128)(2,1)} %get-tuple-element.62), channel_id=1, source_target_pairs={{0,1},{1,0},{2,3},{3,2},{4,5},{5,4},{6,7},{7,6},{8,9},{9,8},{10,11... | collective-permute-start | bytes 442376 | tf_op jit(solution)/shard_map/ppermute | solution.py:700
  9.2 8.1 %copy-start.13 = (bf16[128,1024]{1,0:T(8,128)(2,1)S(1)}, bf16[128,1024]{1,0:T(8,128)(2,1)}, u32[]{:S(2)}) copy-start(bf16[128,1024]{1,0:T(8,128)(2,1)} %get-tuple-element.73) | copy-start | bytes 786436
  9.2 8.1 %copy-start.12 = (bf16[128,1024]{1,0:T(8,128)(2,1)S(1)}, bf16[128,1024]{1,0:T(8,128)(2,1)}, u32[]{:S(2)}) copy-start(bf16[128,1024]{1,0:T(8,128)(2,1)} %get-tuple-element.74) | copy-start | bytes 786436
  9.2 9.7 %copy-start.11 = (bf16[128,1024]{1,0:T(8,128)(2,1)S(1)}, bf16[128,1024]{1,0:T(8,128)(2,1)}, u32[]{:S(2)}) copy-start(bf16[128,1024]{1,0:T(8,128)(2,1)} %get-tuple-element.75) | copy-start | bytes 786436
  11.6 7.6 %copy-start.5 = (bf16[144,512]{1,0:T(8,128)(2,1)}, bf16[144,512]{1,0:T(8,128)(2,1)S(1)}, u32[]{:S(2)}) copy-start(bf16[144,512]{1,0:T(8,128)(2,1)S(1)} %collective-permute-done.refs_3_.refs_7_) | copy-start | bytes 442372
  12.2 7.0 %copy-start.6 = (bf16[144,512]{1,0:T(8,128)(2,1)}, bf16[144,512]{1,0:T(8,128)(2,1)S(1)}, u32[]{:S(2)}) copy-start(bf16[144,512]{1,0:T(8,128)(2,1)S(1)} %collective-permute-done.1.refs_2_.refs_6_) | copy-start | bytes 442372
  12.2 7.0 %copy-start.7 = (bf16[144,512]{1,0:T(8,128)(2,1)}, bf16[144,512]{1,0:T(8,128)(2,1)S(1)}, u32[]{:S(2)}) copy-start(bf16[144,512]{1,0:T(8,128)(2,1)S(1)} %collective-permute-done.2.refs_1_.refs_5_) | copy-start | bytes 442372
  13.0 6.2 %collective-permute-start.6 = (bf16[32,512]{1,0:T(8,128)(2,1)S(1)}, bf16[32,512]{1,0:T(8,128)(2,1)S(1)}, u32[]{:S(2)}, u32[]{:S(2)}) collective-permute-start(bf16[32,512]{1,0:T(8,128)(2,1)S(1)} %fusion.1), channel_id=1, source_target_pairs={{0,4},{4,8},{8,12},{12,16},{16,20},{20,24},{24,28},{1,5},{5,9},{9,... | collective-permute-start | bytes 98312 | tf_op jit(solution)/shard_map/ppermute | solution.py:759
  17.3 15.7 %collective-permute-start.3 = (bf16[128,1024]{1,0:T(8,128)(2,1)S(1)}, bf16[128,1024]{1,0:T(8,128)(2,1)S(1)}, u32[]{:S(2)}, u32[]{:S(2)}) collective-permute-start(bf16[128,1024]{1,0:T(8,128)(2,1)S(1)} %copy-done.13), channel_id=1, source_target_pairs={{0,1},{1,0},{2,3},{3,2},{4,5},{5,4},{6,7},{7,6},{8,9},{9,8},{10,11... | collective-permute-start | bytes 786440 | tf_op jit(solution)/shard_map/ppermute | solution.py:700
  17.4 15.6 %collective-permute-start.4 = (bf16[128,1024]{1,0:T(8,128)(2,1)S(1)}, bf16[128,1024]{1,0:T(8,128)(2,1)S(1)}, u32[]{:S(2)}, u32[]{:S(2)}) collective-permute-start(bf16[128,1024]{1,0:T(8,128)(2,1)S(1)} %copy-done.12), channel_id=1, source_target_pairs={{0,2},{1,3},{2,0},{3,1},{4,6},{5,7},{6,4},{7,5},{8,10},{9,11},{10,... | collective-permute-start | bytes 786440 | tf_op jit(solution)/shard_map/ppermute | solution.py:700
  18.9 14.1 %collective-permute-start.5 = (bf16[128,1024]{1,0:T(8,128)(2,1)S(1)}, bf16[128,1024]{1,0:T(8,128)(2,1)S(1)}, u32[]{:S(2)}, u32[]{:S(2)}) collective-permute-start(bf16[128,1024]{1,0:T(8,128)(2,1)S(1)} %copy-done.11), channel_id=1, source_target_pairs={{0,3},{1,2},{2,1},{3,0},{4,7},{5,6},{6,5},{7,4},{8,11},{9,10},{10,... | collective-permute-start | bytes 786440 | tf_op jit(solution)/shard_map/ppermute | solution.py:700
  19.3 0.6 copy-start.23
  33.0 0.7 copy-start.14
  33.0 0.8 copy-start.15
  33.0 0.8 copy-start.16
  33.8 14.0 %copy-start.19 = (bf16[128,512]{1,0:T(8,128)(2,1)S(1)}, bf16[128,512]{1,0:T(8,128)(2,1)}, u32[]{:S(2)}) copy-start(bf16[128,512]{1,0:T(8,128)(2,1)} %get-tuple-element.84) | copy-start | bytes 393220
  33.9 14.2 %copy-start.18 = (bf16[128,512]{1,0:T(8,128)(2,1)S(1)}, bf16[128,512]{1,0:T(8,128)(2,1)}, u32[]{:S(2)}) copy-start(bf16[128,512]{1,0:T(8,128)(2,1)} %get-tuple-element.85) | copy-start | bytes 393220
  33.9 15.7 %copy-start.10 = (bf16[128,1024]{1,0:T(8,128)(2,1)S(1)}, bf16[128,1024]{1,0:T(8,128)(2,1)}, u32[]{:S(2)}) copy-start(bf16[128,1024]{1,0:T(8,128)(2,1)} %get-tuple-element.88) | copy-start | bytes 786436
  33.9 15.8 %copy-start.9 = (bf16[128,1024]{1,0:T(8,128)(2,1)S(1)}, bf16[128,1024]{1,0:T(8,128)(2,1)}, u32[]{:S(2)}) copy-start(bf16[128,1024]{1,0:T(8,128)(2,1)} %get-tuple-element.89) | copy-start | bytes 786436
  33.9 16.3 %copy-start.8 = (bf16[128,1024]{1,0:T(8,128)(2,1)S(1)}, bf16[128,1024]{1,0:T(8,128)(2,1)}, u32[]{:S(2)}) copy-start(bf16[128,1024]{1,0:T(8,128)(2,1)} %get-tuple-element.90) | copy-start | bytes 786436
  33.9 20.5 %copy-start.17 = (bf16[128,512]{1,0:T(8,128)(2,1)S(1)}, bf16[128,512]{1,0:T(8,128)(2,1)}, u32[]{:S(2)}) copy-start(bf16[128,512]{1,0:T(8,128)(2,1)} %get-tuple-element.86) | copy-start | bytes 393220
  41.5 41.3 %collective-permute-start.14 = (bf16[1024,2048]{1,0:T(8,128)(2,1)}, bf16[1024,2048]{1,0:T(8,128)(2,1)}, u32[]{:S(2)}, u32[]{:S(2)}) collective-permute-start(bf16[1024,2048]{1,0:T(8,128)(2,1)} %own_weight.3), channel_id=1, source_target_pairs={{0,1},{1,0},{2,3},{3,2},{4,5},{5,4},{6,7},{7,6},{8,9},{9,8},{10,11... | collective-permute-start | bytes 12582920 | tf_op jit(solution)/shard_map/ppermute | solution.py:769
  41.9 21.1 %all-to-all-start = ((bf16[8,1,128,256]{3,2,1,0:T(8,128)(2,1)}), bf16[8,1,128,256]{3,2,1,0:T(8,128)(2,1)S(1)}, u32[]{:S(2)}, u32[]{:S(2)}) async-start(bf16[8,1,128,256]{3,2,1,0:T(8,128)(2,1)} %bitcast.10), calls=%async_computation | async-start | bytes 1048576 | tf_op jit(solution)/shard_map/all_to_all | solution.py:720
  47.8 2.4 %collective-permute-start.7 = (bf16[128,512]{1,0:T(8,128)(2,1)S(1)}, bf16[128,512]{1,0:T(8,128)(2,1)S(1)}, u32[]{:S(2)}, u32[]{:S(2)}) collective-permute-start(bf16[128,512]{1,0:T(8,128)(2,1)S(1)} %copy-done.19), channel_id=1, source_target_pairs={{0,1},{1,0},{2,3},{3,2},{4,5},{5,4},{6,7},{7,6},{8,9},{9,8},{10,11... | collective-permute-start | bytes 393224 | tf_op jit(solution)/shard_map/ppermute | solution.py:700
  48.1 6.3 %collective-permute-start.8 = (bf16[128,512]{1,0:T(8,128)(2,1)S(1)}, bf16[128,512]{1,0:T(8,128)(2,1)S(1)}, u32[]{:S(2)}, u32[]{:S(2)}) collective-permute-start(bf16[128,512]{1,0:T(8,128)(2,1)S(1)} %copy-done.18), channel_id=1, source_target_pairs={{0,2},{1,3},{2,0},{3,1},{4,6},{5,7},{6,4},{7,5},{8,10},{9,11},{10,... | collective-permute-start | bytes 393224 | tf_op jit(solution)/shard_map/ppermute | solution.py:700
  49.6 18.8 %collective-permute-start.10 = (bf16[128,1024]{1,0:T(8,128)(2,1)S(1)}, bf16[128,1024]{1,0:T(8,128)(2,1)S(1)}, u32[]{:S(2)}, u32[]{:S(2)}) collective-permute-start(bf16[128,1024]{1,0:T(8,128)(2,1)S(1)} %copy-done.10), channel_id=1, source_target_pairs={{0,1},{1,0},{2,3},{3,2},{4,5},{5,4},{6,7},{7,6},{8,9},{9,8},{10,11... | collective-permute-start | bytes 786440 | tf_op jit(solution)/shard_map/ppermute | solution.py:700
  49.6 18.8 %collective-permute-start.11 = (bf16[128,1024]{1,0:T(8,128)(2,1)S(1)}, bf16[128,1024]{1,0:T(8,128)(2,1)S(1)}, u32[]{:S(2)}, u32[]{:S(2)}) collective-permute-start(bf16[128,1024]{1,0:T(8,128)(2,1)S(1)} %copy-done.9), channel_id=1, source_target_pairs={{0,2},{1,3},{2,0},{3,1},{4,6},{5,7},{6,4},{7,5},{8,10},{9,11},{10,... | collective-permute-start | bytes 786440 | tf_op jit(solution)/shard_map/ppermute | solution.py:700
  50.2 14.5 %copy-start.20 = (bf16[128,512]{1,0:T(8,128)(2,1)}, bf16[128,512]{1,0:T(8,128)(2,1)S(1)}, u32[]{:S(2)}) copy-start(bf16[128,512]{1,0:T(8,128)(2,1)S(1)} %collective-permute-done.7.refs_1_) | copy-start | bytes 393220
  50.2 18.2 %collective-permute-start.12 = (bf16[128,1024]{1,0:T(8,128)(2,1)S(1)}, bf16[128,1024]{1,0:T(8,128)(2,1)S(1)}, u32[]{:S(2)}, u32[]{:S(2)}) collective-permute-start(bf16[128,1024]{1,0:T(8,128)(2,1)S(1)} %copy-done.8), channel_id=1, source_target_pairs={{0,3},{1,2},{2,1},{3,0},{4,7},{5,6},{6,5},{7,4},{8,11},{9,10},{10,... | collective-permute-start | bytes 786440 | tf_op jit(solution)/shard_map/ppermute | solution.py:700
  54.4 10.3 %copy-start.21 = (bf16[128,512]{1,0:T(8,128)(2,1)}, bf16[128,512]{1,0:T(8,128)(2,1)S(1)}, u32[]{:S(2)}) copy-start(bf16[128,512]{1,0:T(8,128)(2,1)S(1)} %collective-permute-done.8.refs_2_) | copy-start | bytes 393220
  54.4 14.0 %collective-permute-start.9 = (bf16[128,512]{1,0:T(8,128)(2,1)S(1)}, bf16[128,512]{1,0:T(8,128)(2,1)S(1)}, u32[]{:S(2)}, u32[]{:S(2)}) collective-permute-start(bf16[128,512]{1,0:T(8,128)(2,1)S(1)} %copy-done.17), channel_id=1, source_target_pairs={{0,3},{1,2},{2,1},{3,0},{4,7},{5,6},{6,5},{7,4},{8,11},{9,10},{10,... | collective-permute-start | bytes 393224 | tf_op jit(solution)/shard_map/ppermute | solution.py:700
  64.7 12.8 %all-to-all-start.1 = ((bf16[8,1,128,128]{3,2,1,0:T(8,128)(2,1)}), bf16[8,1,128,128]{3,2,1,0:T(8,128)(2,1)S(1)}, u32[]{:S(2)}, u32[]{:S(2)}) async-start(bf16[8,1,128,128]{3,2,1,0:T(8,128)(2,1)} %handoff.1), calls=%async_computation.1 | async-start | bytes 524288 | tf_op jit(solution)/shard_map/all_to_all | solution.py:725
  68.4 0.6 copy-start.22
  69.0 8.5 %copy-start.3 = (f32[128]{0:T(128)S(1)}, f32[128]{0:T(128)}, u32[]{:S(2)}) copy-start(f32[128]{0:T(128)} %param.20) | copy-start | bytes 1540
  77.5 1.2 %copy-start = (bf16[8,512,128]{2,1,0:T(8,128)(2,1)S(1)}, bf16[8,512,128]{2,1,0:T(8,128)(2,1)}, u32[]{:S(2)}) copy-start(bf16[8,512,128]{2,1,0:T(8,128)(2,1)} %get-tuple-element.100.refs_0_.refs_1_) | copy-start | bytes 3145732
  78.7 1.2 %copy-start.1 = (bf16[8,512,128]{2,1,0:T(8,128)(2,1)S(1)}, bf16[8,512,128]{2,1,0:T(8,128)(2,1)}, u32[]{:S(2)}) copy-start(bf16[8,512,128]{2,1,0:T(8,128)(2,1)} %get-tuple-element.101.refs_2_.refs_3_) | copy-start | bytes 3145732
  79.9 0.9 copy-start.2
  80.8 2.2 %copy-start.4 = (bf16[1024,2048]{1,0:T(8,128)(2,1)S(1)}, bf16[1024,2048]{1,0:T(8,128)(2,1)}, u32[]{:S(2)}) copy-start(bf16[1024,2048]{1,0:T(8,128)(2,1)} %own_weight.3) | copy-start | bytes 12582916
  80.8 2.0 %collective-permute-start.13 = (bf16[2,128,1024]{2,1,0:T(8,128)(2,1)S(1)}, bf16[2,128,1024]{2,1,0:T(8,128)(2,1)S(1)}, u32[]{:S(2)}, u32[]{:S(2)}) collective-permute-start(bf16[2,128,1024]{2,1,0:T(8,128)(2,1)S(1)} %normed_rows.3), channel_id=1, source_target_pairs={{0,1},{1,0},{2,3},{3,2},{4,5},{5,4},{6,7},{7,6},{8,9},{9,8},{10,11... | collective-permute-start | bytes 1572872 | tf_op jit(solution)/shard_map/ppermute | solution.py:778
  85.8 9.3 %collective-permute-start.16 = (bf16[128,1024]{1,0:T(8,128)(2,1)S(1)}, bf16[128,1024]{1,0:T(8,128)(2,1)S(1)}, u32[]{:S(2)}, u32[]{:S(2)}) collective-permute-start(bf16[128,1024]{1,0:T(8,128)(2,1)S(1)} %get-tuple-element.106), channel_id=1, source_target_pairs={{0,2},{1,3},{2,0},{3,1},{4,6},{5,7},{6,4},{7,5},{8,10},{9,11},{10,... | collective-permute-start | bytes 786440 | tf_op jit(solution)/shard_map/ppermute | solution.py:789
  90.1 9.5 %collective-permute-start.15 = (bf16[128,1024]{1,0:T(8,128)(2,1)S(1)}, bf16[128,1024]{1,0:T(8,128)(2,1)S(1)}, u32[]{:S(2)}, u32[]{:S(2)}) collective-permute-start(bf16[128,1024]{1,0:T(8,128)(2,1)S(1)} %get-tuple-element.104), channel_id=1, source_target_pairs={{0,2},{1,3},{2,0},{3,1},{4,6},{5,7},{6,4},{7,5},{8,10},{9,11},{10,... | collective-permute-start | bytes 786440 | tf_op jit(solution)/shard_map/ppermute | solution.py:789

commit v4 on v3

--- a/solution.py
+++ b/solution.py
@@ -181,7 +181,7 @@
 def key_kernel(groups_count, heads, member, *refs):
     pieces, refs = refs[:groups_count], refs[groups_count:]
     gate_pieces, refs = refs[:groups_count], refs[groups_count:]
-    edge, taps, t_out, kt_out, ktail_out, w_out, d_out, p_out, last_out, map_out, padded, gates = refs
+    edge, taps, t_out, kt_out, d_out, rows_out, map_out, padded, gates = refs
     here = pieces[0].shape[1] // DK
     count = here * SHARE
     blocks = gates.shape[0] // CH
@@ -204,15 +204,21 @@
     turned = {g: jnp.transpose(keys[g]) for g in groups}
     sides = {g: split(turned[g]) for g in groups}
     kk = {g: product(as_left(keys[g]), right_of(*sides[g])) for g in groups}
-    lane = lax.broadcasted_iota(jnp.int32, (8, gates.shape[1]), 1)
-    order = lax.broadcasted_iota(jnp.int32, (8, gates.shape[1]), 0)
-    pick = ones_where(lane == first + order)
+    lane = lax.broadcasted_iota(jnp.int32, (2 * count, gates.shape[1]), 1)
+    order = lax.broadcasted_iota(jnp.int32, (2 * count, gates.shape[1]), 0)
+    pick = ones_where(lane == first + jnp.where(order < count, order, order - count + heads))
     across = [
         lax.dot_general(
             pick,
             gates[c * CH : (c + 1) * CH, :],
             (((1,), (1,)), ((), ())),
             preferred_element_type=f32,
+        )
+        for c in range(blocks)
+    ]
+    growing = [
+        jnp.exp(
+            jnp.dot(across[c].astype(bf16), ones_where(row <= column), preferred_element_type=f32)
         )
         for c in range(blocks)
     ]
@@ -224,47 +230,96 @@
         strength = chunk_of(strengths, c)[:, e * CH : (e + 1) * CH]
         k = e // SHARE
         lower[c, e] = jnp.where(column < row, strength * kk[c, k] * ratios, 0.0)
-        ktail[c, e] = as_left(turned[c, k] * ratios[CH - 1 : CH])
-        ktail_out[k, c, e % SHARE] = ktail[c, e]
-        last_out[k, c, e % SHARE] = growth[CH - 8 : CH]
+        ktail[c, e] = (turned[c, k] * ratios[CH - 1 : CH]).astype(bf16)
+        rows_out[k, c, e % SHARE] = jnp.concatenate(
+            [ratios[CH - 1 : CH], growing[c][count + e : count + e + 1], growth[CH - 6 : CH]],
+            axis=0,
+        )
     inverse = unit_lower_inverses(lower)
     solving = {(c, e): as_left(inverse[c, e] * across[c][e : e + 1]) for c, e in problems}
     solved = {
-        (c, e): product(solving[c, e], as_right(decays[c][1][e] * keys[c, e // SHARE]))
+        (c, e): jnp.dot(
+            solving[c, e][:, :CH],
+            (decays[c][1][e] * keys[c, e // SHARE]).astype(bf16),
+            preferred_element_type=f32,
+        ).astype(bf16)
         for c, e in problems
     }
-    erasing = {pc: split(solved[pc]) for pc in problems}
-    maps = {pc: as_left(product(ktail[pc], right_of(*erasing[pc]))) for pc in problems}
+    maps = {
+        pc: jnp.dot(ktail[pc], solved[pc], preferred_element_type=f32).astype(bf16)
+        for pc in problems
+    }
     for c, e in problems:
         k = e // SHARE
-        t_out[k, c, e % SHARE] = solving[c, e]
-        w_out[k, c, e % SHARE] = jnp.concatenate(erasing[c, e], axis=1)
+        t_out[k, c, e % SHARE] = solving[c, e][:, :CH]
         d_out[k, c, e % SHARE] = maps[c, e]
-    running = []
-    for e in range(count):
-        high, low = maps[0, e][:, :DK], maps[0, e][:, DK:]
-        running.append(
-            decays[0][1][e][CH - 1 : CH] * eye - (high.astype(f32) + low.astype(f32))
-        )
+    running = [
+        decays[0][1][e][CH - 1 : CH] * eye - maps[0, e].astype(f32) for e in range(count)
+    ]
     for c in range(1, blocks):
-        parts = [split(x) for x in running]
-        for e in range(count):
-            p_out[e // SHARE, c - 1, e % SHARE] = jnp.concatenate(parts[e], axis=1)
         running = [
-            decays[c][1][e][CH - 1 : CH] * running[e] - product(maps[c, e], right_of(*parts[e]))
+            decays[c][1][e][CH - 1 : CH] * running[e]
+            - jnp.dot(maps[c, e], running[e].astype(bf16), preferred_element_type=f32)
             for e in range(count)
         ]
     for e in range(count):
         map_out[e] = (eye - running[e]).astype(bf16)
 
 
+def prefix_kernel(t_in, kt_in, d_in, rows_in, w_out, p_out):
+    here, blocks = t_in.shape[0], t_in.shape[1]
+    count = here * SHARE
+    row, column = grids()
+    eye = jnp.where(row == column, 1.0, 0.0)
+
+    def at(ref, c, e):
+        return ref[e // SHARE, c, e % SHARE]
+
+    keys = {
+        (c, k): jnp.transpose(whole_of(kt_in[k, c])).astype(bf16)
+        for c in range(blocks)
+        for k in range(here)
+    }
+    problems = [(c, e) for c in range(blocks) for e in range(count)]
+    scaled = {
+        (c, e): (at(t_in, c, e).astype(f32) * at(rows_in, c, e)[1:2]).astype(bf16) for c, e in problems
+    }
+    for c, e in problems:
+        solved = jnp.dot(scaled[c, e], keys[c, e // SHARE], preferred_element_type=f32)
+        w_out[e // SHARE, c, e % SHARE] = solved.astype(bf16)
+    running = [
+        at(rows_in, 0, e)[7:8] * eye - at(d_in, 0, e).astype(f32) for e in range(count)
+    ]
+    for c in range(1, blocks):
+        parts = [x.astype(bf16) for x in running]
+        for e in range(count):
+            p_out[e // SHARE, c - 1, e % SHARE] = parts[e]
+        if c + 1 < blocks:
+            running = [
+                at(rows_in, c, e)[7:8] * running[e]
+                - jnp.dot(at(d_in, c, e), parts[e], preferred_element_type=f32)
+                for e in range(count)
+            ]
+
+
+def both_of(left, parts):
+    both = jnp.dot(left, jnp.concatenate(parts, axis=1), preferred_element_type=f32)
+    half = both.shape[1] // 2
+    return both[:, :half] + both[:, half:]
+
+
+def whole_of(both):
+    half = both.shape[1] // 2
+    return both[:, :half].astype(f32) + both[:, half:].astype(f32)
+
+
 def right_from(both):
     return jnp.concatenate([both, both], axis=0)
 
 
 def value_kernel(groups_count, member, *refs):
     pieces, refs = refs[:groups_count], refs[groups_count:]
-    edge, taps, t_in, ktail, d_in, last, maps, u_out, z_out, span_out, padded, before = refs
+    edge, taps, t_in, kt_in, d_in, rows_in, maps, u_out, z_out, span_out, padded, before = refs
     blocks = t_in.shape[1]
     width = pieces[0].shape[1]
     count = width // DV
@@ -280,24 +335,31 @@
 
     written = {
         (c, e): split(
-            product(
+            jnp.dot(
                 at(t_in, c, e),
-                as_right(values[c * CH : (c + 1) * CH, e * DV : (e + 1) * DV]),
+                values[c * CH : (c + 1) * CH, e * DV : (e + 1) * DV].astype(bf16),
+                preferred_element_type=f32,
             )
         )
         for c, e in problems
     }
-    adds = {pc: product(at(ktail, *pc), right_of(*written[pc])) for pc in problems}
+    tailed = {
+        (c, e): (whole_of(kt_in[e // SHARE, c]) * at(rows_in, c, e)[0:1]).astype(bf16)
+        for c, e in problems
+    }
+    adds = {
+        pc: jnp.dot(tailed[pc], written[pc][0], preferred_element_type=f32) for pc in problems
+    }
     for c, e in problems:
         u_out[e // SHARE, c, e % SHARE] = jnp.concatenate(written[c, e], axis=1)
     running = [adds[0, e] for e in range(count)]
     for c in range(1, blocks):
-        parts = [split(x) for x in running]
+        parts = [x.astype(bf16) for x in running]
         for e in range(count):
-            z_out[e // SHARE, c - 1, e % SHARE] = jnp.concatenate(parts[e], axis=1)
+            z_out[e // SHARE, c - 1, e % SHARE] = parts[e]
         running = [
-            at(last, c, e)[7:8] * running[e]
-            - product(at(d_in, c, e), right_of(*parts[e]))
+            at(rows_in, c, e)[7:8] * running[e]
+            - jnp.dot(at(d_in, c, e), parts[e], preferred_element_type=f32)
             + adds[c, e]
             for e in range(count)
         ]
@@ -334,7 +396,8 @@
     mix = {(c, e): as_left(qk[c, e // SHARE] * decays[c][0][e]) for c, e in problems}
     entry = {
         (c, e): as_left(
-            decays[c][1][e] * queries[c, e // SHARE] - product(mix[c, e], at(w_in, c, e))
+            decays[c][1][e] * queries[c, e // SHARE]
+            - jnp.dot(mix[c, e], at(w_in, c, e), preferred_element_type=f32)
         )
         for c, e in problems
     }
@@ -345,12 +408,16 @@
             f_out[e, here] = entry[c, e][:, :DK]
             g_out[e, here] = local[c, e].astype(bf16)
         else:
-            f_out[e, here] = product(entry[c, e], at(p_in, c - 1, e)).astype(bf16)
-            total = local[c, e] + product(entry[c, e], at(z_in, c - 1, e))
+            f_out[e, here] = jnp.dot(
+                entry[c, e], at(p_in, c - 1, e), preferred_element_type=f32
+            ).astype(bf16)
+            total = local[c, e] + jnp.dot(
+                entry[c, e], at(z_in, c - 1, e), preferred_element_type=f32
+            )
             g_out[e, here] = total.astype(bf16)
 
 
-def handoff_kernel(spans_in, out):
+def handoff_kernel(terms, out):
     spans, heads, width = out.shape[0], out.shape[1], out.shape[3]
     running = [jnp.zeros(out.shape[2:], f32) for h in range(heads)]
     for j in range(spans):
@@ -359,12 +426,12 @@
         if j + 1 < spans:
             for h in range(heads):
                 erased = jnp.dot(
-                    spans_in[j, h, :, :DK],
+                    terms[j, h, :, :DK],
                     jnp.concatenate(split(running[h]), axis=1),
                     preferred_element_type=f32,
                 )
                 erased = erased[:, :width] + erased[:, width:]
-                running[h] = running[h] - erased + spans_in[j, h, :, DK:].astype(f32)
+                running[h] = running[h] - erased + terms[j, h, :, DK:].astype(f32)
 
 
 def norm_kernel(count, member, *refs):
@@ -490,8 +557,11 @@
     return pl.BlockSpec((rows, width), lambda p, me: (0, p))
 
 
-def heads_at_once(key_heads):
-    return 2 if key_heads % 2 == 0 else 1
+KEY_STEP, VALUE_STEP, PREFIX_STEP, QUERY_STEP = 2, 2, 2, 2
+
+
+def heads_at_once(key_heads, most):
+    return most if key_heads % most == 0 else key_heads
 
 
 def cost(microseconds):
@@ -515,19 +585,16 @@
     own = packed[0].shape[0] - EDGE
     tokens = groups * own
     key_heads = taps.shape[1] // DK
-    each = heads_at_once(key_heads)
+    each = heads_at_once(key_heads, KEY_STEP)
     blocks = tokens // CH
     wide = (blocks, SHARE, CH, 2 * CH)
     kinds = [
-        wide,
+        (blocks, SHARE, CH, CH),
         (blocks, DK, 2 * CH),
-        wide,
-        wide,
-        wide,
-        (blocks - 1, SHARE, DK, 2 * DK),
+        (blocks, SHARE, DK, DK),
         (blocks, SHARE, 8, CH),
     ]
-    types = [bf16] * 6 + [f32]
+    types = [bf16] * 3 + [f32]
     return pl.pallas_call(
         functools.partial(key_kernel, groups, key_heads * SHARE),
         grid_spec=grid_of(
@@ -548,12 +615,12 @@
     )(member, *packed, *packed, edge, taps)
 
 
-def value_terms(member, pieces, edge, taps, t_in, ktail, d_in, last, maps):
+def value_terms(member, pieces, edge, taps, t_in, kt_in, d_in, rows_in, maps):
     groups = len(pieces)
     own = pieces[0].shape[0]
     tokens = groups * own
     key_heads = t_in.shape[0]
-    each = heads_at_once(key_heads)
+    each = heads_at_once(key_heads, VALUE_STEP)
     blocks = tokens // CH
     width = each * SHARE * DV
     return pl.pallas_call(
@@ -563,11 +630,11 @@
             [columns_of(own, width)] * groups
             + [pl.BlockSpec((EDGE, key_heads * DK), lambda p, me: (1, 0))]
             + [columns_of(taps.shape[0], width)]
-            + [per_head(each, x.shape[1:]) for x in (t_in, ktail, d_in, last)]
+            + [per_head(each, x.shape[1:]) for x in (t_in, kt_in, d_in, rows_in)]
             + [pl.BlockSpec((each * SHARE, DK, DK), lambda p, me: (p, 0, 0))],
             [
                 per_head(each, (blocks, SHARE, CH, 2 * DV)),
-                per_head(each, (blocks - 1, SHARE, DK, 2 * DV)),
+                per_head(each, (blocks - 1, SHARE, DK, DV)),
                 pl.BlockSpec((each * SHARE, DK, DK + DV), lambda p, me: (p, 0, 0)),
             ],
             [
@@ -577,13 +644,13 @@
         ),
         out_shape=[
             shape((key_heads, blocks, SHARE, CH, 2 * DV), bf16),
-            shape((key_heads, blocks - 1, SHARE, DK, 2 * DV), bf16),
+            shape((key_heads, blocks - 1, SHARE, DK, DV), bf16),
             shape((key_heads * SHARE, DK, DK + DV), bf16),
         ],
         compiler_params=params(),
         cost_estimate=cost(7),
         name="value_terms",
-    )(member, *pieces, edge, taps, t_in, ktail, d_in, last, maps)
+    )(member, *pieces, edge, taps, t_in, kt_in, d_in, rows_in, maps)
 
 
 def query_terms(member, pieces, edge, packed, taps, kt, w, p, u, z):
@@ -591,7 +658,7 @@
     own = pieces[0].shape[0]
     tokens = groups * own
     key_heads = kt.shape[0]
-    each = heads_at_once(key_heads)
+    each = heads_at_once(key_heads, QUERY_STEP)
     out = pl.BlockSpec((each * SHARE, tokens, DK), lambda p, me: (p, 0, 0))
     return pl.pallas_call(
         functools.partial(query_kernel, groups, key_heads * SHARE),
@@ -612,15 +679,35 @@
     )(member, *pieces, *packed, edge, taps, kt, w, p, u, z)
 
 
-def handoff(spans):
-    dims = spans.shape[:3] + (spans.shape[3] - DK,)
+def handoff(terms):
+    dims = terms.shape[:3] + (terms.shape[3] - DK,)
     return pl.pallas_call(
         handoff_kernel,
         out_shape=shape(dims, bf16),
         compiler_params=params(16),
         cost_estimate=cost(1),
         name="handoff",
-    )(spans)
+    )(terms)
+
+
+def prefix_terms(t, kt, d, rows):
+    key_heads, blocks = t.shape[0], t.shape[1]
+    each = heads_at_once(key_heads, PREFIX_STEP)
+
+    def some(dims):
+        return pl.BlockSpec((each,) + dims, lambda p: (p,) + (0,) * len(dims))
+
+    outs = [(blocks, SHARE, CH, DK), (blocks - 1, SHARE, DK, DK)]
+    return pl.pallas_call(
+        prefix_kernel,
+        grid=(key_heads // each,),
+        in_specs=[some(x.shape[1:]) for x in (t, kt, d, rows)],
+        out_specs=[some(dims) for dims in outs],
+        out_shape=[shape((key_heads,) + dims, bf16) for dims in outs],
+        compiler_params=params(),
+        cost_estimate=cost(5),
+        name="prefix_terms",
+    )(t, kt, d, rows)
 
 
 def normed_rows(member, f, g, state, gate, gain, parity):
@@ -752,23 +839,23 @@
     edge = packed[0][-2 * EDGE :]
     for d in range(1, groups):
         edge = jnp.where((member[0] ^ d) == groups - 1, packed[d][-2 * EDGE :], edge)
+    edge = jnp.where(lax.axis_index("seq") == spans - 1, jnp.zeros_like(edge), edge)
     value_out = pack(member, value_input, groups)
     query_out = pack(member, query_input, groups)
     gate_out = pack(member, gate_input, groups)
     edge, *value_out = after_all([edge, *value_out], [*query_out, *gate_out])
-    edge = lax.ppermute(edge, "seq", [(s, s + 1) for s in range(spans - 1)])
+    edge = lax.ppermute(edge, "seq", [(s, (s + 1) % spans) for s in range(spans)])
     value_rows = to_members(value_out)
-    t, kt, ktail, w, d, p, last, maps = key_terms(member, packed, edge, filter_key)
-    u, z, terms = value_terms(
-        member, value_rows, edge, filter_value, t, ktail, d, last, maps
-    )
-    query_rows = to_members(after_all(query_out, [terms]))
-    gate_rows = to_members(after_all(gate_out, [terms]))
-    (own_weight,) = after_all([out_weight], [terms])
+    t, kt, d, rows, maps = key_terms(member, packed, edge, filter_key)
+    u, z, adds = value_terms(member, value_rows, edge, filter_value, t, kt, d, rows, maps)
+    query_rows = to_members(after_all(query_out, [adds]))
+    gate_rows = to_members(after_all(gate_out, [adds]))
     swap = [(i, i ^ 1) for i in range(groups)]
+    (own_weight,) = after_all([out_weight], [adds])
     other_weight = lax.ppermute(own_weight, "head", swap)
-    terms = to_runners(terms)
-    entries = handoff(terms)
+    w, p = prefix_terms(*after_all([t, kt, d, rows], [adds]))
+    adds, w, p = after_all([to_runners(adds), w, p], [])
+    entries = handoff(adds)
     query_rows = after_all(query_rows, [entries, *gate_rows])
     f, g = query_terms(member, query_rows, edge, packed, filter_query, kt, w, p, u, z)
     state = from_runners(entries, heads)

time: 101 us -> 96 us (0.950)
  starting transfers between devices: 25.1 us -> 21.1 us
    all_to_all x1, waiting for transfers between devices: 8.53 us -> 5.07 us  [to_runners(): return lax.all_to_all(pieces, 'seq', 0, 0)]
    pallas_call x0 -> x1, Pallas kernels: none -> 3.4 us  [prefix_terms(): pl.pallas_call(prefix_kernel, grid=(key_heads // each,), in_specs=[some(x...]
    ppermute x1, waiting for transfers between devices: 0.01 us -> 3.06 us  [on_device(): lax.ppermute(edge, 'seq', [(s, (s + 1) % spans) for s in range(spans)])]
    pallas_call x1, Pallas kernels: 13.1 us -> 10.6 us  [key_terms(): pl.pallas_call(functools.partial(key_kernel, groups, key_heads * SHARE),...]
    all_to_all x1, starting transfers between devices: 5.92 us -> 3.51 us  [to_runners(): return lax.all_to_all(pieces, 'seq', 0, 0)]
    ppermute x1, starting transfers between devices: 4.24 us -> 2.38 us  [on_device(): lax.ppermute(edge, 'seq', [(s, (s + 1) % spans) for s in range(spans)])]
    pallas_call x1, Pallas kernels: 7.59 us -> 6.22 us  [value_terms(): pl.pallas_call(functools.partial(value_kernel, groups), grid_spec=grid_of...]
  transfers between devices with their start and end apart: 19 -> 19, of which waited for: 7 -> 9; matrix products, arithmetic and copies ran while one was open for 0% -> 0% of each run, Pallas kernels for 34% -> 36%
where the time goes in v4:
time: 96 us; the launch traced here: 95.3 us
  Pallas kernels  46.4 us (48%)
  waiting for transfers between devices  22.1 us (23%)
  starting transfers between devices  21.1 us (22%)
  local copies, waits for them, and re-layouts  4.59 us (5%)
    pallas_call x1, Pallas kernels, key_terms(): pl.pallas_call(functools.partial(key_kernel, groups, key_heads * SHARE),...  10.6 us
    ppermute x12, starting transfers between devices, to_members(): lax.ppermute(pieces[d], 'head', [(i, i ^ d) for i in range(groups)])  9.25 us
    ppermute x2, waiting for transfers between devices, on_device(): lax.ppermute(part, 'head', [(i, i ^ 2 * step + 2) for i in range(groups)])  9.09 us
    pallas_call x1, Pallas kernels, query_terms(): pl.pallas_call(functools.partial(query_kernel, groups, key_heads * SHARE)...  7.73 us
    pallas_call x3, Pallas kernels, pack(): pl.pallas_call(functools.partial(pack_kernel, groups), grid_spec=grid_of(...  6.52 us
    pallas_call x1, Pallas kernels, value_terms(): pl.pallas_call(functools.partial(value_kernel, groups), grid_spec=grid_of...  6.22 us
    pallas_call x2, Pallas kernels, projected(): pl.pallas_call(project_kernel, grid=(width // tile,), in_specs=[whole, wh...  5.56 us
    all_to_all x1, waiting for transfers between devices, to_runners(): return lax.all_to_all(pieces, 'seq', 0, 0)  5.07 us
  transfers between devices with their start and end apart: 19, of which 9 were waited for; matrix products, arithmetic and copies ran while one was open for 0% of the time, Pallas kernels for 36%

profile of v4, /device:TPU:0, one launch (start us, length us, event | category | flops | bytes accessed | tf_op | source)
XLA Modules:
  0.0 95.3 jit_solution(8885099140362979827)
XLA Ops:
  0.0 2.1 %pack_keys.1 = (bf16[144,512]{1,0:T(8,128)(2,1)}, bf16[144,512]{1,0:T(8,128)(2,1)}, bf16[144,512]{1,0:T(8,128)(2,1)}, bf16[144,512]{1,0:T(8,128)(2,1)}) custom-call(s32[1]{0:T(128)} %bitcast.member, bf16[128,2048]{1,0:T(8,128)(2,1)} %refs_0_.5, bf16[128,4096]{1,0:T(8,128)(2,1)} %refs_0_.6, bf16[128,2048]{1,0:T(8,128)(2,1)} %refs_2_.1, ...), custom_call_target="tpu_custom_call" | custom-call | flops 3000000000 | bytes 9000000 | tf_op jit(solution)/shard_map/pack_keys/pallas_call | solution.py:537
  2.1 2.4 %collective-permute-start = (bf16[144,512]{1,0:T(8,128)(2,1)}, bf16[144,512]{1,0:T(8,128)(2,1)S(1)}, u32[]{:S(2)}, u32[]{:S(2)}) collective-permute-start(bf16[144,512]{1,0:T(8,128)(2,1)} %get-tuple-element.66), channel_id=1, source_target_pairs={{0,3},{1,2},{2,1},{3,0},{4,7},{5,6},{6,5},{7,4},{8,11},{9,10},{10,... | collective-permute-start | bytes 442376 | tf_op jit(solution)/shard_map/ppermute | solution.py:787
  4.5 0.6 collective-permute-start.1
  5.1 0.1 collective-permute-start.2
  5.1 1.9 %pack.3 = (bf16[128,512]{1,0:T(8,128)(2,1)}, bf16[128,512]{1,0:T(8,128)(2,1)}, bf16[128,512]{1,0:T(8,128)(2,1)}, bf16[128,512]{1,0:T(8,128)(2,1)}) custom-call(s32[1]{0:T(128)} %bitcast.member, bf16[128,2048]{1,0:T(8,128)(2,1)} %refs_2_.1), custom_call_target="tpu_custom_call" | custom-call | flops 3000000000 | bytes 9000000 | tf_op jit(solution)/shard_map/pack/pallas_call | solution.py:512
  7.0 2.3 %pack.4 = (bf16[128,1024]{1,0:T(8,128)(2,1)}, bf16[128,1024]{1,0:T(8,128)(2,1)}, bf16[128,1024]{1,0:T(8,128)(2,1)}, bf16[128,1024]{1,0:T(8,128)(2,1)}) custom-call(s32[1]{0:T(128)} %bitcast.member, bf16[128,4096]{1,0:T(8,128)(2,1)} %refs_0_.6), custom_call_target="tpu_custom_call" | custom-call | flops 3000000000 | bytes 9000000 | tf_op jit(solution)/shard_map/pack/pallas_call | solution.py:512
  9.3 2.4 %pack.5 = (bf16[128,1024]{1,0:T(8,128)(2,1)}, bf16[128,1024]{1,0:T(8,128)(2,1)}, bf16[128,1024]{1,0:T(8,128)(2,1)}, bf16[128,1024]{1,0:T(8,128)(2,1)}) custom-call(s32[1]{0:T(128)} %bitcast.member, bf16[128,4096]{1,0:T(8,128)(2,1)} %refs_0_.7), custom_call_target="tpu_custom_call" | custom-call | flops 3000000000 | bytes 9000000 | tf_op jit(solution)/shard_map/pack/pallas_call | solution.py:512
  11.7 0.0 collective-permute-done.refs_3_.refs_7_
  11.7 0.6 collective-permute-done.1.refs_2_.refs_6_
  12.2 0.0 collective-permute-done.2.refs_1_.refs_5_
  12.2 0.8 fusion.2
  13.0 2.4 %collective-permute-start.6 = (bf16[32,512]{1,0:T(8,128)(2,1)S(1)}, bf16[32,512]{1,0:T(8,128)(2,1)S(1)}, u32[]{:S(2)}, u32[]{:S(2)}) collective-permute-start(bf16[32,512]{1,0:T(8,128)(2,1)S(1)} %fusion.2), channel_id=1, source_target_pairs={{0,4},{4,8},{8,12},{12,16},{16,20},{20,24},{24,28},{28,0},{1,5},{5... | collective-permute-start | bytes 98312 | tf_op jit(solution)/shard_map/ppermute | solution.py:847
  15.4 0.0 collective-permute-start.3
  15.4 1.6 %collective-permute-start.4 = (bf16[128,1024]{1,0:T(8,128)(2,1)S(1)}, bf16[128,1024]{1,0:T(8,128)(2,1)S(1)}, u32[]{:S(2)}, u32[]{:S(2)}) collective-permute-start(bf16[128,1024]{1,0:T(8,128)(2,1)S(1)} %copy-done.12), channel_id=1, source_target_pairs={{0,2},{1,3},{2,0},{3,1},{4,6},{5,7},{6,4},{7,5},{8,10},{9,11},{10,... | collective-permute-start | bytes 786440 | tf_op jit(solution)/shard_map/ppermute | solution.py:787
  17.0 0.3 collective-permute-start.5
  17.3 3.1 %collective-permute-done.6.refs_8_.refs_4_ = bf16[32,512]{1,0:T(8,128)(2,1)S(1)} collective-permute-done((bf16[32,512]{1,0:T(8,128)(2,1)S(1)}, bf16[32,512]{1,0:T(8,128)(2,1)S(1)}, u32[]{:S(2)}, u32[]{:S(2)}) %collective-permute-start.6) | collective-permute-done | bytes 32800 | tf_op jit(solution)/shard_map/ppermute | solution.py:847
  20.4 0.0 copy-done.6
  20.4 0.6 copy-done.23
  21.0 10.6 %key_terms.1 = (bf16[4,4,2,128,128]{4,3,2,1,0:T(8,128)(2,1)}, bf16[4,4,128,256]{3,2,1,0:T(8,128)(2,1)}, bf16[4,4,2,128,128]{4,3,2,1,0:T(8,128)(2,1)}, f32[4,4,2,8,128]{4,3,2,1,0:T(8,128)}, bf16[8,128,128]{2,1,0:T(8,128)(2,1)}) custom-call(s32[1]{0:T(128)} %bitcast.member, bf16[144,512]{1,0:T(8,128)(2,1)} %get-tuple-element.69.refs_0_.refs_4_, ...), custom_call_target="tpu_custom_call" | custom-call | flops 12000000000 | bytes 36000000 | tf_op jit(solution)/shard_map/key_terms/pallas_call | solution.py:598
  31.6 0.0 collective-permute-done.3.refs_1_
  31.6 0.0 copy-start.14
  31.7 0.0 collective-permute-done.4.refs_2_
  31.7 0.0 collective-permute-done.5.refs_3_
  31.7 0.7 copy-done.14
  32.4 0.1 copy-done.15
  32.4 0.1 copy-done.16
  32.6 6.2 %value_terms.1 = (bf16[4,4,2,128,256]{4,3,2,1,0:T(8,128)(2,1)}, bf16[4,3,2,128,128]{4,3,2,1,0:T(8,128)(2,1)}, bf16[8,128,256]{2,1,0:T(8,128)(2,1)}) custom-call(s32[1]{0:T(128)} %bitcast.member, bf16[128,1024]{1,0:T(8,128)(2,1)} %get-tuple-element.78.refs_0_, bf16[128,1024]{1,0:T(8,128)(2,1)} %copy-done.14, bf16[128,1024]{1,0:T(8,128)(2,1)} %copy-done.15, ...), custom_call_target="tpu_custom_call" | custom-call | flops 7000000000 | bytes 21000000 | tf_op jit(solution)/shard_map/value_terms/pallas_call | solution.py:626
  38.8 0.1 collective-permute-start.14
  38.9 3.5 %all-to-all-start = ((bf16[8,1,128,256]{3,2,1,0:T(8,128)(2,1)}), bf16[8,1,128,256]{3,2,1,0:T(8,128)(2,1)S(1)}, u32[]{:S(2)}, u32[]{:S(2)}) async-start(bf16[8,1,128,256]{3,2,1,0:T(8,128)(2,1)} %bitcast.10), calls=%async_computation | async-start | bytes 1048576 | tf_op jit(solution)/shard_map/all_to_all | solution.py:807
  42.4 0.5 collective-permute-start.7
  42.9 0.0 copy-done.18
  42.9 1.6 %collective-permute-start.8 = (bf16[128,512]{1,0:T(8,128)(2,1)S(1)}, bf16[128,512]{1,0:T(8,128)(2,1)S(1)}, u32[]{:S(2)}, u32[]{:S(2)}) collective-permute-start(bf16[128,512]{1,0:T(8,128)(2,1)S(1)} %copy-done.18), channel_id=1, source_target_pairs={{0,2},{1,3},{2,0},{3,1},{4,6},{5,7},{6,4},{7,5},{8,10},{9,11},{10,... | collective-permute-start | bytes 393224 | tf_op jit(solution)/shard_map/ppermute | solution.py:787
  44.6 0.0 collective-permute-start.9
  44.6 0.5 collective-permute-start.10
  45.1 1.1 %collective-permute-done.7.refs_1_ = bf16[128,512]{1,0:T(8,128)(2,1)S(1)} collective-permute-done((bf16[128,512]{1,0:T(8,128)(2,1)S(1)}, bf16[128,512]{1,0:T(8,128)(2,1)S(1)}, u32[]{:S(2)}, u32[]{:S(2)}) %collective-permute-start.7) | collective-permute-done | bytes 131104 | tf_op jit(solution)/shard_map/ppermute | solution.py:787
  46.2 1.6 %collective-permute-start.11 = (bf16[128,1024]{1,0:T(8,128)(2,1)S(1)}, bf16[128,1024]{1,0:T(8,128)(2,1)S(1)}, u32[]{:S(2)}, u32[]{:S(2)}) collective-permute-start(bf16[128,1024]{1,0:T(8,128)(2,1)S(1)} %copy-done.9), channel_id=1, source_target_pairs={{0,2},{1,3},{2,0},{3,1},{4,6},{5,7},{6,4},{7,5},{8,10},{9,11},{10,... | collective-permute-start | bytes 786440 | tf_op jit(solution)/shard_map/ppermute | solution.py:787
  47.9 1.4 %collective-permute-done.8.refs_2_ = bf16[128,512]{1,0:T(8,128)(2,1)S(1)} collective-permute-done((bf16[128,512]{1,0:T(8,128)(2,1)S(1)}, bf16[128,512]{1,0:T(8,128)(2,1)S(1)}, u32[]{:S(2)}, u32[]{:S(2)}) %collective-permute-start.8) | collective-permute-done | bytes 131104 | tf_op jit(solution)/shard_map/ppermute | solution.py:787
  49.3 0.0 collective-permute-start.12
  49.3 3.4 %prefix_terms.1 = (bf16[4,4,2,128,128]{4,3,2,1,0:T(8,128)(2,1)}, bf16[4,3,2,128,128]{4,3,2,1,0:T(8,128)(2,1)}) custom-call(bf16[4,4,2,128,128]{4,3,2,1,0:T(8,128)(2,1)} %get-tuple-element.93.refs_6_.t_in, bf16[4,4,128,256]{3,2,1,0:T(8,128)(2,1)} %get-tuple-element.94.refs_7_.kt_in.refs_10_, bf16[4,4,2,128,128]{4,3,2,1,0:T(8,128)(2,1)} %get-tuple-element.95.refs_8_.d_in, ...), custom_call_target="tpu_custom_call" | custom-call | flops 5000000000 | bytes 15000000 | tf_op jit(solution)/shard_map/prefix_terms/pallas_call | solution.py:701
  52.7 0.0 copy-done.21
  52.7 5.1 %all-to-all-done.terms = bf16[8,1,128,256]{3,2,1,0:T(8,128)(2,1)S(1)} async-done(((bf16[8,1,128,256]{3,2,1,0:T(8,128)(2,1)}), bf16[8,1,128,256]{3,2,1,0:T(8,128)(2,1)S(1)}, u32[]{:S(2)}, u32[]{:S(2)}) %all-to-all-start) | async-done | bytes 524320 | tf_op jit(solution)/shard_map/all_to_all | solution.py:807
  57.8 1.8 %handoff.1 = bf16[8,1,128,128]{3,2,1,0:T(8,128)(2,1)} custom-call(bf16[8,1,128,256]{3,2,1,0:T(8,128)(2,1)S(1)} %all-to-all-done.terms), custom_call_target="tpu_custom_call" | custom-call | flops 1000000000 | bytes 3000000 | tf_op jit(solution)/shard_map/handoff/pallas_call | solution.py:684
  59.5 3.6 %all-to-all-start.1 = ((bf16[8,1,128,128]{3,2,1,0:T(8,128)(2,1)}), bf16[8,1,128,128]{3,2,1,0:T(8,128)(2,1)S(1)}, u32[]{:S(2)}, u32[]{:S(2)}) async-start(bf16[8,1,128,128]{3,2,1,0:T(8,128)(2,1)} %handoff.1), calls=%async_computation.1 | async-start | bytes 524288 | tf_op jit(solution)/shard_map/all_to_all | solution.py:812
  63.2 0.0 collective-permute-done.9.refs_3_
  63.2 0.0 collective-permute-done.10.refs_4_
  63.2 0.0 collective-permute-done.11.refs_5_
  63.2 0.0 collective-permute-done.12.refs_5_
  63.2 0.6 copy-done.22
  63.8 7.7 %query_terms.1 = (bf16[8,512,128]{2,1,0:T(8,128)(2,1)}, bf16[8,512,128]{2,1,0:T(8,128)(2,1)}) custom-call(s32[1]{0:T(128)} %bitcast.member, bf16[128,512]{1,0:T(8,128)(2,1)} %get-tuple-element.104.refs_0_, bf16[128,512]{1,0:T(8,128)(2,1)} %copy-done.20, bf16[128,512]{1,0:T(8,128)(2,1)} %copy-done.21, bf16[128,512]{1,0:T(8,128)(2,1)} %copy-done.22, ...), custom_call_target="tpu_custom_call" | custom-call | flops 8999999488 | bytes 27000000 | tf_op jit(solution)/shard_map/query_terms/pallas_call | solution.py:663
  71.6 0.7 all-to-all-done.1
  72.3 1.2 %copy-done = bf16[8,512,128]{2,1,0:T(8,128)(2,1)S(1)} copy-done((bf16[8,512,128]{2,1,0:T(8,128)(2,1)S(1)}, bf16[8,512,128]{2,1,0:T(8,128)(2,1)}, u32[]{:S(2)}) %copy-start) | copy-done | bytes 1048600
  73.5 1.2 %copy-done.1 = bf16[8,512,128]{2,1,0:T(8,128)(2,1)S(1)} copy-done((bf16[8,512,128]{2,1,0:T(8,128)(2,1)S(1)}, bf16[8,512,128]{2,1,0:T(8,128)(2,1)}, u32[]{:S(2)}) %copy-start.1) | copy-done | bytes 1048600
  74.8 0.8 normed_rows.3
  75.6 0.1 collective-permute-start.13
  75.7 0.8 normed_rows.2.mine
  76.5 1.1 %collective-permute-done.13.theirs = bf16[2,128,1024]{2,1,0:T(8,128)(2,1)S(1)} collective-permute-done((bf16[2,128,1024]{2,1,0:T(8,128)(2,1)S(1)}, bf16[2,128,1024]{2,1,0:T(8,128)(2,1)S(1)}, u32[]{:S(2)}, u32[]{:S(2)}) %collective-permute-start.13) | collective-permute-done | bytes 524320 | tf_op jit(solution)/shard_map/ppermute | solution.py:865
  77.6 0.0 collective-permute-done.14.other_weight
  77.6 2.8 %projected.3 = (f32[128,1024]{1,0:T(8,128)S(1)}, bf16[128,1024]{1,0:T(8,128)(2,1)S(1)}) custom-call(bf16[2,128,1024]{2,1,0:T(8,128)(2,1)S(1)} %normed_rows.2.mine, bf16[2,128,1024]{2,1,0:T(8,128)(2,1)S(1)} %collective-permute-done.13.theirs, bf16[1024,2048]{1,0:T(8,128)(2,1)S(1)} %copy-done.4, bf16[1024,2048]{1,0:T(8,128)(2,1)} %collective-permute-done.14.other_weight), custom_call_target="tpu_custom_call" | custom-call | flops 3000000000 | bytes 9000000 | tf_op jit(solution)/shard_map/projected/pallas_call | solution.py:750
  80.4 1.7 %collective-permute-start.16 = (bf16[128,1024]{1,0:T(8,128)(2,1)S(1)}, bf16[128,1024]{1,0:T(8,128)(2,1)S(1)}, u32[]{:S(2)}, u32[]{:S(2)}) collective-permute-start(bf16[128,1024]{1,0:T(8,128)(2,1)S(1)} %get-tuple-element.118), channel_id=1, source_target_pairs={{0,2},{1,3},{2,0},{3,1},{4,6},{5,7},{6,4},{7,5},{8,10},{9,11},{10,... | collective-permute-start | bytes 786440 | tf_op jit(solution)/shard_map/ppermute | solution.py:876
  82.1 2.8 %projected.2 = (f32[128,1024]{1,0:T(8,128)S(1)}, bf16[128,1024]{1,0:T(8,128)(2,1)S(1)}) custom-call(bf16[2,128,1024]{2,1,0:T(8,128)(2,1)S(1)} %normed_rows.2.mine, bf16[2,128,1024]{2,1,0:T(8,128)(2,1)S(1)} %collective-permute-done.13.theirs, bf16[1024,2048]{1,0:T(8,128)(2,1)S(1)} %copy-done.4, bf16[1024,2048]{1,0:T(8,128)(2,1)} %collective-permute-done.14.other_weight), custom_call_target="tpu_custom_call" | custom-call | flops 3000000000 | bytes 9000000 | tf_op jit(solution)/shard_map/projected/pallas_call | solution.py:750
  84.9 0.4 collective-permute-start.15
  85.3 4.3 %collective-permute-done.16.refs_3_ = bf16[128,1024]{1,0:T(8,128)(2,1)S(1)} collective-permute-done((bf16[128,1024]{1,0:T(8,128)(2,1)S(1)}, bf16[128,1024]{1,0:T(8,128)(2,1)S(1)}, u32[]{:S(2)}, u32[]{:S(2)}) %collective-permute-start.16) | collective-permute-done | bytes 262176 | tf_op jit(solution)/shard_map/ppermute | solution.py:876
  89.6 4.8 %collective-permute-done.15.refs_1_ = bf16[128,1024]{1,0:T(8,128)(2,1)S(1)} collective-permute-done((bf16[128,1024]{1,0:T(8,128)(2,1)S(1)}, bf16[128,1024]{1,0:T(8,128)(2,1)S(1)}, u32[]{:S(2)}, u32[]{:S(2)}) %collective-permute-start.15) | collective-permute-done | bytes 262176 | tf_op jit(solution)/shard_map/ppermute | solution.py:876
  94.4 0.9 summed_parts.1
  (37 shorter events, 0.1 us)
Async XLA Ops:
  2.1 9.6 %collective-permute-start = (bf16[144,512]{1,0:T(8,128)(2,1)}, bf16[144,512]{1,0:T(8,128)(2,1)S(1)}, u32[]{:S(2)}, u32[]{:S(2)}) collective-permute-start(bf16[144,512]{1,0:T(8,128)(2,1)} %get-tuple-element.66), channel_id=1, source_target_pairs={{0,3},{1,2},{2,1},{3,0},{4,7},{5,6},{6,5},{7,4},{8,11},{9,10},{10,... | collective-permute-start | bytes 442376 | tf_op jit(solution)/shard_map/ppermute | solution.py:787
  4.5 7.8 %collective-permute-start.1 = (bf16[144,512]{1,0:T(8,128)(2,1)}, bf16[144,512]{1,0:T(8,128)(2,1)S(1)}, u32[]{:S(2)}, u32[]{:S(2)}) collective-permute-start(bf16[144,512]{1,0:T(8,128)(2,1)} %get-tuple-element.67), channel_id=1, source_target_pairs={{0,2},{1,3},{2,0},{3,1},{4,6},{5,7},{6,4},{7,5},{8,10},{9,11},{10,... | collective-permute-start | bytes 442376 | tf_op jit(solution)/shard_map/ppermute | solution.py:787
  5.1 7.2 %collective-permute-start.2 = (bf16[144,512]{1,0:T(8,128)(2,1)}, bf16[144,512]{1,0:T(8,128)(2,1)S(1)}, u32[]{:S(2)}, u32[]{:S(2)}) collective-permute-start(bf16[144,512]{1,0:T(8,128)(2,1)} %get-tuple-element.68), channel_id=1, source_target_pairs={{0,1},{1,0},{2,3},{3,2},{4,5},{5,4},{6,7},{7,6},{8,9},{9,8},{10,11... | collective-permute-start | bytes 442376 | tf_op jit(solution)/shard_map/ppermute | solution.py:787
  9.3 6.1 %copy-start.13 = (bf16[128,1024]{1,0:T(8,128)(2,1)S(1)}, bf16[128,1024]{1,0:T(8,128)(2,1)}, u32[]{:S(2)}) copy-start(bf16[128,1024]{1,0:T(8,128)(2,1)} %get-tuple-element.79) | copy-start | bytes 786436
  9.3 6.1 %copy-start.12 = (bf16[128,1024]{1,0:T(8,128)(2,1)S(1)}, bf16[128,1024]{1,0:T(8,128)(2,1)}, u32[]{:S(2)}) copy-start(bf16[128,1024]{1,0:T(8,128)(2,1)} %get-tuple-element.80) | copy-start | bytes 786436
  9.3 7.7 %copy-start.11 = (bf16[128,1024]{1,0:T(8,128)(2,1)S(1)}, bf16[128,1024]{1,0:T(8,128)(2,1)}, u32[]{:S(2)}) copy-start(bf16[128,1024]{1,0:T(8,128)(2,1)} %get-tuple-element.81) | copy-start | bytes 786436
  11.7 8.7 %copy-start.5 = (bf16[144,512]{1,0:T(8,128)(2,1)}, bf16[144,512]{1,0:T(8,128)(2,1)S(1)}, u32[]{:S(2)}) copy-start(bf16[144,512]{1,0:T(8,128)(2,1)S(1)} %collective-permute-done.refs_3_.refs_7_) | copy-start | bytes 442372
  12.2 8.1 %copy-start.6 = (bf16[144,512]{1,0:T(8,128)(2,1)}, bf16[144,512]{1,0:T(8,128)(2,1)S(1)}, u32[]{:S(2)}) copy-start(bf16[144,512]{1,0:T(8,128)(2,1)S(1)} %collective-permute-done.1.refs_2_.refs_6_) | copy-start | bytes 442372
  12.2 8.1 %copy-start.7 = (bf16[144,512]{1,0:T(8,128)(2,1)}, bf16[144,512]{1,0:T(8,128)(2,1)S(1)}, u32[]{:S(2)}) copy-start(bf16[144,512]{1,0:T(8,128)(2,1)S(1)} %collective-permute-done.2.refs_1_.refs_5_) | copy-start | bytes 442372
  13.0 7.3 %collective-permute-start.6 = (bf16[32,512]{1,0:T(8,128)(2,1)S(1)}, bf16[32,512]{1,0:T(8,128)(2,1)S(1)}, u32[]{:S(2)}, u32[]{:S(2)}) collective-permute-start(bf16[32,512]{1,0:T(8,128)(2,1)S(1)} %fusion.2), channel_id=1, source_target_pairs={{0,4},{4,8},{8,12},{12,16},{16,20},{20,24},{24,28},{28,0},{1,5},{5... | collective-permute-start | bytes 98312 | tf_op jit(solution)/shard_map/ppermute | solution.py:847
  15.4 16.2 %collective-permute-start.3 = (bf16[128,1024]{1,0:T(8,128)(2,1)S(1)}, bf16[128,1024]{1,0:T(8,128)(2,1)S(1)}, u32[]{:S(2)}, u32[]{:S(2)}) collective-permute-start(bf16[128,1024]{1,0:T(8,128)(2,1)S(1)} %copy-done.13), channel_id=1, source_target_pairs={{0,1},{1,0},{2,3},{3,2},{4,5},{5,4},{6,7},{7,6},{8,9},{9,8},{10,11... | collective-permute-start | bytes 786440 | tf_op jit(solution)/shard_map/ppermute | solution.py:787
  15.4 16.2 %collective-permute-start.4 = (bf16[128,1024]{1,0:T(8,128)(2,1)S(1)}, bf16[128,1024]{1,0:T(8,128)(2,1)S(1)}, u32[]{:S(2)}, u32[]{:S(2)}) collective-permute-start(bf16[128,1024]{1,0:T(8,128)(2,1)S(1)} %copy-done.12), channel_id=1, source_target_pairs={{0,2},{1,3},{2,0},{3,1},{4,6},{5,7},{6,4},{7,5},{8,10},{9,11},{10,... | collective-permute-start | bytes 786440 | tf_op jit(solution)/shard_map/ppermute | solution.py:787
  17.0 14.7 %collective-permute-start.5 = (bf16[128,1024]{1,0:T(8,128)(2,1)S(1)}, bf16[128,1024]{1,0:T(8,128)(2,1)S(1)}, u32[]{:S(2)}, u32[]{:S(2)}) collective-permute-start(bf16[128,1024]{1,0:T(8,128)(2,1)S(1)} %copy-done.11), channel_id=1, source_target_pairs={{0,3},{1,2},{2,1},{3,0},{4,7},{5,6},{6,5},{7,4},{8,11},{9,10},{10,... | collective-permute-start | bytes 786440 | tf_op jit(solution)/shard_map/ppermute | solution.py:787
  20.4 0.6 copy-start.23
  31.6 0.7 copy-start.14
  31.7 0.8 copy-start.15
  31.7 0.9 copy-start.16
  32.5 9.8 %copy-start.19 = (bf16[128,512]{1,0:T(8,128)(2,1)S(1)}, bf16[128,512]{1,0:T(8,128)(2,1)}, u32[]{:S(2)}) copy-start(bf16[128,512]{1,0:T(8,128)(2,1)} %get-tuple-element.90) | copy-start | bytes 393220
  32.5 10.4 %copy-start.18 = (bf16[128,512]{1,0:T(8,128)(2,1)S(1)}, bf16[128,512]{1,0:T(8,128)(2,1)}, u32[]{:S(2)}) copy-start(bf16[128,512]{1,0:T(8,128)(2,1)} %get-tuple-element.91) | copy-start | bytes 393220
  32.5 12.1 %copy-start.17 = (bf16[128,512]{1,0:T(8,128)(2,1)S(1)}, bf16[128,512]{1,0:T(8,128)(2,1)}, u32[]{:S(2)}) copy-start(bf16[128,512]{1,0:T(8,128)(2,1)} %get-tuple-element.92) | copy-start | bytes 393220
  32.5 12.1 %copy-start.10 = (bf16[128,1024]{1,0:T(8,128)(2,1)S(1)}, bf16[128,1024]{1,0:T(8,128)(2,1)}, u32[]{:S(2)}) copy-start(bf16[128,1024]{1,0:T(8,128)(2,1)} %get-tuple-element.101) | copy-start | bytes 786436
  32.5 13.7 %copy-start.9 = (bf16[128,1024]{1,0:T(8,128)(2,1)S(1)}, bf16[128,1024]{1,0:T(8,128)(2,1)}, u32[]{:S(2)}) copy-start(bf16[128,1024]{1,0:T(8,128)(2,1)} %get-tuple-element.102) | copy-start | bytes 786436
  32.6 16.7 %copy-start.8 = (bf16[128,1024]{1,0:T(8,128)(2,1)S(1)}, bf16[128,1024]{1,0:T(8,128)(2,1)}, u32[]{:S(2)}) copy-start(bf16[128,1024]{1,0:T(8,128)(2,1)} %get-tuple-element.103) | copy-start | bytes 786436
  38.8 38.8 %collective-permute-start.14 = (bf16[1024,2048]{1,0:T(8,128)(2,1)}, bf16[1024,2048]{1,0:T(8,128)(2,1)}, u32[]{:S(2)}, u32[]{:S(2)}) collective-permute-start(bf16[1024,2048]{1,0:T(8,128)(2,1)} %own_weight.3), channel_id=1, source_target_pairs={{0,1},{1,0},{2,3},{3,2},{4,5},{5,4},{6,7},{7,6},{8,9},{9,8},{10,11... | collective-permute-start | bytes 12582920 | tf_op jit(solution)/shard_map/ppermute | solution.py:855
  38.9 18.9 %all-to-all-start = ((bf16[8,1,128,256]{3,2,1,0:T(8,128)(2,1)}), bf16[8,1,128,256]{3,2,1,0:T(8,128)(2,1)S(1)}, u32[]{:S(2)}, u32[]{:S(2)}) async-start(bf16[8,1,128,256]{3,2,1,0:T(8,128)(2,1)} %bitcast.10), calls=%async_computation | async-start | bytes 1048576 | tf_op jit(solution)/shard_map/all_to_all | solution.py:807
  42.4 3.8 %collective-permute-start.7 = (bf16[128,512]{1,0:T(8,128)(2,1)S(1)}, bf16[128,512]{1,0:T(8,128)(2,1)S(1)}, u32[]{:S(2)}, u32[]{:S(2)}) collective-permute-start(bf16[128,512]{1,0:T(8,128)(2,1)S(1)} %copy-done.19), channel_id=1, source_target_pairs={{0,1},{1,0},{2,3},{3,2},{4,5},{5,4},{6,7},{7,6},{8,9},{9,8},{10,11... | collective-permute-start | bytes 393224 | tf_op jit(solution)/shard_map/ppermute | solution.py:787
  42.9 6.3 %collective-permute-start.8 = (bf16[128,512]{1,0:T(8,128)(2,1)S(1)}, bf16[128,512]{1,0:T(8,128)(2,1)S(1)}, u32[]{:S(2)}, u32[]{:S(2)}) collective-permute-start(bf16[128,512]{1,0:T(8,128)(2,1)S(1)} %copy-done.18), channel_id=1, source_target_pairs={{0,2},{1,3},{2,0},{3,1},{4,6},{5,7},{6,4},{7,5},{8,10},{9,11},{10,... | collective-permute-start | bytes 393224 | tf_op jit(solution)/shard_map/ppermute | solution.py:787
  44.6 18.6 %collective-permute-start.9 = (bf16[128,512]{1,0:T(8,128)(2,1)S(1)}, bf16[128,512]{1,0:T(8,128)(2,1)S(1)}, u32[]{:S(2)}, u32[]{:S(2)}) collective-permute-start(bf16[128,512]{1,0:T(8,128)(2,1)S(1)} %copy-done.17), channel_id=1, source_target_pairs={{0,3},{1,2},{2,1},{3,0},{4,7},{5,6},{6,5},{7,4},{8,11},{9,10},{10,... | collective-permute-start | bytes 393224 | tf_op jit(solution)/shard_map/ppermute | solution.py:787
  44.6 18.6 %collective-permute-start.10 = (bf16[128,1024]{1,0:T(8,128)(2,1)S(1)}, bf16[128,1024]{1,0:T(8,128)(2,1)S(1)}, u32[]{:S(2)}, u32[]{:S(2)}) collective-permute-start(bf16[128,1024]{1,0:T(8,128)(2,1)S(1)} %copy-done.10), channel_id=1, source_target_pairs={{0,1},{1,0},{2,3},{3,2},{4,5},{5,4},{6,7},{7,6},{8,9},{9,8},{10,11... | collective-permute-start | bytes 786440 | tf_op jit(solution)/shard_map/ppermute | solution.py:787
  46.2 6.5 %copy-start.20 = (bf16[128,512]{1,0:T(8,128)(2,1)}, bf16[128,512]{1,0:T(8,128)(2,1)S(1)}, u32[]{:S(2)}) copy-start(bf16[128,512]{1,0:T(8,128)(2,1)S(1)} %collective-permute-done.7.refs_1_) | copy-start | bytes 393220
  46.2 17.0 %collective-permute-start.11 = (bf16[128,1024]{1,0:T(8,128)(2,1)S(1)}, bf16[128,1024]{1,0:T(8,128)(2,1)S(1)}, u32[]{:S(2)}, u32[]{:S(2)}) collective-permute-start(bf16[128,1024]{1,0:T(8,128)(2,1)S(1)} %copy-done.9), channel_id=1, source_target_pairs={{0,2},{1,3},{2,0},{3,1},{4,6},{5,7},{6,4},{7,5},{8,10},{9,11},{10,... | collective-permute-start | bytes 786440 | tf_op jit(solution)/shard_map/ppermute | solution.py:787
  49.3 3.4 %copy-start.21 = (bf16[128,512]{1,0:T(8,128)(2,1)}, bf16[128,512]{1,0:T(8,128)(2,1)S(1)}, u32[]{:S(2)}) copy-start(bf16[128,512]{1,0:T(8,128)(2,1)S(1)} %collective-permute-done.8.refs_2_) | copy-start | bytes 393220
  49.3 13.9 %collective-permute-start.12 = (bf16[128,1024]{1,0:T(8,128)(2,1)S(1)}, bf16[128,1024]{1,0:T(8,128)(2,1)S(1)}, u32[]{:S(2)}, u32[]{:S(2)}) collective-permute-start(bf16[128,1024]{1,0:T(8,128)(2,1)S(1)} %copy-done.8), channel_id=1, source_target_pairs={{0,3},{1,2},{2,1},{3,0},{4,7},{5,6},{6,5},{7,4},{8,11},{9,10},{10,... | collective-permute-start | bytes 786440 | tf_op jit(solution)/shard_map/ppermute | solution.py:787
  59.5 12.8 %all-to-all-start.1 = ((bf16[8,1,128,128]{3,2,1,0:T(8,128)(2,1)}), bf16[8,1,128,128]{3,2,1,0:T(8,128)(2,1)S(1)}, u32[]{:S(2)}, u32[]{:S(2)}) async-start(bf16[8,1,128,128]{3,2,1,0:T(8,128)(2,1)} %handoff.1), calls=%async_computation.1 | async-start | bytes 524288 | tf_op jit(solution)/shard_map/all_to_all | solution.py:812
  63.2 0.7 copy-start.22
  63.8 8.5 %copy-start.3 = (f32[128]{0:T(128)S(1)}, f32[128]{0:T(128)}, u32[]{:S(2)}) copy-start(f32[128]{0:T(128)} %param.20) | copy-start | bytes 1540
  63.8 11.8 %copy-start.2 = (bf16[128,1024]{1,0:T(8,128)(2,1)S(1)}, bf16[128,1024]{1,0:T(8,128)(2,1)}, u32[]{:S(2)}) copy-start(bf16[128,1024]{1,0:T(8,128)(2,1)} %get-tuple-element.100.refs_4_) | copy-start | bytes 786436
  72.3 1.2 %copy-start = (bf16[8,512,128]{2,1,0:T(8,128)(2,1)S(1)}, bf16[8,512,128]{2,1,0:T(8,128)(2,1)}, u32[]{:S(2)}) copy-start(bf16[8,512,128]{2,1,0:T(8,128)(2,1)} %get-tuple-element.112.refs_0_.refs_1_) | copy-start | bytes 3145732
  73.5 1.2 %copy-start.1 = (bf16[8,512,128]{2,1,0:T(8,128)(2,1)S(1)}, bf16[8,512,128]{2,1,0:T(8,128)(2,1)}, u32[]{:S(2)}) copy-start(bf16[8,512,128]{2,1,0:T(8,128)(2,1)} %get-tuple-element.113.refs_2_.refs_3_) | copy-start | bytes 3145732
  74.8 2.8 %copy-start.4 = (bf16[1024,2048]{1,0:T(8,128)(2,1)S(1)}, bf16[1024,2048]{1,0:T(8,128)(2,1)}, u32[]{:S(2)}) copy-start(bf16[1024,2048]{1,0:T(8,128)(2,1)} %own_weight.3) | copy-start | bytes 12582916
  75.6 2.0 %collective-permute-start.13 = (bf16[2,128,1024]{2,1,0:T(8,128)(2,1)S(1)}, bf16[2,128,1024]{2,1,0:T(8,128)(2,1)S(1)}, u32[]{:S(2)}, u32[]{:S(2)}) collective-permute-start(bf16[2,128,1024]{2,1,0:T(8,128)(2,1)S(1)} %normed_rows.3), channel_id=1, source_target_pairs={{0,1},{1,0},{2,3},{3,2},{4,5},{5,4},{6,7},{7,6},{8,9},{9,8},{10,11... | collective-permute-start | bytes 1572872 | tf_op jit(solution)/shard_map/ppermute | solution.py:865
  80.4 9.2 %collective-permute-start.16 = (bf16[128,1024]{1,0:T(8,128)(2,1)S(1)}, bf16[128,1024]{1,0:T(8,128)(2,1)S(1)}, u32[]{:S(2)}, u32[]{:S(2)}) collective-permute-start(bf16[128,1024]{1,0:T(8,128)(2,1)S(1)} %get-tuple-element.118), channel_id=1, source_target_pairs={{0,2},{1,3},{2,0},{3,1},{4,6},{5,7},{6,4},{7,5},{8,10},{9,11},{10,... | collective-permute-start | bytes 786440 | tf_op jit(solution)/shard_map/ppermute | solution.py:876
  84.9 9.5 %collective-permute-start.15 = (bf16[128,1024]{1,0:T(8,128)(2,1)S(1)}, bf16[128,1024]{1,0:T(8,128)(2,1)S(1)}, u32[]{:S(2)}, u32[]{:S(2)}) collective-permute-start(bf16[128,1024]{1,0:T(8,128)(2,1)S(1)} %get-tuple-element.116), channel_id=1, source_target_pairs={{0,2},{1,3},{2,0},{3,1},{4,6},{5,7},{6,4},{7,5},{8,10},{9,11},{10,... | collective-permute-start | bytes 786440 | tf_op jit(solution)/shard_map/ppermute | solution.py:876

commit v5 on v4

--- a/solution.py
+++ b/solution.py
@@ -100,19 +100,23 @@
     return picked[:, : count * CH], picked[:, count * CH :].astype(bf16)
 
 
-def decay_terms(rates, count):
+def decay_terms(rates, count, with_growth=True):
     row, column = grids()
     below = ones_where(column <= row)
     pieces = []
     for e in range(count):
         rate = rates[:, e * CH : (e + 1) * CH]
-        pieces += [jnp.where(row > column, rate, jnp.zeros_like(rate)), rate]
+        pieces.append(jnp.where(row > column, rate, jnp.zeros_like(rate)))
+    if with_growth:
+        pieces.append(rates)
     sums = jnp.dot(below, jnp.concatenate(pieces, axis=1), preferred_element_type=f32)
     ratios, growth = [], []
     for e in range(count):
-        at = 2 * e * CH
+        at = e * CH
         ratios.append(jnp.where(column <= row, jnp.exp(sums[:, at : at + CH]), 0.0))
-        growth.append(jnp.exp(sums[:, at + CH : at + 2 * CH]))
+        if with_growth:
+            at += count * CH
+            growth.append(jnp.exp(sums[:, at : at + CH]))
     return ratios, growth
 
 
@@ -199,7 +203,7 @@
 
     strengths, rates = strengths_and_rates(gates[...], first, count, heads)
     unit = [unit_rows(filtered[:, k * DK : (k + 1) * DK]) for k in range(here)]
-    decays = [decay_terms(chunk_of(rates, c), count) for c in range(blocks)]
+    ratio = [decay_terms(chunk_of(rates, c), count, False)[0] for c in range(blocks)]
     keys = {(c, k): chunk_of(unit[k], c) for c, k in groups}
     turned = {g: jnp.transpose(keys[g]) for g in groups}
     sides = {g: split(turned[g]) for g in groups}
@@ -222,25 +226,32 @@
         )
         for c in range(blocks)
     ]
-    lower, ktail = {}, {}
+    lower, ktail, ends = {}, {}, {}
     for c, k in groups:
         kt_out[k, c] = jnp.concatenate(sides[c, k], axis=1)
     for c, e in problems:
-        ratios, growth = decays[c][0][e], decays[c][1][e]
+        ratios = ratio[c][e]
         strength = chunk_of(strengths, c)[:, e * CH : (e + 1) * CH]
         k = e // SHARE
         lower[c, e] = jnp.where(column < row, strength * kk[c, k] * ratios, 0.0)
         ktail[c, e] = (turned[c, k] * ratios[CH - 1 : CH]).astype(bf16)
+        growth = growing[c][count + e : count + e + 1]
+        ends[c, e] = jnp.broadcast_to(growth[:, CH - 1 : CH], (1, CH))
         rows_out[k, c, e % SHARE] = jnp.concatenate(
-            [ratios[CH - 1 : CH], growing[c][count + e : count + e + 1], growth[CH - 6 : CH]],
-            axis=0,
+            [ratios[CH - 1 : CH], growth] + [ends[c, e]] * 6, axis=0
         )
     inverse = unit_lower_inverses(lower)
-    solving = {(c, e): as_left(inverse[c, e] * across[c][e : e + 1]) for c, e in problems}
+    solving = {
+        (c, e): (inverse[c, e] * across[c][e : e + 1]).astype(bf16) for c, e in problems
+    }
+    rounded = {g: keys[g].astype(bf16) for g in groups}
     solved = {
         (c, e): jnp.dot(
-            solving[c, e][:, :CH],
-            (decays[c][1][e] * keys[c, e // SHARE]).astype(bf16),
+            (
+                inverse[c, e]
+                * (across[c][e : e + 1] * growing[c][count + e : count + e + 1])
+            ).astype(bf16),
+            rounded[c, e // SHARE],
             preferred_element_type=f32,
         ).astype(bf16)
         for c, e in problems
@@ -251,14 +262,14 @@
     }
     for c, e in problems:
         k = e // SHARE
-        t_out[k, c, e % SHARE] = solving[c, e][:, :CH]
+        t_out[k, c, e % SHARE] = solving[c, e]
         d_out[k, c, e % SHARE] = maps[c, e]
     running = [
-        decays[0][1][e][CH - 1 : CH] * eye - maps[0, e].astype(f32) for e in range(count)
+        ends[0, e] * eye - maps[0, e].astype(f32) for e in range(count)
     ]
     for c in range(1, blocks):
         running = [
-            decays[c][1][e][CH - 1 : CH] * running[e]
+            ends[c, e] * running[e]
             - jnp.dot(maps[c, e], running[e].astype(bf16), preferred_element_type=f32)
             for e in range(count)
         ]
@@ -371,7 +382,7 @@
 def query_kernel(groups_count, heads, member, *refs):
     pieces, refs = refs[:groups_count], refs[groups_count:]
     gate_pieces, refs = refs[:groups_count], refs[groups_count:]
-    edge, taps, kt_in, w_in, p_in, u_in, z_in, f_out, g_out, padded, gates = refs
+    edge, taps, kt_in, w_in, p_in, u_in, z_in, out, padded, gates = refs
     here = pieces[0].shape[1] // DK
     count = here * SHARE
     blocks = gates.shape[0] // CH
@@ -405,16 +416,14 @@
     for c, e in problems:
         here = slice(c * CH, (c + 1) * CH)
         if c == 0:
-            f_out[e, here] = entry[c, e][:, :DK]
-            g_out[e, here] = local[c, e].astype(bf16)
+            out[e, here, :DK] = entry[c, e][:, :DK]
+            out[e, here, DK:] = local[c, e].astype(bf16)
         else:
-            f_out[e, here] = jnp.dot(
+            out[e, here, :DK] = jnp.dot(
                 entry[c, e], at(p_in, c - 1, e), preferred_element_type=f32
             ).astype(bf16)
-            total = local[c, e] + jnp.dot(
-                entry[c, e], at(z_in, c - 1, e), preferred_element_type=f32
-            )
-            g_out[e, here] = total.astype(bf16)
+            later = jnp.dot(entry[c, e], at(z_in, c - 1, e), preferred_element_type=f32)
+            out[e, here, DK:] = (local[c, e] + later).astype(bf16)
 
 
 def handoff_kernel(terms, out):
@@ -435,14 +444,13 @@
 
 
 def norm_kernel(count, member, *refs):
-    f_in, refs = refs[:count], refs[count:]
-    g_in, refs = refs[:count], refs[count:]
+    terms, refs = refs[:count], refs[count:]
     gate, refs = refs[:count], refs[count:]
     state, gain, out = refs
     cells = [(i, h) for i in range(count) for h in range(state.shape[0])]
     core = {
-        (i, h): g_in[i][h].astype(f32)
-        + jnp.dot(f_in[i][h], state[h], preferred_element_type=f32)
+        (i, h): terms[i][h, :, DK:].astype(f32)
+        + jnp.dot(terms[i][h, :, :DK], state[h], preferred_element_type=f32)
         for i, h in cells
     }
     scale = {
@@ -659,7 +667,7 @@
     tokens = groups * own
     key_heads = kt.shape[0]
     each = heads_at_once(key_heads, QUERY_STEP)
-    out = pl.BlockSpec((each * SHARE, tokens, DK), lambda p, me: (p, 0, 0))
+    out = pl.BlockSpec((each * SHARE, tokens, DK + DV), lambda p, me: (p, 0, 0))
     return pl.pallas_call(
         functools.partial(query_kernel, groups, key_heads * SHARE),
         grid_spec=grid_of(
@@ -669,10 +677,10 @@
             + [pl.BlockSpec((EDGE, each * DK), lambda p, me: (1, p))]
             + [columns_of(taps.shape[0], each * DK)]
             + [per_head(each, x.shape[1:]) for x in (kt, w, p, u, z)],
-            [out, out],
+            out,
             [pltpu.VMEM((tokens + 8, each * DK), f32), pltpu.VMEM((tokens, 128), bf16)],
         ),
-        out_shape=[shape((key_heads * SHARE, tokens, DK), bf16)] * 2,
+        out_shape=shape((key_heads * SHARE, tokens, DK + DV), bf16),
         compiler_params=params(),
         cost_estimate=cost(9),
         name="query_terms",
@@ -710,14 +718,14 @@
     )(t, kt, d, rows)
 
 
-def normed_rows(member, f, g, state, gate, gain, parity):
+def normed_rows(member, terms, state, gate, gain, parity):
     heads = state.shape[0]
     count = len(gate)
     size, width = gate[0].shape
 
     def token_block(i):
         return pl.BlockSpec(
-            (heads, size, DK), lambda p, me: (0, me[0] ^ (2 * i + parity), 0)
+            (heads, size, DK + DV), lambda p, me: (0, me[0] ^ (2 * i + parity), 0)
         )
 
     whole = pl.BlockSpec((size, width), lambda p, me: (0, 0))
@@ -725,7 +733,7 @@
         functools.partial(norm_kernel, count),
         grid_spec=grid_of(
             1,
-            [token_block(i) for i in range(count)] * 2
+            [token_block(i) for i in range(count)]
             + [whole] * count
             + [
                 pl.BlockSpec((heads, DK, DV), lambda p, me: (0, 0, 0)),
@@ -738,7 +746,7 @@
         compiler_params=params(16),
         cost_estimate=cost(1),
         name="normed_rows",
-    )(member, *([f] * count), *([g] * count), *gate, state, gain)
+    )(member, *([terms] * count), *gate, state, gain)
 
 
 def projected(mine, theirs, own_weight, other_weight, start, width):
@@ -857,13 +865,13 @@
     adds, w, p = after_all([to_runners(adds), w, p], [])
     entries = handoff(adds)
     query_rows = after_all(query_rows, [entries, *gate_rows])
-    f, g = query_terms(member, query_rows, edge, packed, filter_query, kt, w, p, u, z)
+    terms = query_terms(member, query_rows, edge, packed, filter_query, kt, w, p, u, z)
     state = from_runners(entries, heads)
 
     gain = norm_gain.reshape(1, DV)
-    theirs = normed_rows(member, f, g, state, gate_rows[1::2], gain, 1)
+    theirs = normed_rows(member, terms, state, gate_rows[1::2], gain, 1)
     theirs = lax.ppermute(theirs, "head", swap)
-    mine = normed_rows(member, f, g, state, gate_rows[0::2], gain, 0)
+    mine = normed_rows(member, terms, state, gate_rows[0::2], gain, 0)
     width = out_weight.shape[1]
     cuts = 2
     parts = []

time: 96 us -> 95.2 us (level)
    unnamed x48 -> x46, local copies, waits for them, and re-layouts: 4.59 us -> 3.72 us
  transfers between devices with their start and end apart: 19 -> 19, of which waited for: 9 -> 9; matrix products, arithmetic and copies ran while one was open for 0% -> 0% of each run, Pallas kernels for 36% -> 37%
where the time goes in v5:
time: 95.2 us; the launch traced here: 94.5 us
  Pallas kernels  46.5 us (49%)
  waiting for transfers between devices  22.2 us (23%)
  starting transfers between devices  21 us (22%)
  local copies, waits for them, and re-layouts  3.72 us (4%)
    pallas_call x1, Pallas kernels, key_terms(): pl.pallas_call(functools.partial(key_kernel, groups, key_heads * SHARE),...  10.7 us
    ppermute x12, starting transfers between devices, to_members(): lax.ppermute(pieces[d], 'head', [(i, i ^ d) for i in range(groups)])  9.23 us
    ppermute x2, waiting for transfers between devices, on_device(): lax.ppermute(part, 'head', [(i, i ^ 2 * step + 2) for i in range(groups)])  9.09 us
    pallas_call x1, Pallas kernels, query_terms(): pl.pallas_call(functools.partial(query_kernel, groups, key_heads * SHARE)...  7.76 us
    pallas_call x3, Pallas kernels, pack(): pl.pallas_call(functools.partial(pack_kernel, groups), grid_spec=grid_of(...  6.49 us
    pallas_call x1, Pallas kernels, value_terms(): pl.pallas_call(functools.partial(value_kernel, groups), grid_spec=grid_of...  6.22 us
    pallas_call x2, Pallas kernels, projected(): pl.pallas_call(project_kernel, grid=(width // tile,), in_specs=[whole, wh...  5.56 us
    all_to_all x1, waiting for transfers between devices, to_runners(): return lax.all_to_all(pieces, 'seq', 0, 0)  5.06 us
  transfers between devices with their start and end apart: 19, of which 9 were waited for; matrix products, arithmetic and copies ran while one was open for 0% of the time, Pallas kernels for 37%

profile of v5, /device:TPU:0, one launch (start us, length us, event | category | flops | bytes accessed | tf_op | source)
XLA Modules:
  0.0 94.5 jit_solution(15759375238612362234)
XLA Ops:
  0.0 2.1 %pack_keys.1 = (bf16[144,512]{1,0:T(8,128)(2,1)}, bf16[144,512]{1,0:T(8,128)(2,1)}, bf16[144,512]{1,0:T(8,128)(2,1)}, bf16[144,512]{1,0:T(8,128)(2,1)}) custom-call(s32[1]{0:T(128)} %bitcast.member, bf16[128,2048]{1,0:T(8,128)(2,1)} %refs_0_.5, bf16[128,4096]{1,0:T(8,128)(2,1)} %refs_0_.6, bf16[128,2048]{1,0:T(8,128)(2,1)} %refs_2_.1, ...), custom_call_target="tpu_custom_call" | custom-call | flops 3000000000 | bytes 9000000 | tf_op jit(solution)/shard_map/pack_keys/pallas_call | solution.py:545
  2.1 2.4 %collective-permute-start = (bf16[144,512]{1,0:T(8,128)(2,1)}, bf16[144,512]{1,0:T(8,128)(2,1)S(1)}, u32[]{:S(2)}, u32[]{:S(2)}) collective-permute-start(bf16[144,512]{1,0:T(8,128)(2,1)} %get-tuple-element.64), channel_id=1, source_target_pairs={{0,3},{1,2},{2,1},{3,0},{4,7},{5,6},{6,5},{7,4},{8,11},{9,10},{10,... | collective-permute-start | bytes 442376 | tf_op jit(solution)/shard_map/ppermute | solution.py:795
  4.5 0.6 collective-permute-start.1
  5.1 0.1 collective-permute-start.2
  5.2 1.9 %pack.3 = (bf16[128,512]{1,0:T(8,128)(2,1)}, bf16[128,512]{1,0:T(8,128)(2,1)}, bf16[128,512]{1,0:T(8,128)(2,1)}, bf16[128,512]{1,0:T(8,128)(2,1)}) custom-call(s32[1]{0:T(128)} %bitcast.member, bf16[128,2048]{1,0:T(8,128)(2,1)} %refs_2_.1), custom_call_target="tpu_custom_call" | custom-call | flops 3000000000 | bytes 9000000 | tf_op jit(solution)/shard_map/pack/pallas_call | solution.py:520
  7.0 2.2 %pack.4 = (bf16[128,1024]{1,0:T(8,128)(2,1)}, bf16[128,1024]{1,0:T(8,128)(2,1)}, bf16[128,1024]{1,0:T(8,128)(2,1)}, bf16[128,1024]{1,0:T(8,128)(2,1)}) custom-call(s32[1]{0:T(128)} %bitcast.member, bf16[128,4096]{1,0:T(8,128)(2,1)} %refs_0_.6), custom_call_target="tpu_custom_call" | custom-call | flops 3000000000 | bytes 9000000 | tf_op jit(solution)/shard_map/pack/pallas_call | solution.py:520
  9.3 2.4 %pack.5 = (bf16[128,1024]{1,0:T(8,128)(2,1)}, bf16[128,1024]{1,0:T(8,128)(2,1)}, bf16[128,1024]{1,0:T(8,128)(2,1)}, bf16[128,1024]{1,0:T(8,128)(2,1)}) custom-call(s32[1]{0:T(128)} %bitcast.member, bf16[128,4096]{1,0:T(8,128)(2,1)} %refs_0_.7), custom_call_target="tpu_custom_call" | custom-call | flops 3000000000 | bytes 9000000 | tf_op jit(solution)/shard_map/pack/pallas_call | solution.py:520
  11.7 0.0 collective-permute-done.refs_3_.refs_7_
  11.7 0.6 collective-permute-done.1.refs_2_.refs_6_
  12.3 0.0 collective-permute-done.2.refs_1_.refs_5_
  12.3 0.8 fusion.2
  13.1 2.4 %collective-permute-start.6 = (bf16[32,512]{1,0:T(8,128)(2,1)S(1)}, bf16[32,512]{1,0:T(8,128)(2,1)S(1)}, u32[]{:S(2)}, u32[]{:S(2)}) collective-permute-start(bf16[32,512]{1,0:T(8,128)(2,1)S(1)} %fusion.2), channel_id=1, source_target_pairs={{0,4},{4,8},{8,12},{12,16},{16,20},{20,24},{24,28},{28,0},{1,5},{5... | collective-permute-start | bytes 98312 | tf_op jit(solution)/shard_map/ppermute | solution.py:855
  15.4 0.0 copy-done.12
  15.5 0.0 collective-permute-start.3
  15.5 1.6 %collective-permute-start.4 = (bf16[128,1024]{1,0:T(8,128)(2,1)S(1)}, bf16[128,1024]{1,0:T(8,128)(2,1)S(1)}, u32[]{:S(2)}, u32[]{:S(2)}) collective-permute-start(bf16[128,1024]{1,0:T(8,128)(2,1)S(1)} %copy-done.11), channel_id=1, source_target_pairs={{0,2},{1,3},{2,0},{3,1},{4,6},{5,7},{6,4},{7,5},{8,10},{9,11},{10,... | collective-permute-start | bytes 786440 | tf_op jit(solution)/shard_map/ppermute | solution.py:795
  17.0 0.3 collective-permute-start.5
  17.3 3.1 %collective-permute-done.6.refs_8_.refs_4_ = bf16[32,512]{1,0:T(8,128)(2,1)S(1)} collective-permute-done((bf16[32,512]{1,0:T(8,128)(2,1)S(1)}, bf16[32,512]{1,0:T(8,128)(2,1)S(1)}, u32[]{:S(2)}, u32[]{:S(2)}) %collective-permute-start.6) | collective-permute-done | bytes 32800 | tf_op jit(solution)/shard_map/ppermute | solution.py:855
  20.4 0.0 copy-start.22
  20.4 0.6 copy-done.22
  21.0 10.7 %key_terms.1 = (bf16[4,4,2,128,128]{4,3,2,1,0:T(8,128)(2,1)}, bf16[4,4,128,256]{3,2,1,0:T(8,128)(2,1)}, bf16[4,4,2,128,128]{4,3,2,1,0:T(8,128)(2,1)}, f32[4,4,2,8,128]{4,3,2,1,0:T(8,128)}, bf16[8,128,128]{2,1,0:T(8,128)(2,1)}) custom-call(s32[1]{0:T(128)} %bitcast.member, bf16[144,512]{1,0:T(8,128)(2,1)} %get-tuple-element.67.refs_0_.refs_4_, ...), custom_call_target="tpu_custom_call" | custom-call | flops 12000000000 | bytes 36000000 | tf_op jit(solution)/shard_map/key_terms/pallas_call | solution.py:606
  31.7 0.0 collective-permute-done.3.refs_1_
  31.8 0.0 copy-start.13
  31.8 0.0 collective-permute-done.4.refs_2_
  31.8 0.0 collective-permute-done.5.refs_3_
  31.8 0.6 copy-done.13
  32.5 0.1 copy-done.14
  32.6 0.1 copy-done.15
  32.7 6.2 %value_terms.1 = (bf16[4,4,2,128,256]{4,3,2,1,0:T(8,128)(2,1)}, bf16[4,3,2,128,128]{4,3,2,1,0:T(8,128)(2,1)}, bf16[8,128,256]{2,1,0:T(8,128)(2,1)}) custom-call(s32[1]{0:T(128)} %bitcast.member, bf16[128,1024]{1,0:T(8,128)(2,1)} %get-tuple-element.76.refs_0_, bf16[128,1024]{1,0:T(8,128)(2,1)} %copy-done.13, bf16[128,1024]{1,0:T(8,128)(2,1)} %copy-done.14, ...), custom_call_target="tpu_custom_call" | custom-call | flops 7000000000 | bytes 21000000 | tf_op jit(solution)/shard_map/value_terms/pallas_call | solution.py:634
  38.9 0.1 collective-permute-start.14
  39.0 3.5 %all-to-all-start = ((bf16[8,1,128,256]{3,2,1,0:T(8,128)(2,1)}), bf16[8,1,128,256]{3,2,1,0:T(8,128)(2,1)S(1)}, u32[]{:S(2)}, u32[]{:S(2)}) async-start(bf16[8,1,128,256]{3,2,1,0:T(8,128)(2,1)} %bitcast.10), calls=%async_computation | async-start | bytes 1048576 | tf_op jit(solution)/shard_map/all_to_all | solution.py:815
  42.5 0.0 copy-done.18
  42.5 0.5 collective-permute-start.7
  43.1 1.6 %collective-permute-start.8 = (bf16[128,512]{1,0:T(8,128)(2,1)S(1)}, bf16[128,512]{1,0:T(8,128)(2,1)S(1)}, u32[]{:S(2)}, u32[]{:S(2)}) collective-permute-start(bf16[128,512]{1,0:T(8,128)(2,1)S(1)} %copy-done.17), channel_id=1, source_target_pairs={{0,2},{1,3},{2,0},{3,1},{4,6},{5,7},{6,4},{7,5},{8,10},{9,11},{10,... | collective-permute-start | bytes 393224 | tf_op jit(solution)/shard_map/ppermute | solution.py:795
  44.7 0.0 collective-permute-start.9
  44.7 0.0 copy-done.9
  44.7 0.5 collective-permute-start.10
  45.2 1.1 %collective-permute-done.7.refs_1_ = bf16[128,512]{1,0:T(8,128)(2,1)S(1)} collective-permute-done((bf16[128,512]{1,0:T(8,128)(2,1)S(1)}, bf16[128,512]{1,0:T(8,128)(2,1)S(1)}, u32[]{:S(2)}, u32[]{:S(2)}) %collective-permute-start.7) | collective-permute-done | bytes 131104 | tf_op jit(solution)/shard_map/ppermute | solution.py:795
  46.3 1.6 %collective-permute-start.11 = (bf16[128,1024]{1,0:T(8,128)(2,1)S(1)}, bf16[128,1024]{1,0:T(8,128)(2,1)S(1)}, u32[]{:S(2)}, u32[]{:S(2)}) collective-permute-start(bf16[128,1024]{1,0:T(8,128)(2,1)S(1)} %copy-done.8), channel_id=1, source_target_pairs={{0,2},{1,3},{2,0},{3,1},{4,6},{5,7},{6,4},{7,5},{8,10},{9,11},{10,... | collective-permute-start | bytes 786440 | tf_op jit(solution)/shard_map/ppermute | solution.py:795
  47.9 1.4 %collective-permute-done.8.refs_2_ = bf16[128,512]{1,0:T(8,128)(2,1)S(1)} collective-permute-done((bf16[128,512]{1,0:T(8,128)(2,1)S(1)}, bf16[128,512]{1,0:T(8,128)(2,1)S(1)}, u32[]{:S(2)}, u32[]{:S(2)}) %collective-permute-start.8) | collective-permute-done | bytes 131104 | tf_op jit(solution)/shard_map/ppermute | solution.py:795
  49.4 0.0 collective-permute-start.12
  49.4 3.4 %prefix_terms.1 = (bf16[4,4,2,128,128]{4,3,2,1,0:T(8,128)(2,1)}, bf16[4,3,2,128,128]{4,3,2,1,0:T(8,128)(2,1)}) custom-call(bf16[4,4,2,128,128]{4,3,2,1,0:T(8,128)(2,1)} %get-tuple-element.91.refs_6_.t_in, bf16[4,4,128,256]{3,2,1,0:T(8,128)(2,1)} %get-tuple-element.92.refs_7_.kt_in.refs_10_, bf16[4,4,2,128,128]{4,3,2,1,0:T(8,128)(2,1)} %get-tuple-element.93.refs_8_.d_in, ...), custom_call_target="tpu_custom_call" | custom-call | flops 5000000000 | bytes 15000000 | tf_op jit(solution)/shard_map/prefix_terms/pallas_call | solution.py:709
  52.8 5.1 %all-to-all-done.terms = bf16[8,1,128,256]{3,2,1,0:T(8,128)(2,1)S(1)} async-done(((bf16[8,1,128,256]{3,2,1,0:T(8,128)(2,1)}), bf16[8,1,128,256]{3,2,1,0:T(8,128)(2,1)S(1)}, u32[]{:S(2)}, u32[]{:S(2)}) %all-to-all-start) | async-done | bytes 524320 | tf_op jit(solution)/shard_map/all_to_all | solution.py:815
  57.9 1.8 %handoff.1 = bf16[8,1,128,128]{3,2,1,0:T(8,128)(2,1)} custom-call(bf16[8,1,128,256]{3,2,1,0:T(8,128)(2,1)S(1)} %all-to-all-done.terms), custom_call_target="tpu_custom_call" | custom-call | flops 1000000000 | bytes 3000000 | tf_op jit(solution)/shard_map/handoff/pallas_call | solution.py:692
  59.6 3.6 %all-to-all-start.1 = ((bf16[8,1,128,128]{3,2,1,0:T(8,128)(2,1)}), bf16[8,1,128,128]{3,2,1,0:T(8,128)(2,1)S(1)}, u32[]{:S(2)}, u32[]{:S(2)}) async-start(bf16[8,1,128,128]{3,2,1,0:T(8,128)(2,1)} %handoff.1), calls=%async_computation.1 | async-start | bytes 524288 | tf_op jit(solution)/shard_map/all_to_all | solution.py:820
  63.3 0.0 collective-permute-done.9.refs_3_
  63.3 0.0 collective-permute-done.10.refs_2_
  63.3 0.0 collective-permute-done.11.refs_3_
  63.3 0.0 collective-permute-done.12.refs_3_
  63.3 0.6 copy-done.21
  63.9 7.8 %query_terms.1.refs_0_.refs_1_ = bf16[8,512,256]{2,1,0:T(8,128)(2,1)} custom-call(s32[1]{0:T(128)} %bitcast.member, bf16[128,512]{1,0:T(8,128)(2,1)} %get-tuple-element.102.refs_0_, bf16[128,512]{1,0:T(8,128)(2,1)} %copy-done.19, bf16[128,512]{1,0:T(8,128)(2,1)} %copy-done.20, bf16[128,512]{1,0:T(8,128)(2,1)} %copy-done.21, ...), custom_call_target="tpu_custom_call" | custom-call | flops 8999999488 | bytes 27000000 | tf_op jit(solution)/shard_map/query_terms/pallas_call | solution.py:671
  71.7 0.7 all-to-all-done.1
  72.4 1.6 %copy-done = bf16[8,512,256]{2,1,0:T(8,128)(2,1)S(1)} copy-done((bf16[8,512,256]{2,1,0:T(8,128)(2,1)S(1)}, bf16[8,512,256]{2,1,0:T(8,128)(2,1)}, u32[]{:S(2)}) %copy-start) | copy-done | bytes 2097176
  74.0 0.8 normed_rows.3
  74.8 0.1 collective-permute-start.13
  74.9 0.8 normed_rows.2.mine
  75.7 1.1 %collective-permute-done.13.theirs = bf16[2,128,1024]{2,1,0:T(8,128)(2,1)S(1)} collective-permute-done((bf16[2,128,1024]{2,1,0:T(8,128)(2,1)S(1)}, bf16[2,128,1024]{2,1,0:T(8,128)(2,1)S(1)}, u32[]{:S(2)}, u32[]{:S(2)}) %collective-permute-start.13) | collective-permute-done | bytes 524320 | tf_op jit(solution)/shard_map/ppermute | solution.py:873
  76.8 0.0 collective-permute-done.14.other_weight
  76.8 2.8 %projected.3 = (f32[128,1024]{1,0:T(8,128)S(1)}, bf16[128,1024]{1,0:T(8,128)(2,1)S(1)}) custom-call(bf16[2,128,1024]{2,1,0:T(8,128)(2,1)S(1)} %normed_rows.2.mine, bf16[2,128,1024]{2,1,0:T(8,128)(2,1)S(1)} %collective-permute-done.13.theirs, bf16[1024,2048]{1,0:T(8,128)(2,1)S(1)} %copy-done.3, bf16[1024,2048]{1,0:T(8,128)(2,1)} %collective-permute-done.14.other_weight), custom_call_target="tpu_custom_call" | custom-call | flops 3000000000 | bytes 9000000 | tf_op jit(solution)/shard_map/projected/pallas_call | solution.py:758
  79.6 1.7 %collective-permute-start.16 = (bf16[128,1024]{1,0:T(8,128)(2,1)S(1)}, bf16[128,1024]{1,0:T(8,128)(2,1)S(1)}, u32[]{:S(2)}, u32[]{:S(2)}) collective-permute-start(bf16[128,1024]{1,0:T(8,128)(2,1)S(1)} %get-tuple-element.114), channel_id=1, source_target_pairs={{0,2},{1,3},{2,0},{3,1},{4,6},{5,7},{6,4},{7,5},{8,10},{9,11},{10,... | collective-permute-start | bytes 786440 | tf_op jit(solution)/shard_map/ppermute | solution.py:884
  81.3 2.8 %projected.2 = (f32[128,1024]{1,0:T(8,128)S(1)}, bf16[128,1024]{1,0:T(8,128)(2,1)S(1)}) custom-call(bf16[2,128,1024]{2,1,0:T(8,128)(2,1)S(1)} %normed_rows.2.mine, bf16[2,128,1024]{2,1,0:T(8,128)(2,1)S(1)} %collective-permute-done.13.theirs, bf16[1024,2048]{1,0:T(8,128)(2,1)S(1)} %copy-done.3, bf16[1024,2048]{1,0:T(8,128)(2,1)} %collective-permute-done.14.other_weight), custom_call_target="tpu_custom_call" | custom-call | flops 3000000000 | bytes 9000000 | tf_op jit(solution)/shard_map/projected/pallas_call | solution.py:758
  84.1 0.5 collective-permute-start.15
  84.5 4.3 %collective-permute-done.16.refs_3_ = bf16[128,1024]{1,0:T(8,128)(2,1)S(1)} collective-permute-done((bf16[128,1024]{1,0:T(8,128)(2,1)S(1)}, bf16[128,1024]{1,0:T(8,128)(2,1)S(1)}, u32[]{:S(2)}, u32[]{:S(2)}) %collective-permute-start.16) | collective-permute-done | bytes 262176 | tf_op jit(solution)/shard_map/ppermute | solution.py:884
  88.8 4.8 %collective-permute-done.15.refs_1_ = bf16[128,1024]{1,0:T(8,128)(2,1)S(1)} collective-permute-done((bf16[128,1024]{1,0:T(8,128)(2,1)S(1)}, bf16[128,1024]{1,0:T(8,128)(2,1)S(1)}, u32[]{:S(2)}, u32[]{:S(2)}) %collective-permute-start.15) | collective-permute-done | bytes 262176 | tf_op jit(solution)/shard_map/ppermute | solution.py:884
  93.6 0.9 summed_parts.1
  (35 shorter events, 0.1 us)
Async XLA Ops:
  2.1 9.6 %collective-permute-start = (bf16[144,512]{1,0:T(8,128)(2,1)}, bf16[144,512]{1,0:T(8,128)(2,1)S(1)}, u32[]{:S(2)}, u32[]{:S(2)}) collective-permute-start(bf16[144,512]{1,0:T(8,128)(2,1)} %get-tuple-element.64), channel_id=1, source_target_pairs={{0,3},{1,2},{2,1},{3,0},{4,7},{5,6},{6,5},{7,4},{8,11},{9,10},{10,... | collective-permute-start | bytes 442376 | tf_op jit(solution)/shard_map/ppermute | solution.py:795
  4.5 7.8 %collective-permute-start.1 = (bf16[144,512]{1,0:T(8,128)(2,1)}, bf16[144,512]{1,0:T(8,128)(2,1)S(1)}, u32[]{:S(2)}, u32[]{:S(2)}) collective-permute-start(bf16[144,512]{1,0:T(8,128)(2,1)} %get-tuple-element.65), channel_id=1, source_target_pairs={{0,2},{1,3},{2,0},{3,1},{4,6},{5,7},{6,4},{7,5},{8,10},{9,11},{10,... | collective-permute-start | bytes 442376 | tf_op jit(solution)/shard_map/ppermute | solution.py:795
  5.1 7.2 %collective-permute-start.2 = (bf16[144,512]{1,0:T(8,128)(2,1)}, bf16[144,512]{1,0:T(8,128)(2,1)S(1)}, u32[]{:S(2)}, u32[]{:S(2)}) collective-permute-start(bf16[144,512]{1,0:T(8,128)(2,1)} %get-tuple-element.66), channel_id=1, source_target_pairs={{0,1},{1,0},{2,3},{3,2},{4,5},{5,4},{6,7},{7,6},{8,9},{9,8},{10,11... | collective-permute-start | bytes 442376 | tf_op jit(solution)/shard_map/ppermute | solution.py:795
  9.3 6.2 %copy-start.12 = (bf16[128,1024]{1,0:T(8,128)(2,1)S(1)}, bf16[128,1024]{1,0:T(8,128)(2,1)}, u32[]{:S(2)}) copy-start(bf16[128,1024]{1,0:T(8,128)(2,1)} %get-tuple-element.77) | copy-start | bytes 786436
  9.3 6.2 %copy-start.11 = (bf16[128,1024]{1,0:T(8,128)(2,1)S(1)}, bf16[128,1024]{1,0:T(8,128)(2,1)}, u32[]{:S(2)}) copy-start(bf16[128,1024]{1,0:T(8,128)(2,1)} %get-tuple-element.78) | copy-start | bytes 786436
  9.3 7.7 %copy-start.10 = (bf16[128,1024]{1,0:T(8,128)(2,1)S(1)}, bf16[128,1024]{1,0:T(8,128)(2,1)}, u32[]{:S(2)}) copy-start(bf16[128,1024]{1,0:T(8,128)(2,1)} %get-tuple-element.79) | copy-start | bytes 786436
  11.7 8.7 %copy-start.4 = (bf16[144,512]{1,0:T(8,128)(2,1)}, bf16[144,512]{1,0:T(8,128)(2,1)S(1)}, u32[]{:S(2)}) copy-start(bf16[144,512]{1,0:T(8,128)(2,1)S(1)} %collective-permute-done.refs_3_.refs_7_) | copy-start | bytes 442372
  12.3 8.1 %copy-start.5 = (bf16[144,512]{1,0:T(8,128)(2,1)}, bf16[144,512]{1,0:T(8,128)(2,1)S(1)}, u32[]{:S(2)}) copy-start(bf16[144,512]{1,0:T(8,128)(2,1)S(1)} %collective-permute-done.1.refs_2_.refs_6_) | copy-start | bytes 442372
  12.3 8.1 %copy-start.6 = (bf16[144,512]{1,0:T(8,128)(2,1)}, bf16[144,512]{1,0:T(8,128)(2,1)S(1)}, u32[]{:S(2)}) copy-start(bf16[144,512]{1,0:T(8,128)(2,1)S(1)} %collective-permute-done.2.refs_1_.refs_5_) | copy-start | bytes 442372
  13.1 7.3 %collective-permute-start.6 = (bf16[32,512]{1,0:T(8,128)(2,1)S(1)}, bf16[32,512]{1,0:T(8,128)(2,1)S(1)}, u32[]{:S(2)}, u32[]{:S(2)}) collective-permute-start(bf16[32,512]{1,0:T(8,128)(2,1)S(1)} %fusion.2), channel_id=1, source_target_pairs={{0,4},{4,8},{8,12},{12,16},{16,20},{20,24},{24,28},{28,0},{1,5},{5... | collective-permute-start | bytes 98312 | tf_op jit(solution)/shard_map/ppermute | solution.py:855
  15.5 16.3 %collective-permute-start.3 = (bf16[128,1024]{1,0:T(8,128)(2,1)S(1)}, bf16[128,1024]{1,0:T(8,128)(2,1)S(1)}, u32[]{:S(2)}, u32[]{:S(2)}) collective-permute-start(bf16[128,1024]{1,0:T(8,128)(2,1)S(1)} %copy-done.12), channel_id=1, source_target_pairs={{0,1},{1,0},{2,3},{3,2},{4,5},{5,4},{6,7},{7,6},{8,9},{9,8},{10,11... | collective-permute-start | bytes 786440 | tf_op jit(solution)/shard_map/ppermute | solution.py:795
  15.5 16.3 %collective-permute-start.4 = (bf16[128,1024]{1,0:T(8,128)(2,1)S(1)}, bf16[128,1024]{1,0:T(8,128)(2,1)S(1)}, u32[]{:S(2)}, u32[]{:S(2)}) collective-permute-start(bf16[128,1024]{1,0:T(8,128)(2,1)S(1)} %copy-done.11), channel_id=1, source_target_pairs={{0,2},{1,3},{2,0},{3,1},{4,6},{5,7},{6,4},{7,5},{8,10},{9,11},{10,... | collective-permute-start | bytes 786440 | tf_op jit(solution)/shard_map/ppermute | solution.py:795
  17.0 14.8 %collective-permute-start.5 = (bf16[128,1024]{1,0:T(8,128)(2,1)S(1)}, bf16[128,1024]{1,0:T(8,128)(2,1)S(1)}, u32[]{:S(2)}, u32[]{:S(2)}) collective-permute-start(bf16[128,1024]{1,0:T(8,128)(2,1)S(1)} %copy-done.10), channel_id=1, source_target_pairs={{0,3},{1,2},{2,1},{3,0},{4,7},{5,6},{6,5},{7,4},{8,11},{9,10},{10,... | collective-permute-start | bytes 786440 | tf_op jit(solution)/shard_map/ppermute | solution.py:795
  20.4 0.6 copy-start.22
  31.8 0.7 copy-start.13
  31.8 0.8 copy-start.14
  31.8 0.8 copy-start.15
  32.6 9.9 %copy-start.18 = (bf16[128,512]{1,0:T(8,128)(2,1)S(1)}, bf16[128,512]{1,0:T(8,128)(2,1)}, u32[]{:S(2)}) copy-start(bf16[128,512]{1,0:T(8,128)(2,1)} %get-tuple-element.88) | copy-start | bytes 393220
  32.6 10.4 %copy-start.17 = (bf16[128,512]{1,0:T(8,128)(2,1)S(1)}, bf16[128,512]{1,0:T(8,128)(2,1)}, u32[]{:S(2)}) copy-start(bf16[128,512]{1,0:T(8,128)(2,1)} %get-tuple-element.89) | copy-start | bytes 393220
  32.6 12.0 %copy-start.16 = (bf16[128,512]{1,0:T(8,128)(2,1)S(1)}, bf16[128,512]{1,0:T(8,128)(2,1)}, u32[]{:S(2)}) copy-start(bf16[128,512]{1,0:T(8,128)(2,1)} %get-tuple-element.90) | copy-start | bytes 393220
  32.6 12.0 %copy-start.9 = (bf16[128,1024]{1,0:T(8,128)(2,1)S(1)}, bf16[128,1024]{1,0:T(8,128)(2,1)}, u32[]{:S(2)}) copy-start(bf16[128,1024]{1,0:T(8,128)(2,1)} %get-tuple-element.99) | copy-start | bytes 786436
  32.7 13.7 %copy-start.8 = (bf16[128,1024]{1,0:T(8,128)(2,1)S(1)}, bf16[128,1024]{1,0:T(8,128)(2,1)}, u32[]{:S(2)}) copy-start(bf16[128,1024]{1,0:T(8,128)(2,1)} %get-tuple-element.100) | copy-start | bytes 786436
  32.7 16.7 %copy-start.7 = (bf16[128,1024]{1,0:T(8,128)(2,1)S(1)}, bf16[128,1024]{1,0:T(8,128)(2,1)}, u32[]{:S(2)}) copy-start(bf16[128,1024]{1,0:T(8,128)(2,1)} %get-tuple-element.101) | copy-start | bytes 786436
  38.9 37.9 %collective-permute-start.14 = (bf16[1024,2048]{1,0:T(8,128)(2,1)}, bf16[1024,2048]{1,0:T(8,128)(2,1)}, u32[]{:S(2)}, u32[]{:S(2)}) collective-permute-start(bf16[1024,2048]{1,0:T(8,128)(2,1)} %own_weight.3), channel_id=1, source_target_pairs={{0,1},{1,0},{2,3},{3,2},{4,5},{5,4},{6,7},{7,6},{8,9},{9,8},{10,11... | collective-permute-start | bytes 12582920 | tf_op jit(solution)/shard_map/ppermute | solution.py:863
  39.0 18.9 %all-to-all-start = ((bf16[8,1,128,256]{3,2,1,0:T(8,128)(2,1)}), bf16[8,1,128,256]{3,2,1,0:T(8,128)(2,1)S(1)}, u32[]{:S(2)}, u32[]{:S(2)}) async-start(bf16[8,1,128,256]{3,2,1,0:T(8,128)(2,1)} %bitcast.10), calls=%async_computation | async-start | bytes 1048576 | tf_op jit(solution)/shard_map/all_to_all | solution.py:815
  42.5 3.8 %collective-permute-start.7 = (bf16[128,512]{1,0:T(8,128)(2,1)S(1)}, bf16[128,512]{1,0:T(8,128)(2,1)S(1)}, u32[]{:S(2)}, u32[]{:S(2)}) collective-permute-start(bf16[128,512]{1,0:T(8,128)(2,1)S(1)} %copy-done.18), channel_id=1, source_target_pairs={{0,1},{1,0},{2,3},{3,2},{4,5},{5,4},{6,7},{7,6},{8,9},{9,8},{10,11... | collective-permute-start | bytes 393224 | tf_op jit(solution)/shard_map/ppermute | solution.py:795
  43.1 6.3 %collective-permute-start.8 = (bf16[128,512]{1,0:T(8,128)(2,1)S(1)}, bf16[128,512]{1,0:T(8,128)(2,1)S(1)}, u32[]{:S(2)}, u32[]{:S(2)}) collective-permute-start(bf16[128,512]{1,0:T(8,128)(2,1)S(1)} %copy-done.17), channel_id=1, source_target_pairs={{0,2},{1,3},{2,0},{3,1},{4,6},{5,7},{6,4},{7,5},{8,10},{9,11},{10,... | collective-permute-start | bytes 393224 | tf_op jit(solution)/shard_map/ppermute | solution.py:795
  44.7 18.6 %collective-permute-start.9 = (bf16[128,512]{1,0:T(8,128)(2,1)S(1)}, bf16[128,512]{1,0:T(8,128)(2,1)S(1)}, u32[]{:S(2)}, u32[]{:S(2)}) collective-permute-start(bf16[128,512]{1,0:T(8,128)(2,1)S(1)} %copy-done.16), channel_id=1, source_target_pairs={{0,3},{1,2},{2,1},{3,0},{4,7},{5,6},{6,5},{7,4},{8,11},{9,10},{10,... | collective-permute-start | bytes 393224 | tf_op jit(solution)/shard_map/ppermute | solution.py:795
  44.7 18.6 %collective-permute-start.10 = (bf16[128,1024]{1,0:T(8,128)(2,1)S(1)}, bf16[128,1024]{1,0:T(8,128)(2,1)S(1)}, u32[]{:S(2)}, u32[]{:S(2)}) collective-permute-start(bf16[128,1024]{1,0:T(8,128)(2,1)S(1)} %copy-done.9), channel_id=1, source_target_pairs={{0,1},{1,0},{2,3},{3,2},{4,5},{5,4},{6,7},{7,6},{8,9},{9,8},{10,11... | collective-permute-start | bytes 786440 | tf_op jit(solution)/shard_map/ppermute | solution.py:795
  46.3 6.5 %copy-start.19 = (bf16[128,512]{1,0:T(8,128)(2,1)}, bf16[128,512]{1,0:T(8,128)(2,1)S(1)}, u32[]{:S(2)}) copy-start(bf16[128,512]{1,0:T(8,128)(2,1)S(1)} %collective-permute-done.7.refs_1_) | copy-start | bytes 393220
  46.3 17.0 %collective-permute-start.11 = (bf16[128,1024]{1,0:T(8,128)(2,1)S(1)}, bf16[128,1024]{1,0:T(8,128)(2,1)S(1)}, u32[]{:S(2)}, u32[]{:S(2)}) collective-permute-start(bf16[128,1024]{1,0:T(8,128)(2,1)S(1)} %copy-done.8), channel_id=1, source_target_pairs={{0,2},{1,3},{2,0},{3,1},{4,6},{5,7},{6,4},{7,5},{8,10},{9,11},{10,... | collective-permute-start | bytes 786440 | tf_op jit(solution)/shard_map/ppermute | solution.py:795
  49.4 3.4 %copy-start.20 = (bf16[128,512]{1,0:T(8,128)(2,1)}, bf16[128,512]{1,0:T(8,128)(2,1)S(1)}, u32[]{:S(2)}) copy-start(bf16[128,512]{1,0:T(8,128)(2,1)S(1)} %collective-permute-done.8.refs_2_) | copy-start | bytes 393220
  49.4 13.9 %collective-permute-start.12 = (bf16[128,1024]{1,0:T(8,128)(2,1)S(1)}, bf16[128,1024]{1,0:T(8,128)(2,1)S(1)}, u32[]{:S(2)}, u32[]{:S(2)}) collective-permute-start(bf16[128,1024]{1,0:T(8,128)(2,1)S(1)} %copy-done.7), channel_id=1, source_target_pairs={{0,3},{1,2},{2,1},{3,0},{4,7},{5,6},{6,5},{7,4},{8,11},{9,10},{10,... | collective-permute-start | bytes 786440 | tf_op jit(solution)/shard_map/ppermute | solution.py:795
  59.6 12.8 %all-to-all-start.1 = ((bf16[8,1,128,128]{3,2,1,0:T(8,128)(2,1)}), bf16[8,1,128,128]{3,2,1,0:T(8,128)(2,1)S(1)}, u32[]{:S(2)}, u32[]{:S(2)}) async-start(bf16[8,1,128,128]{3,2,1,0:T(8,128)(2,1)} %handoff.1), calls=%async_computation.1 | async-start | bytes 524288 | tf_op jit(solution)/shard_map/all_to_all | solution.py:820
  63.3 0.7 copy-start.21
  63.9 8.5 %copy-start.2 = (f32[128]{0:T(128)S(1)}, f32[128]{0:T(128)}, u32[]{:S(2)}) copy-start(f32[128]{0:T(128)} %param.20) | copy-start | bytes 1540
  63.9 11.0 %copy-start.1 = (bf16[128,1024]{1,0:T(8,128)(2,1)S(1)}, bf16[128,1024]{1,0:T(8,128)(2,1)}, u32[]{:S(2)}) copy-start(bf16[128,1024]{1,0:T(8,128)(2,1)} %get-tuple-element.98.refs_2_) | copy-start | bytes 786436
  72.4 1.6 %copy-start = (bf16[8,512,256]{2,1,0:T(8,128)(2,1)S(1)}, bf16[8,512,256]{2,1,0:T(8,128)(2,1)}, u32[]{:S(2)}) copy-start(bf16[8,512,256]{2,1,0:T(8,128)(2,1)} %query_terms.1.refs_0_.refs_1_) | copy-start | bytes 6291460
  74.0 2.8 %copy-start.3 = (bf16[1024,2048]{1,0:T(8,128)(2,1)S(1)}, bf16[1024,2048]{1,0:T(8,128)(2,1)}, u32[]{:S(2)}) copy-start(bf16[1024,2048]{1,0:T(8,128)(2,1)} %own_weight.3) | copy-start | bytes 12582916
  74.8 2.0 %collective-permute-start.13 = (bf16[2,128,1024]{2,1,0:T(8,128)(2,1)S(1)}, bf16[2,128,1024]{2,1,0:T(8,128)(2,1)S(1)}, u32[]{:S(2)}, u32[]{:S(2)}) collective-permute-start(bf16[2,128,1024]{2,1,0:T(8,128)(2,1)S(1)} %normed_rows.3), channel_id=1, source_target_pairs={{0,1},{1,0},{2,3},{3,2},{4,5},{5,4},{6,7},{7,6},{8,9},{9,8},{10,11... | collective-permute-start | bytes 1572872 | tf_op jit(solution)/shard_map/ppermute | solution.py:873
  79.6 9.2 %collective-permute-start.16 = (bf16[128,1024]{1,0:T(8,128)(2,1)S(1)}, bf16[128,1024]{1,0:T(8,128)(2,1)S(1)}, u32[]{:S(2)}, u32[]{:S(2)}) collective-permute-start(bf16[128,1024]{1,0:T(8,128)(2,1)S(1)} %get-tuple-element.114), channel_id=1, source_target_pairs={{0,2},{1,3},{2,0},{3,1},{4,6},{5,7},{6,4},{7,5},{8,10},{9,11},{10,... | collective-permute-start | bytes 786440 | tf_op jit(solution)/shard_map/ppermute | solution.py:884
  84.1 9.5 %collective-permute-start.15 = (bf16[128,1024]{1,0:T(8,128)(2,1)S(1)}, bf16[128,1024]{1,0:T(8,128)(2,1)S(1)}, u32[]{:S(2)}, u32[]{:S(2)}) collective-permute-start(bf16[128,1024]{1,0:T(8,128)(2,1)S(1)} %get-tuple-element.112), channel_id=1, source_target_pairs={{0,2},{1,3},{2,0},{3,1},{4,6},{5,7},{6,4},{7,5},{8,10},{9,11},{10,... | collective-permute-start | bytes 786440 | tf_op jit(solution)/shard_map/ppermute | solution.py:884

commit v6 on v5

--- a/solution.py
+++ b/solution.py
@@ -14,6 +14,7 @@
 CH = 128
 EDGE = 16
 SHARE = HV // HK
+ANYWHERE = pl.BlockSpec(memory_space=pl.ANY)
 ODD_ROWS = 16
 
 norm_floor = 1e-06
@@ -767,26 +768,29 @@
     )(mine, theirs, own_weight, other_weight)
 
 
-def sum_kernel(cuts, *refs):
-    parts, out = refs[:-1], refs[-1]
-    each = len(parts) // cuts
-    for cut in range(cuts):
-        total = parts[cut * each][...]
-        for part in parts[cut * each + 1 : (cut + 1) * each]:
-            total = total + part[...].astype(f32)
-        width = total.shape[1]
-        out[:, cut * width : (cut + 1) * width] = total.astype(bf16)
-
-
-def summed_parts(parts, cuts):
+def sum_kernel(count, *refs):
+    parts, out = refs[:count], refs[-1]
+    total = parts[0][...]
+    for part in parts[1:]:
+        total = total + part[...].astype(f32)
+    out[...] = total.astype(bf16)
+
+
+def summed_parts(parts, before, cut, cuts):
     rows, width = parts[0].shape
+    whole = pl.BlockSpec((rows, width), lambda p: (0, 0))
+    more = [] if before is None else [before]
     return pl.pallas_call(
-        functools.partial(sum_kernel, cuts),
+        functools.partial(sum_kernel, len(parts)),
+        grid=(1,),
+        in_specs=[whole] * len(parts) + [ANYWHERE] * len(more),
+        out_specs=pl.BlockSpec((rows, width), lambda p: (0, cut)),
         out_shape=shape((rows, width * cuts), bf16),
+        input_output_aliases={len(parts): 0} if more else {},
         compiler_params=params(16),
         cost_estimate=cost(1),
         name="summed_parts",
-    )(*parts)
+    )(*parts, *more)
 
 
 def to_members(pieces):
@@ -879,12 +883,14 @@
         kept, *sent = projected(
             mine, theirs, out_weight, other_weight, cut * width // cuts, width // cuts
         )
-        parts.append(kept)
-        parts += [
+        parts.append([kept] + [
             lax.ppermute(part, "head", [(i, i ^ (2 * step + 2)) for i in range(groups)])
             for step, part in enumerate(sent)
-        ]
-    return summed_parts(parts, cuts)
+        ])
+    total = None
+    for cut in range(cuts):
+        total = summed_parts(parts[cut], total, cut, cuts)
+    return total
 
 
 def solution(mesh):

time: 95.2 us -> 95 us (level)
  no operation moved by 1% of the time
where the time goes in v6:
time: 95 us; the launch traced here: 94.4 us
  Pallas kernels  47.1 us (50%)
  waiting for transfers between devices  21.4 us (23%)
  starting transfers between devices  21 us (22%)
  local copies, waits for them, and re-layouts  3.72 us (4%)
    pallas_call x1, Pallas kernels, key_terms(): pl.pallas_call(functools.partial(key_kernel, groups, key_heads * SHARE),...  10.7 us
    ppermute x12, starting transfers between devices, to_members(): lax.ppermute(pieces[d], 'head', [(i, i ^ d) for i in range(groups)])  9.23 us
    ppermute x2, waiting for transfers between devices, on_device(): lax.ppermute(part, 'head', [(i, i ^ 2 * step + 2) for i in range(groups)])  8.34 us
    pallas_call x1, Pallas kernels, query_terms(): pl.pallas_call(functools.partial(query_kernel, groups, key_heads * SHARE)...  7.76 us
    pallas_call x3, Pallas kernels, pack(): pl.pallas_call(functools.partial(pack_kernel, groups), grid_spec=grid_of(...  6.49 us
    pallas_call x1, Pallas kernels, value_terms(): pl.pallas_call(functools.partial(value_kernel, groups), grid_spec=grid_of...  6.22 us
    pallas_call x2, Pallas kernels, projected(): pl.pallas_call(project_kernel, grid=(width // tile,), in_specs=[whole, wh...  5.56 us
    all_to_all x1, waiting for transfers between devices, to_runners(): return lax.all_to_all(pieces, 'seq', 0, 0)  5.06 us
  transfers between devices with their start and end apart: 19, of which 9 were waited for; matrix products, arithmetic and copies ran while one was open for 0% of the time, Pallas kernels for 37%

profile of v6, /device:TPU:0, one launch (start us, length us, event | category | flops | bytes accessed | tf_op | source)
XLA Modules:
  0.0 94.4 jit_solution(15011598484793622757)
XLA Ops:
  0.0 2.1 %pack_keys.1 = (bf16[144,512]{1,0:T(8,128)(2,1)}, bf16[144,512]{1,0:T(8,128)(2,1)}, bf16[144,512]{1,0:T(8,128)(2,1)}, bf16[144,512]{1,0:T(8,128)(2,1)}) custom-call(s32[1]{0:T(128)} %bitcast.member, bf16[128,2048]{1,0:T(8,128)(2,1)} %refs_0_.5, bf16[128,4096]{1,0:T(8,128)(2,1)} %refs_0_.6, bf16[128,2048]{1,0:T(8,128)(2,1)} %refs_2_.1, ...), custom_call_target="tpu_custom_call" | custom-call | flops 3000000000 | bytes 9000000 | tf_op jit(solution)/shard_map/pack_keys/pallas_call | solution.py:546
  2.1 2.4 %collective-permute-start = (bf16[144,512]{1,0:T(8,128)(2,1)}, bf16[144,512]{1,0:T(8,128)(2,1)S(1)}, u32[]{:S(2)}, u32[]{:S(2)}) collective-permute-start(bf16[144,512]{1,0:T(8,128)(2,1)} %get-tuple-element.64), channel_id=1, source_target_pairs={{0,3},{1,2},{2,1},{3,0},{4,7},{5,6},{6,5},{7,4},{8,11},{9,10},{10,... | collective-permute-start | bytes 442376 | tf_op jit(solution)/shard_map/ppermute | solution.py:799
  4.5 0.6 collective-permute-start.1
  5.1 0.1 collective-permute-start.2
  5.2 1.9 %pack.3 = (bf16[128,512]{1,0:T(8,128)(2,1)}, bf16[128,512]{1,0:T(8,128)(2,1)}, bf16[128,512]{1,0:T(8,128)(2,1)}, bf16[128,512]{1,0:T(8,128)(2,1)}) custom-call(s32[1]{0:T(128)} %bitcast.member, bf16[128,2048]{1,0:T(8,128)(2,1)} %refs_2_.1), custom_call_target="tpu_custom_call" | custom-call | flops 3000000000 | bytes 9000000 | tf_op jit(solution)/shard_map/pack/pallas_call | solution.py:521
  7.0 2.2 %pack.4 = (bf16[128,1024]{1,0:T(8,128)(2,1)}, bf16[128,1024]{1,0:T(8,128)(2,1)}, bf16[128,1024]{1,0:T(8,128)(2,1)}, bf16[128,1024]{1,0:T(8,128)(2,1)}) custom-call(s32[1]{0:T(128)} %bitcast.member, bf16[128,4096]{1,0:T(8,128)(2,1)} %refs_0_.6), custom_call_target="tpu_custom_call" | custom-call | flops 3000000000 | bytes 9000000 | tf_op jit(solution)/shard_map/pack/pallas_call | solution.py:521
  9.3 2.4 %pack.5 = (bf16[128,1024]{1,0:T(8,128)(2,1)}, bf16[128,1024]{1,0:T(8,128)(2,1)}, bf16[128,1024]{1,0:T(8,128)(2,1)}, bf16[128,1024]{1,0:T(8,128)(2,1)}) custom-call(s32[1]{0:T(128)} %bitcast.member, bf16[128,4096]{1,0:T(8,128)(2,1)} %refs_0_.7), custom_call_target="tpu_custom_call" | custom-call | flops 3000000000 | bytes 9000000 | tf_op jit(solution)/shard_map/pack/pallas_call | solution.py:521
  11.7 0.0 collective-permute-done.refs_3_.refs_7_
  11.7 0.6 collective-permute-done.1.refs_2_.refs_6_
  12.3 0.0 collective-permute-done.2.refs_1_.refs_5_
  12.3 0.8 fusion.2
  13.1 2.4 %collective-permute-start.6 = (bf16[32,512]{1,0:T(8,128)(2,1)S(1)}, bf16[32,512]{1,0:T(8,128)(2,1)S(1)}, u32[]{:S(2)}, u32[]{:S(2)}) collective-permute-start(bf16[32,512]{1,0:T(8,128)(2,1)S(1)} %fusion.2), channel_id=1, source_target_pairs={{0,4},{4,8},{8,12},{12,16},{16,20},{20,24},{24,28},{28,0},{1,5},{5... | collective-permute-start | bytes 98312 | tf_op jit(solution)/shard_map/ppermute | solution.py:859
  15.5 0.0 collective-permute-start.3
  15.5 0.0 copy-done.11
  15.5 1.6 %collective-permute-start.4 = (bf16[128,1024]{1,0:T(8,128)(2,1)S(1)}, bf16[128,1024]{1,0:T(8,128)(2,1)S(1)}, u32[]{:S(2)}, u32[]{:S(2)}) collective-permute-start(bf16[128,1024]{1,0:T(8,128)(2,1)S(1)} %copy-done.11), channel_id=1, source_target_pairs={{0,2},{1,3},{2,0},{3,1},{4,6},{5,7},{6,4},{7,5},{8,10},{9,11},{10,... | collective-permute-start | bytes 786440 | tf_op jit(solution)/shard_map/ppermute | solution.py:799
  17.0 0.3 collective-permute-start.5
  17.3 3.1 %collective-permute-done.6.refs_8_.refs_4_ = bf16[32,512]{1,0:T(8,128)(2,1)S(1)} collective-permute-done((bf16[32,512]{1,0:T(8,128)(2,1)S(1)}, bf16[32,512]{1,0:T(8,128)(2,1)S(1)}, u32[]{:S(2)}, u32[]{:S(2)}) %collective-permute-start.6) | collective-permute-done | bytes 32800 | tf_op jit(solution)/shard_map/ppermute | solution.py:859
  20.4 0.0 copy-done.4
  20.4 0.6 copy-done.22
  21.0 10.7 %key_terms.1 = (bf16[4,4,2,128,128]{4,3,2,1,0:T(8,128)(2,1)}, bf16[4,4,128,256]{3,2,1,0:T(8,128)(2,1)}, bf16[4,4,2,128,128]{4,3,2,1,0:T(8,128)(2,1)}, f32[4,4,2,8,128]{4,3,2,1,0:T(8,128)}, bf16[8,128,128]{2,1,0:T(8,128)(2,1)}) custom-call(s32[1]{0:T(128)} %bitcast.member, bf16[144,512]{1,0:T(8,128)(2,1)} %get-tuple-element.67.refs_0_.refs_4_, ...), custom_call_target="tpu_custom_call" | custom-call | flops 12000000000 | bytes 36000000 | tf_op jit(solution)/shard_map/key_terms/pallas_call | solution.py:607
  31.7 0.0 collective-permute-done.3.refs_1_
  31.8 0.0 collective-permute-done.4.refs_2_
  31.8 0.0 collective-permute-done.5.refs_3_
  31.8 0.0 copy-start.15
  31.8 0.6 copy-done.13
  32.5 0.1 copy-done.14
  32.6 0.1 copy-done.15
  32.7 6.2 %value_terms.1 = (bf16[4,4,2,128,256]{4,3,2,1,0:T(8,128)(2,1)}, bf16[4,3,2,128,128]{4,3,2,1,0:T(8,128)(2,1)}, bf16[8,128,256]{2,1,0:T(8,128)(2,1)}) custom-call(s32[1]{0:T(128)} %bitcast.member, bf16[128,1024]{1,0:T(8,128)(2,1)} %get-tuple-element.76.refs_0_, bf16[128,1024]{1,0:T(8,128)(2,1)} %copy-done.13, bf16[128,1024]{1,0:T(8,128)(2,1)} %copy-done.14, ...), custom_call_target="tpu_custom_call" | custom-call | flops 7000000000 | bytes 21000000 | tf_op jit(solution)/shard_map/value_terms/pallas_call | solution.py:635
  38.9 0.1 collective-permute-start.14
  39.0 3.5 %all-to-all-start = ((bf16[8,1,128,256]{3,2,1,0:T(8,128)(2,1)}), bf16[8,1,128,256]{3,2,1,0:T(8,128)(2,1)S(1)}, u32[]{:S(2)}, u32[]{:S(2)}) async-start(bf16[8,1,128,256]{3,2,1,0:T(8,128)(2,1)} %bitcast.10), calls=%async_computation | async-start | bytes 1048576 | tf_op jit(solution)/shard_map/all_to_all | solution.py:819
  42.5 0.5 collective-permute-start.7
  43.1 1.6 %collective-permute-start.8 = (bf16[128,512]{1,0:T(8,128)(2,1)S(1)}, bf16[128,512]{1,0:T(8,128)(2,1)S(1)}, u32[]{:S(2)}, u32[]{:S(2)}) collective-permute-start(bf16[128,512]{1,0:T(8,128)(2,1)S(1)} %copy-done.17), channel_id=1, source_target_pairs={{0,2},{1,3},{2,0},{3,1},{4,6},{5,7},{6,4},{7,5},{8,10},{9,11},{10,... | collective-permute-start | bytes 393224 | tf_op jit(solution)/shard_map/ppermute | solution.py:799
  44.7 0.0 copy-done.16
  44.7 0.0 collective-permute-start.9
  44.7 0.5 collective-permute-start.10
  45.2 1.1 %collective-permute-done.7.refs_1_ = bf16[128,512]{1,0:T(8,128)(2,1)S(1)} collective-permute-done((bf16[128,512]{1,0:T(8,128)(2,1)S(1)}, bf16[128,512]{1,0:T(8,128)(2,1)S(1)}, u32[]{:S(2)}, u32[]{:S(2)}) %collective-permute-start.7) | collective-permute-done | bytes 131104 | tf_op jit(solution)/shard_map/ppermute | solution.py:799
  46.3 1.6 %collective-permute-start.11 = (bf16[128,1024]{1,0:T(8,128)(2,1)S(1)}, bf16[128,1024]{1,0:T(8,128)(2,1)S(1)}, u32[]{:S(2)}, u32[]{:S(2)}) collective-permute-start(bf16[128,1024]{1,0:T(8,128)(2,1)S(1)} %copy-done.8), channel_id=1, source_target_pairs={{0,2},{1,3},{2,0},{3,1},{4,6},{5,7},{6,4},{7,5},{8,10},{9,11},{10,... | collective-permute-start | bytes 786440 | tf_op jit(solution)/shard_map/ppermute | solution.py:799
  47.9 1.4 %collective-permute-done.8.refs_2_ = bf16[128,512]{1,0:T(8,128)(2,1)S(1)} collective-permute-done((bf16[128,512]{1,0:T(8,128)(2,1)S(1)}, bf16[128,512]{1,0:T(8,128)(2,1)S(1)}, u32[]{:S(2)}, u32[]{:S(2)}) %collective-permute-start.8) | collective-permute-done | bytes 131104 | tf_op jit(solution)/shard_map/ppermute | solution.py:799
  49.4 0.0 collective-permute-start.12
  49.4 3.4 %prefix_terms.1 = (bf16[4,4,2,128,128]{4,3,2,1,0:T(8,128)(2,1)}, bf16[4,3,2,128,128]{4,3,2,1,0:T(8,128)(2,1)}) custom-call(bf16[4,4,2,128,128]{4,3,2,1,0:T(8,128)(2,1)} %get-tuple-element.91.refs_6_.t_in, bf16[4,4,128,256]{3,2,1,0:T(8,128)(2,1)} %get-tuple-element.92.refs_7_.kt_in.refs_10_, bf16[4,4,2,128,128]{4,3,2,1,0:T(8,128)(2,1)} %get-tuple-element.93.refs_8_.d_in, ...), custom_call_target="tpu_custom_call" | custom-call | flops 5000000000 | bytes 15000000 | tf_op jit(solution)/shard_map/prefix_terms/pallas_call | solution.py:710
  52.8 5.1 %all-to-all-done.terms = bf16[8,1,128,256]{3,2,1,0:T(8,128)(2,1)S(1)} async-done(((bf16[8,1,128,256]{3,2,1,0:T(8,128)(2,1)}), bf16[8,1,128,256]{3,2,1,0:T(8,128)(2,1)S(1)}, u32[]{:S(2)}, u32[]{:S(2)}) %all-to-all-start) | async-done | bytes 524320 | tf_op jit(solution)/shard_map/all_to_all | solution.py:819
  57.9 1.8 %handoff.1 = bf16[8,1,128,128]{3,2,1,0:T(8,128)(2,1)} custom-call(bf16[8,1,128,256]{3,2,1,0:T(8,128)(2,1)S(1)} %all-to-all-done.terms), custom_call_target="tpu_custom_call" | custom-call | flops 1000000000 | bytes 3000000 | tf_op jit(solution)/shard_map/handoff/pallas_call | solution.py:693
  59.6 3.6 %all-to-all-start.1 = ((bf16[8,1,128,128]{3,2,1,0:T(8,128)(2,1)}), bf16[8,1,128,128]{3,2,1,0:T(8,128)(2,1)S(1)}, u32[]{:S(2)}, u32[]{:S(2)}) async-start(bf16[8,1,128,128]{3,2,1,0:T(8,128)(2,1)} %handoff.1), calls=%async_computation.1 | async-start | bytes 524288 | tf_op jit(solution)/shard_map/all_to_all | solution.py:824
  63.3 0.0 collective-permute-done.9.refs_3_
  63.3 0.0 collective-permute-done.10.refs_2_
  63.3 0.0 collective-permute-done.11.refs_3_
  63.3 0.0 collective-permute-done.12.refs_3_
  63.3 0.6 copy-done.21
  63.9 7.8 %query_terms.1.refs_0_.refs_1_ = bf16[8,512,256]{2,1,0:T(8,128)(2,1)} custom-call(s32[1]{0:T(128)} %bitcast.member, bf16[128,512]{1,0:T(8,128)(2,1)} %get-tuple-element.102.refs_0_, bf16[128,512]{1,0:T(8,128)(2,1)} %copy-done.19, bf16[128,512]{1,0:T(8,128)(2,1)} %copy-done.20, bf16[128,512]{1,0:T(8,128)(2,1)} %copy-done.21, ...), custom_call_target="tpu_custom_call" | custom-call | flops 8999999488 | bytes 27000000 | tf_op jit(solution)/shard_map/query_terms/pallas_call | solution.py:672
  71.7 0.7 all-to-all-done.1
  72.4 1.6 %copy-done = bf16[8,512,256]{2,1,0:T(8,128)(2,1)S(1)} copy-done((bf16[8,512,256]{2,1,0:T(8,128)(2,1)S(1)}, bf16[8,512,256]{2,1,0:T(8,128)(2,1)}, u32[]{:S(2)}) %copy-start) | copy-done | bytes 2097176
  74.0 0.8 normed_rows.3
  74.8 0.1 collective-permute-start.13
  74.9 0.8 normed_rows.2.mine
  75.7 1.1 %collective-permute-done.13.theirs = bf16[2,128,1024]{2,1,0:T(8,128)(2,1)S(1)} collective-permute-done((bf16[2,128,1024]{2,1,0:T(8,128)(2,1)S(1)}, bf16[2,128,1024]{2,1,0:T(8,128)(2,1)S(1)}, u32[]{:S(2)}, u32[]{:S(2)}) %collective-permute-start.13) | collective-permute-done | bytes 524320 | tf_op jit(solution)/shard_map/ppermute | solution.py:877
  76.8 0.0 collective-permute-done.14.other_weight
  76.8 2.8 %projected.3 = (f32[128,1024]{1,0:T(8,128)S(1)}, bf16[128,1024]{1,0:T(8,128)(2,1)S(1)}) custom-call(bf16[2,128,1024]{2,1,0:T(8,128)(2,1)S(1)} %normed_rows.2.mine, bf16[2,128,1024]{2,1,0:T(8,128)(2,1)S(1)} %collective-permute-done.13.theirs, bf16[1024,2048]{1,0:T(8,128)(2,1)S(1)} %copy-done.3, bf16[1024,2048]{1,0:T(8,128)(2,1)} %collective-permute-done.14.other_weight), custom_call_target="tpu_custom_call" | custom-call | flops 3000000000 | bytes 9000000 | tf_op jit(solution)/shard_map/projected/pallas_call | solution.py:759
  79.6 1.7 %collective-permute-start.16 = (bf16[128,1024]{1,0:T(8,128)(2,1)S(1)}, bf16[128,1024]{1,0:T(8,128)(2,1)S(1)}, u32[]{:S(2)}, u32[]{:S(2)}) collective-permute-start(bf16[128,1024]{1,0:T(8,128)(2,1)S(1)} %get-tuple-element.114), channel_id=1, source_target_pairs={{0,2},{1,3},{2,0},{3,1},{4,6},{5,7},{6,4},{7,5},{8,10},{9,11},{10,... | collective-permute-start | bytes 786440 | tf_op jit(solution)/shard_map/ppermute | solution.py:887
  81.3 2.8 %projected.2 = (f32[128,1024]{1,0:T(8,128)S(1)}, bf16[128,1024]{1,0:T(8,128)(2,1)S(1)}) custom-call(bf16[2,128,1024]{2,1,0:T(8,128)(2,1)S(1)} %normed_rows.2.mine, bf16[2,128,1024]{2,1,0:T(8,128)(2,1)S(1)} %collective-permute-done.13.theirs, bf16[1024,2048]{1,0:T(8,128)(2,1)S(1)} %copy-done.3, bf16[1024,2048]{1,0:T(8,128)(2,1)} %collective-permute-done.14.other_weight), custom_call_target="tpu_custom_call" | custom-call | flops 3000000000 | bytes 9000000 | tf_op jit(solution)/shard_map/projected/pallas_call | solution.py:759
  84.1 0.5 collective-permute-start.15
  84.5 4.3 %collective-permute-done.16.refs_1_ = bf16[128,1024]{1,0:T(8,128)(2,1)S(1)} collective-permute-done((bf16[128,1024]{1,0:T(8,128)(2,1)S(1)}, bf16[128,1024]{1,0:T(8,128)(2,1)S(1)}, u32[]{:S(2)}, u32[]{:S(2)}) %collective-permute-start.16) | collective-permute-done | bytes 262176 | tf_op jit(solution)/shard_map/ppermute | solution.py:887
  88.8 0.7 summed_parts.2.refs_2_
  89.5 4.1 %collective-permute-done.15.refs_1_ = bf16[128,1024]{1,0:T(8,128)(2,1)S(1)} collective-permute-done((bf16[128,1024]{1,0:T(8,128)(2,1)S(1)}, bf16[128,1024]{1,0:T(8,128)(2,1)S(1)}, u32[]{:S(2)}, u32[]{:S(2)}) %collective-permute-start.15) | collective-permute-done | bytes 262176 | tf_op jit(solution)/shard_map/ppermute | solution.py:887
  93.6 0.7 summed_parts.3
  (36 shorter events, 0.1 us)
Async XLA Ops:
  2.1 9.6 %collective-permute-start = (bf16[144,512]{1,0:T(8,128)(2,1)}, bf16[144,512]{1,0:T(8,128)(2,1)S(1)}, u32[]{:S(2)}, u32[]{:S(2)}) collective-permute-start(bf16[144,512]{1,0:T(8,128)(2,1)} %get-tuple-element.64), channel_id=1, source_target_pairs={{0,3},{1,2},{2,1},{3,0},{4,7},{5,6},{6,5},{7,4},{8,11},{9,10},{10,... | collective-permute-start | bytes 442376 | tf_op jit(solution)/shard_map/ppermute | solution.py:799
  4.5 7.8 %collective-permute-start.1 = (bf16[144,512]{1,0:T(8,128)(2,1)}, bf16[144,512]{1,0:T(8,128)(2,1)S(1)}, u32[]{:S(2)}, u32[]{:S(2)}) collective-permute-start(bf16[144,512]{1,0:T(8,128)(2,1)} %get-tuple-element.65), channel_id=1, source_target_pairs={{0,2},{1,3},{2,0},{3,1},{4,6},{5,7},{6,4},{7,5},{8,10},{9,11},{10,... | collective-permute-start | bytes 442376 | tf_op jit(solution)/shard_map/ppermute | solution.py:799
  5.1 7.2 %collective-permute-start.2 = (bf16[144,512]{1,0:T(8,128)(2,1)}, bf16[144,512]{1,0:T(8,128)(2,1)S(1)}, u32[]{:S(2)}, u32[]{:S(2)}) collective-permute-start(bf16[144,512]{1,0:T(8,128)(2,1)} %get-tuple-element.66), channel_id=1, source_target_pairs={{0,1},{1,0},{2,3},{3,2},{4,5},{5,4},{6,7},{7,6},{8,9},{9,8},{10,11... | collective-permute-start | bytes 442376 | tf_op jit(solution)/shard_map/ppermute | solution.py:799
  9.3 6.2 %copy-start.12 = (bf16[128,1024]{1,0:T(8,128)(2,1)S(1)}, bf16[128,1024]{1,0:T(8,128)(2,1)}, u32[]{:S(2)}) copy-start(bf16[128,1024]{1,0:T(8,128)(2,1)} %get-tuple-element.77) | copy-start | bytes 786436
  9.3 6.2 %copy-start.11 = (bf16[128,1024]{1,0:T(8,128)(2,1)S(1)}, bf16[128,1024]{1,0:T(8,128)(2,1)}, u32[]{:S(2)}) copy-start(bf16[128,1024]{1,0:T(8,128)(2,1)} %get-tuple-element.78) | copy-start | bytes 786436
  9.3 7.7 %copy-start.10 = (bf16[128,1024]{1,0:T(8,128)(2,1)S(1)}, bf16[128,1024]{1,0:T(8,128)(2,1)}, u32[]{:S(2)}) copy-start(bf16[128,1024]{1,0:T(8,128)(2,1)} %get-tuple-element.79) | copy-start | bytes 786436
  11.7 8.7 %copy-start.4 = (bf16[144,512]{1,0:T(8,128)(2,1)}, bf16[144,512]{1,0:T(8,128)(2,1)S(1)}, u32[]{:S(2)}) copy-start(bf16[144,512]{1,0:T(8,128)(2,1)S(1)} %collective-permute-done.refs_3_.refs_7_) | copy-start | bytes 442372
  12.3 8.1 %copy-start.5 = (bf16[144,512]{1,0:T(8,128)(2,1)}, bf16[144,512]{1,0:T(8,128)(2,1)S(1)}, u32[]{:S(2)}) copy-start(bf16[144,512]{1,0:T(8,128)(2,1)S(1)} %collective-permute-done.1.refs_2_.refs_6_) | copy-start | bytes 442372
  12.3 8.1 %copy-start.6 = (bf16[144,512]{1,0:T(8,128)(2,1)}, bf16[144,512]{1,0:T(8,128)(2,1)S(1)}, u32[]{:S(2)}) copy-start(bf16[144,512]{1,0:T(8,128)(2,1)S(1)} %collective-permute-done.2.refs_1_.refs_5_) | copy-start | bytes 442372
  13.1 7.3 %collective-permute-start.6 = (bf16[32,512]{1,0:T(8,128)(2,1)S(1)}, bf16[32,512]{1,0:T(8,128)(2,1)S(1)}, u32[]{:S(2)}, u32[]{:S(2)}) collective-permute-start(bf16[32,512]{1,0:T(8,128)(2,1)S(1)} %fusion.2), channel_id=1, source_target_pairs={{0,4},{4,8},{8,12},{12,16},{16,20},{20,24},{24,28},{28,0},{1,5},{5... | collective-permute-start | bytes 98312 | tf_op jit(solution)/shard_map/ppermute | solution.py:859
  15.5 16.3 %collective-permute-start.3 = (bf16[128,1024]{1,0:T(8,128)(2,1)S(1)}, bf16[128,1024]{1,0:T(8,128)(2,1)S(1)}, u32[]{:S(2)}, u32[]{:S(2)}) collective-permute-start(bf16[128,1024]{1,0:T(8,128)(2,1)S(1)} %copy-done.12), channel_id=1, source_target_pairs={{0,1},{1,0},{2,3},{3,2},{4,5},{5,4},{6,7},{7,6},{8,9},{9,8},{10,11... | collective-permute-start | bytes 786440 | tf_op jit(solution)/shard_map/ppermute | solution.py:799
  15.5 16.3 %collective-permute-start.4 = (bf16[128,1024]{1,0:T(8,128)(2,1)S(1)}, bf16[128,1024]{1,0:T(8,128)(2,1)S(1)}, u32[]{:S(2)}, u32[]{:S(2)}) collective-permute-start(bf16[128,1024]{1,0:T(8,128)(2,1)S(1)} %copy-done.11), channel_id=1, source_target_pairs={{0,2},{1,3},{2,0},{3,1},{4,6},{5,7},{6,4},{7,5},{8,10},{9,11},{10,... | collective-permute-start | bytes 786440 | tf_op jit(solution)/shard_map/ppermute | solution.py:799
  17.0 14.8 %collective-permute-start.5 = (bf16[128,1024]{1,0:T(8,128)(2,1)S(1)}, bf16[128,1024]{1,0:T(8,128)(2,1)S(1)}, u32[]{:S(2)}, u32[]{:S(2)}) collective-permute-start(bf16[128,1024]{1,0:T(8,128)(2,1)S(1)} %copy-done.10), channel_id=1, source_target_pairs={{0,3},{1,2},{2,1},{3,0},{4,7},{5,6},{6,5},{7,4},{8,11},{9,10},{10,... | collective-permute-start | bytes 786440 | tf_op jit(solution)/shard_map/ppermute | solution.py:799
  20.4 0.6 copy-start.22
  31.8 0.7 copy-start.13
  31.8 0.8 copy-start.14
  31.8 0.8 copy-start.15
  32.6 9.9 %copy-start.18 = (bf16[128,512]{1,0:T(8,128)(2,1)S(1)}, bf16[128,512]{1,0:T(8,128)(2,1)}, u32[]{:S(2)}) copy-start(bf16[128,512]{1,0:T(8,128)(2,1)} %get-tuple-element.88) | copy-start | bytes 393220
  32.6 10.4 %copy-start.17 = (bf16[128,512]{1,0:T(8,128)(2,1)S(1)}, bf16[128,512]{1,0:T(8,128)(2,1)}, u32[]{:S(2)}) copy-start(bf16[128,512]{1,0:T(8,128)(2,1)} %get-tuple-element.89) | copy-start | bytes 393220
  32.6 12.0 %copy-start.16 = (bf16[128,512]{1,0:T(8,128)(2,1)S(1)}, bf16[128,512]{1,0:T(8,128)(2,1)}, u32[]{:S(2)}) copy-start(bf16[128,512]{1,0:T(8,128)(2,1)} %get-tuple-element.90) | copy-start | bytes 393220
  32.6 12.0 %copy-start.9 = (bf16[128,1024]{1,0:T(8,128)(2,1)S(1)}, bf16[128,1024]{1,0:T(8,128)(2,1)}, u32[]{:S(2)}) copy-start(bf16[128,1024]{1,0:T(8,128)(2,1)} %get-tuple-element.99) | copy-start | bytes 786436
  32.7 13.7 %copy-start.8 = (bf16[128,1024]{1,0:T(8,128)(2,1)S(1)}, bf16[128,1024]{1,0:T(8,128)(2,1)}, u32[]{:S(2)}) copy-start(bf16[128,1024]{1,0:T(8,128)(2,1)} %get-tuple-element.100) | copy-start | bytes 786436
  32.7 16.7 %copy-start.7 = (bf16[128,1024]{1,0:T(8,128)(2,1)S(1)}, bf16[128,1024]{1,0:T(8,128)(2,1)}, u32[]{:S(2)}) copy-start(bf16[128,1024]{1,0:T(8,128)(2,1)} %get-tuple-element.101) | copy-start | bytes 786436
  38.9 37.9 %collective-permute-start.14 = (bf16[1024,2048]{1,0:T(8,128)(2,1)}, bf16[1024,2048]{1,0:T(8,128)(2,1)}, u32[]{:S(2)}, u32[]{:S(2)}) collective-permute-start(bf16[1024,2048]{1,0:T(8,128)(2,1)} %own_weight.3), channel_id=1, source_target_pairs={{0,1},{1,0},{2,3},{3,2},{4,5},{5,4},{6,7},{7,6},{8,9},{9,8},{10,11... | collective-permute-start | bytes 12582920 | tf_op jit(solution)/shard_map/ppermute | solution.py:867
  39.0 18.9 %all-to-all-start = ((bf16[8,1,128,256]{3,2,1,0:T(8,128)(2,1)}), bf16[8,1,128,256]{3,2,1,0:T(8,128)(2,1)S(1)}, u32[]{:S(2)}, u32[]{:S(2)}) async-start(bf16[8,1,128,256]{3,2,1,0:T(8,128)(2,1)} %bitcast.10), calls=%async_computation | async-start | bytes 1048576 | tf_op jit(solution)/shard_map/all_to_all | solution.py:819
  42.5 3.8 %collective-permute-start.7 = (bf16[128,512]{1,0:T(8,128)(2,1)S(1)}, bf16[128,512]{1,0:T(8,128)(2,1)S(1)}, u32[]{:S(2)}, u32[]{:S(2)}) collective-permute-start(bf16[128,512]{1,0:T(8,128)(2,1)S(1)} %copy-done.18), channel_id=1, source_target_pairs={{0,1},{1,0},{2,3},{3,2},{4,5},{5,4},{6,7},{7,6},{8,9},{9,8},{10,11... | collective-permute-start | bytes 393224 | tf_op jit(solution)/shard_map/ppermute | solution.py:799
  43.1 6.3 %collective-permute-start.8 = (bf16[128,512]{1,0:T(8,128)(2,1)S(1)}, bf16[128,512]{1,0:T(8,128)(2,1)S(1)}, u32[]{:S(2)}, u32[]{:S(2)}) collective-permute-start(bf16[128,512]{1,0:T(8,128)(2,1)S(1)} %copy-done.17), channel_id=1, source_target_pairs={{0,2},{1,3},{2,0},{3,1},{4,6},{5,7},{6,4},{7,5},{8,10},{9,11},{10,... | collective-permute-start | bytes 393224 | tf_op jit(solution)/shard_map/ppermute | solution.py:799
  44.7 18.6 %collective-permute-start.9 = (bf16[128,512]{1,0:T(8,128)(2,1)S(1)}, bf16[128,512]{1,0:T(8,128)(2,1)S(1)}, u32[]{:S(2)}, u32[]{:S(2)}) collective-permute-start(bf16[128,512]{1,0:T(8,128)(2,1)S(1)} %copy-done.16), channel_id=1, source_target_pairs={{0,3},{1,2},{2,1},{3,0},{4,7},{5,6},{6,5},{7,4},{8,11},{9,10},{10,... | collective-permute-start | bytes 393224 | tf_op jit(solution)/shard_map/ppermute | solution.py:799
  44.7 18.6 %collective-permute-start.10 = (bf16[128,1024]{1,0:T(8,128)(2,1)S(1)}, bf16[128,1024]{1,0:T(8,128)(2,1)S(1)}, u32[]{:S(2)}, u32[]{:S(2)}) collective-permute-start(bf16[128,1024]{1,0:T(8,128)(2,1)S(1)} %copy-done.9), channel_id=1, source_target_pairs={{0,1},{1,0},{2,3},{3,2},{4,5},{5,4},{6,7},{7,6},{8,9},{9,8},{10,11... | collective-permute-start | bytes 786440 | tf_op jit(solution)/shard_map/ppermute | solution.py:799
  46.3 6.5 %copy-start.19 = (bf16[128,512]{1,0:T(8,128)(2,1)}, bf16[128,512]{1,0:T(8,128)(2,1)S(1)}, u32[]{:S(2)}) copy-start(bf16[128,512]{1,0:T(8,128)(2,1)S(1)} %collective-permute-done.7.refs_1_) | copy-start | bytes 393220
  46.3 17.0 %collective-permute-start.11 = (bf16[128,1024]{1,0:T(8,128)(2,1)S(1)}, bf16[128,1024]{1,0:T(8,128)(2,1)S(1)}, u32[]{:S(2)}, u32[]{:S(2)}) collective-permute-start(bf16[128,1024]{1,0:T(8,128)(2,1)S(1)} %copy-done.8), channel_id=1, source_target_pairs={{0,2},{1,3},{2,0},{3,1},{4,6},{5,7},{6,4},{7,5},{8,10},{9,11},{10,... | collective-permute-start | bytes 786440 | tf_op jit(solution)/shard_map/ppermute | solution.py:799
  49.4 3.4 %copy-start.20 = (bf16[128,512]{1,0:T(8,128)(2,1)}, bf16[128,512]{1,0:T(8,128)(2,1)S(1)}, u32[]{:S(2)}) copy-start(bf16[128,512]{1,0:T(8,128)(2,1)S(1)} %collective-permute-done.8.refs_2_) | copy-start | bytes 393220
  49.4 13.9 %collective-permute-start.12 = (bf16[128,1024]{1,0:T(8,128)(2,1)S(1)}, bf16[128,1024]{1,0:T(8,128)(2,1)S(1)}, u32[]{:S(2)}, u32[]{:S(2)}) collective-permute-start(bf16[128,1024]{1,0:T(8,128)(2,1)S(1)} %copy-done.7), channel_id=1, source_target_pairs={{0,3},{1,2},{2,1},{3,0},{4,7},{5,6},{6,5},{7,4},{8,11},{9,10},{10,... | collective-permute-start | bytes 786440 | tf_op jit(solution)/shard_map/ppermute | solution.py:799
  59.6 12.8 %all-to-all-start.1 = ((bf16[8,1,128,128]{3,2,1,0:T(8,128)(2,1)}), bf16[8,1,128,128]{3,2,1,0:T(8,128)(2,1)S(1)}, u32[]{:S(2)}, u32[]{:S(2)}) async-start(bf16[8,1,128,128]{3,2,1,0:T(8,128)(2,1)} %handoff.1), calls=%async_computation.1 | async-start | bytes 524288 | tf_op jit(solution)/shard_map/all_to_all | solution.py:824
  63.3 0.7 copy-start.21
  63.9 8.5 %copy-start.2 = (f32[128]{0:T(128)S(1)}, f32[128]{0:T(128)}, u32[]{:S(2)}) copy-start(f32[128]{0:T(128)} %param.20) | copy-start | bytes 1540
  63.9 11.0 %copy-start.1 = (bf16[128,1024]{1,0:T(8,128)(2,1)S(1)}, bf16[128,1024]{1,0:T(8,128)(2,1)}, u32[]{:S(2)}) copy-start(bf16[128,1024]{1,0:T(8,128)(2,1)} %get-tuple-element.98.refs_2_) | copy-start | bytes 786436
  72.4 1.6 %copy-start = (bf16[8,512,256]{2,1,0:T(8,128)(2,1)S(1)}, bf16[8,512,256]{2,1,0:T(8,128)(2,1)}, u32[]{:S(2)}) copy-start(bf16[8,512,256]{2,1,0:T(8,128)(2,1)} %query_terms.1.refs_0_.refs_1_) | copy-start | bytes 6291460
  74.0 2.8 %copy-start.3 = (bf16[1024,2048]{1,0:T(8,128)(2,1)S(1)}, bf16[1024,2048]{1,0:T(8,128)(2,1)}, u32[]{:S(2)}) copy-start(bf16[1024,2048]{1,0:T(8,128)(2,1)} %own_weight.3) | copy-start | bytes 12582916
  74.8 2.0 %collective-permute-start.13 = (bf16[2,128,1024]{2,1,0:T(8,128)(2,1)S(1)}, bf16[2,128,1024]{2,1,0:T(8,128)(2,1)S(1)}, u32[]{:S(2)}, u32[]{:S(2)}) collective-permute-start(bf16[2,128,1024]{2,1,0:T(8,128)(2,1)S(1)} %normed_rows.3), channel_id=1, source_target_pairs={{0,1},{1,0},{2,3},{3,2},{4,5},{5,4},{6,7},{7,6},{8,9},{9,8},{10,11... | collective-permute-start | bytes 1572872 | tf_op jit(solution)/shard_map/ppermute | solution.py:877
  79.6 9.2 %collective-permute-start.16 = (bf16[128,1024]{1,0:T(8,128)(2,1)S(1)}, bf16[128,1024]{1,0:T(8,128)(2,1)S(1)}, u32[]{:S(2)}, u32[]{:S(2)}) collective-permute-start(bf16[128,1024]{1,0:T(8,128)(2,1)S(1)} %get-tuple-element.114), channel_id=1, source_target_pairs={{0,2},{1,3},{2,0},{3,1},{4,6},{5,7},{6,4},{7,5},{8,10},{9,11},{10,... | collective-permute-start | bytes 786440 | tf_op jit(solution)/shard_map/ppermute | solution.py:887
  84.1 9.5 %collective-permute-start.15 = (bf16[128,1024]{1,0:T(8,128)(2,1)S(1)}, bf16[128,1024]{1,0:T(8,128)(2,1)S(1)}, u32[]{:S(2)}, u32[]{:S(2)}) collective-permute-start(bf16[128,1024]{1,0:T(8,128)(2,1)S(1)} %get-tuple-element.112), channel_id=1, source_target_pairs={{0,2},{1,3},{2,0},{3,1},{4,6},{5,7},{6,4},{7,5},{8,10},{9,11},{10,... | collective-permute-start | bytes 786440 | tf_op jit(solution)/shard_map/ppermute | solution.py:887
